TPU v7x, 128 devices: a whole 4x4x4 slice. The times are simulated.
128 devices in a mesh: owner: 32 (over z, y, core), col: 4 (over x).
Axes of the slice: x: 4, y: 4, z: 4, core: 2. Of those that a mesh axis runs over, the one named last changes fastest.
Arguments:
- pooled_grad: bfloat16 [32768, 32, 512], P('owner', None, 'col'), may hold values from -40 to 40
- segment_map: int32 [32768, 32, 4], P('owner'), may hold values from 0 to 1023, as said below
- unique_rows: int32 [32, 1024], P('owner'), may hold values from 0 to 8191, as said below
- live_counts: int32 [32], P('owner'), may hold values from 512 to 1024
- embedding: float32 [32, 8192, 512], P('owner', None, 'col'), may hold values from -6 to 6
- accumulator: float32 [32, 8192], P('owner'), may hold values from 50 to 5000
Outputs:
- new_embedding: float32 [32, 8192, 512], P('owner', None, 'col')
- new_accumulator: float32 [32, 8192], P('owner')
Inputs may be any that keep to these rules, and one draw needn't show every extreme that they name: `segment_map`: every entry for table t is below live_counts[t]. `unique_rows`: the slots of table t below live_counts[t] hold distinct rows; later slots hold rows of the table and are ignored.
All inputs are finite; a program needn't handle non-finite values.
Results may differ from a plain program's by a relative error of at most 0.002.
Values may be sent and summed in bfloat16 or wider, within the bound.
No kernel may reach another device: no remote copies, remote signals or barrier semaphores. Data moves between devices by JAX's collectives and lax.ppermute only.
A program may use at most 128 MiB of HBM per device.

v0:
```python
import jax
import jax.numpy as jnp
from jax import lax
from jax.sharding import PartitionSpec as P

learn_rate = 0.5
epsilon = 1e-08


def table_grad(pooled_rows, segment_rows, first_slot, slot_count):
    total_rows = pooled_rows.shape[0]
    block_rows = 2048
    block_total = total_rows // block_rows
    pooled_blocks = pooled_rows.reshape(block_total, block_rows, pooled_rows.shape[1])
    segment_blocks = segment_rows.reshape(block_total, block_rows, segment_rows.shape[1])
    slot_range = first_slot + lax.iota(jnp.int32, slot_count)

    def accumulate(running, paired):
        pooled_piece, segment_piece = paired
        matches = jnp.sum(
            (segment_piece[None, :, :] == slot_range[:, None, None]).astype(jnp.int32), axis=2
        )
        running = running + jnp.dot(
            matches.astype(jnp.bfloat16), pooled_piece, preferred_element_type=jnp.float32
        )
        return (running, None)

    start_value = jnp.zeros((slot_count, pooled_rows.shape[1]), jnp.float32)
    running, _ = lax.scan(accumulate, start_value, (pooled_blocks, segment_blocks))
    return running


def grads_for(pooled_rows, segment_rows, first_slot, slot_count):

    def single_table(paired):
        return table_grad(paired[0], paired[1], first_slot, slot_count)

    return lax.map(
        single_table, (jnp.moveaxis(pooled_rows, 1, 0), jnp.moveaxis(segment_rows, 1, 0))
    )


def square_sum(gradient):
    return lax.psum(jnp.sum(gradient * gradient, axis=2), "col")


def apply_step(gradient, squares, unique_rows, live_counts, embedding, accumulator, full_width):
    tables_here, slot_total = unique_rows.shape
    table_index = lax.iota(jnp.int32, tables_here)[:, None]
    mean_square = squares / full_width
    new_acc = accumulator[table_index, unique_rows] + mean_square
    new_rows = embedding[table_index, unique_rows] - learn_rate * gradient / (
        jnp.sqrt(new_acc)[:, :, None] + epsilon
    )
    live = lax.iota(jnp.int32, slot_total)[None, :] < live_counts[:, None]
    target = jnp.where(live, unique_rows, embedding.shape[1])
    new_embedding = embedding.at[table_index, target].set(new_rows, mode="drop")
    new_accumulator = accumulator.at[table_index, target].set(new_acc, mode="drop")
    return (new_embedding, new_accumulator)


def per_device(pooled_grad, segment_map, unique_rows, live_counts, embedding, accumulator):
    batch_here, tables_total, columns = pooled_grad.shape
    hot_count = segment_map.shape[2]
    tables_here, slot_total = unique_rows.shape
    owners = lax.axis_size("owner")
    full_width = columns * lax.axis_size("col")
    pooled_split = pooled_grad.reshape(batch_here, owners, tables_here, columns)
    segment_split = segment_map.reshape(batch_here, owners, tables_here, hot_count)
    exchanged = grads_for(
        lax.all_to_all(pooled_split, "owner", split_axis=1, concat_axis=0, tiled=True)[:, 0],
        lax.all_to_all(segment_split, "owner", split_axis=1, concat_axis=0, tiled=True)[:, 0],
        0,
        slot_total,
    )
    squares = square_sum(exchanged)
    return apply_step(
        exchanged, squares, unique_rows, live_counts, embedding, accumulator, full_width
    )


def solution(mesh):
    return jax.shard_map(
        per_device,
        mesh=mesh,
        in_specs=(
            P("owner", None, "col"),
            P("owner", None, None),
            P("owner", None),
            P("owner"),
            P("owner", None, "col"),
            P("owner", None),
        ),
        out_specs=(P("owner", None, "col"), P("owner", None)),
        check_vma=False,
    )
```

profile of v0, /device:TPU:0, one launch (start us, length us, event | category | flops | bytes accessed | tf_op | source)
XLA Modules:
  0.0 377.0 jit_solution(4149657751329203144)
XLA Ops:
  1.4 8.4 %all-to-all-start = ((s32[1024,32,1,4]{0,3,2,1:T(4,128)}), s32[1024,32,1,4]{0,3,2,1:T(4,128)S(1)}, u32[]{:S(2)}, u32[]{:S(2)}) async-start(s32[1024,32,1,4]{0,3,2,1:T(4,128)} %bitcast.48), calls=%async_computation | async-start | bytes 1048576 | tf_op jit(solution)/shard_map/all_to_all | solution.py:72
  9.8 9.8 %copy.15 = bf16[1024,32,128]{2,0,1:T(8,128)(2,1)} copy(bf16[1024,32,128]{2,1,0:T(8,128)(2,1)} %param.8) | data formatting | bytes 16777216 | tf_op args[0]
  21.6 5.8 %all-to-all-start.1 = ((bf16[1024,32,1,128]{3,0,2,1:T(8,128)(2,1)}), bf16[1024,32,1,128]{3,0,2,1:T(8,128)(2,1)}, u32[]{:S(2)}, u32[]{:S(2)}) async-start(bf16[1024,32,1,128]{3,0,2,1:T(8,128)(2,1)} %bitcast.44), calls=%async_computation.1 | async-start | bytes 16777216 | tf_op jit(solution)/shard_map/all_to_all | solution.py:71
  32.6 6.5 %gather_fusion = f32[1024]{0:T(1024)S(1)} fusion(f32[1,8192]{1,0:T(1,128)S(1)} %copy.26, s32[1024]{0:T(1024)S(1)} %bitcast.42), kind=kCustom, calls=%fused_computation.1 | custom fusion | bytes 16384 | tf_op jit(solution)/shard_map/gather | solution.py:51
  39.3 93.8 %all-to-all-done.1 = bf16[1024,32,1,128]{3,0,2,1:T(8,128)(2,1)} async-done(((bf16[1024,32,1,128]{3,0,2,1:T(8,128)(2,1)}), bf16[1024,32,1,128]{3,0,2,1:T(8,128)(2,1)}, u32[]{:S(2)}, u32[]{:S(2)}) %all-to-all-start.1) | async-done | bytes 8388640 | tf_op jit(solution)/shard_map/all_to_all | solution.py:71
  133.0 214.8 %while.18 = (s32[]{:T(128)}, f32[1024,128]{1,0:T(8,128)S(1)}, s32[16,2048,4]{1,2,0:T(4,128)S(1)}, bf16[16,2048,128]{2,1,0:T(8,128)(2,1)}, s32[]{:T(128)}, /*index=5*/s32[]{:T(128)}) while((s32[]{:T(128)}, f32[1024,128]{1,0:T(8,128)S(1)}, s32[16,2048,4]{1,2,0:T(4,128)S(1)}, bf16[16,2048,128]{2,1,0:T(8,128)(2,1)}, s32[]{:T(128)}, ...), condition=%wide.region_2.3_spmd.clone, body=%wide.region_0.2_spmd.clone.sunk | while | flops 562298880 | bytes 18448980 | solution.py:29
  133.0 8.6 %convert_reduce_fusion.2 = s32[1024,2048]{1,0:T(8,128)} fusion(s32[2048,4]{0,1:T(4,128)S(1)} %dynamic-slice_bitcast_fusion.2), kind=kLoop, calls=%fused_computation.6.clone.1 | loop fusion | flops 23068672 | bytes 8421376 | tf_op jit(solution)/shard_map/while/body/eval_jaxpr/while/body/eval_jaxpr/reduce_sum | solution.py:20
  141.6 4.8 %fusion.28 = f32[1024,128]{1,0:T(8,128)S(1)} fusion(s32[1024,2048]{1,0:T(8,128)} %convert_reduce_fusion.2, f32[1024,128]{1,0:T(8,128)S(1)} %get-tuple-element.103, bf16[16,2048,128]{2,1,0:T(8,128)(2,1)} %get-tuple-element.111, s32[]{:T(128)} %get-tuple-element.102, pred[]{:T(512)S(6)} %compare.11), kind=kOutput, calls=%fused_computation.9.clone.1 | convolution fusion | flops 539230208 | bytes 9961985 | tf_op jit(solution)/shard_map/while/body/eval_jaxpr/while/body/eval_jaxpr/dot_general | solution.py:23
  146.5 8.6 %convert_reduce_fusion.2 = s32[1024,2048]{1,0:T(8,128)} fusion(s32[2048,4]{0,1:T(4,128)S(1)} %dynamic-slice_bitcast_fusion.2), kind=kLoop, calls=%fused_computation.6.clone.1 | loop fusion | flops 23068672 | bytes 8421376 | tf_op jit(solution)/shard_map/while/body/eval_jaxpr/while/body/eval_jaxpr/reduce_sum | solution.py:20
  155.0 4.8 %fusion.28 = f32[1024,128]{1,0:T(8,128)S(1)} fusion(s32[1024,2048]{1,0:T(8,128)} %convert_reduce_fusion.2, f32[1024,128]{1,0:T(8,128)S(1)} %get-tuple-element.103, bf16[16,2048,128]{2,1,0:T(8,128)(2,1)} %get-tuple-element.111, s32[]{:T(128)} %get-tuple-element.102, pred[]{:T(512)S(6)} %compare.11), kind=kOutput, calls=%fused_computation.9.clone.1 | convolution fusion | flops 539230208 | bytes 9961985 | tf_op jit(solution)/shard_map/while/body/eval_jaxpr/while/body/eval_jaxpr/dot_general | solution.py:23
  159.9 8.6 %convert_reduce_fusion.2 = s32[1024,2048]{1,0:T(8,128)} fusion(s32[2048,4]{0,1:T(4,128)S(1)} %dynamic-slice_bitcast_fusion.2), kind=kLoop, calls=%fused_computation.6.clone.1 | loop fusion | flops 23068672 | bytes 8421376 | tf_op jit(solution)/shard_map/while/body/eval_jaxpr/while/body/eval_jaxpr/reduce_sum | solution.py:20
  168.5 4.8 %fusion.28 = f32[1024,128]{1,0:T(8,128)S(1)} fusion(s32[1024,2048]{1,0:T(8,128)} %convert_reduce_fusion.2, f32[1024,128]{1,0:T(8,128)S(1)} %get-tuple-element.103, bf16[16,2048,128]{2,1,0:T(8,128)(2,1)} %get-tuple-element.111, s32[]{:T(128)} %get-tuple-element.102, pred[]{:T(512)S(6)} %compare.11), kind=kOutput, calls=%fused_computation.9.clone.1 | convolution fusion | flops 539230208 | bytes 9961985 | tf_op jit(solution)/shard_map/while/body/eval_jaxpr/while/body/eval_jaxpr/dot_general | solution.py:23
  173.3 8.6 %convert_reduce_fusion.2 = s32[1024,2048]{1,0:T(8,128)} fusion(s32[2048,4]{0,1:T(4,128)S(1)} %dynamic-slice_bitcast_fusion.2), kind=kLoop, calls=%fused_computation.6.clone.1 | loop fusion | flops 23068672 | bytes 8421376 | tf_op jit(solution)/shard_map/while/body/eval_jaxpr/while/body/eval_jaxpr/reduce_sum | solution.py:20
  186.8 8.6 %convert_reduce_fusion.2 = s32[1024,2048]{1,0:T(8,128)} fusion(s32[2048,4]{0,1:T(4,128)S(1)} %dynamic-slice_bitcast_fusion.2), kind=kLoop, calls=%fused_computation.6.clone.1 | loop fusion | flops 23068672 | bytes 8421376 | tf_op jit(solution)/shard_map/while/body/eval_jaxpr/while/body/eval_jaxpr/reduce_sum | solution.py:20
  200.2 8.6 %convert_reduce_fusion.2 = s32[1024,2048]{1,0:T(8,128)} fusion(s32[2048,4]{0,1:T(4,128)S(1)} %dynamic-slice_bitcast_fusion.2), kind=kLoop, calls=%fused_computation.6.clone.1 | loop fusion | flops 23068672 | bytes 8421376 | tf_op jit(solution)/shard_map/while/body/eval_jaxpr/while/body/eval_jaxpr/reduce_sum | solution.py:20
  208.7 4.8 %fusion.28 = f32[1024,128]{1,0:T(8,128)S(1)} fusion(s32[1024,2048]{1,0:T(8,128)} %convert_reduce_fusion.2, f32[1024,128]{1,0:T(8,128)S(1)} %get-tuple-element.103, bf16[16,2048,128]{2,1,0:T(8,128)(2,1)} %get-tuple-element.111, s32[]{:T(128)} %get-tuple-element.102, pred[]{:T(512)S(6)} %compare.11), kind=kOutput, calls=%fused_computation.9.clone.1 | convolution fusion | flops 539230208 | bytes 9961985 | tf_op jit(solution)/shard_map/while/body/eval_jaxpr/while/body/eval_jaxpr/dot_general | solution.py:23
  213.6 8.6 %convert_reduce_fusion.2 = s32[1024,2048]{1,0:T(8,128)} fusion(s32[2048,4]{0,1:T(4,128)S(1)} %dynamic-slice_bitcast_fusion.2), kind=kLoop, calls=%fused_computation.6.clone.1 | loop fusion | flops 23068672 | bytes 8421376 | tf_op jit(solution)/shard_map/while/body/eval_jaxpr/while/body/eval_jaxpr/reduce_sum | solution.py:20
  222.2 4.8 %fusion.28 = f32[1024,128]{1,0:T(8,128)S(1)} fusion(s32[1024,2048]{1,0:T(8,128)} %convert_reduce_fusion.2, f32[1024,128]{1,0:T(8,128)S(1)} %get-tuple-element.103, bf16[16,2048,128]{2,1,0:T(8,128)(2,1)} %get-tuple-element.111, s32[]{:T(128)} %get-tuple-element.102, pred[]{:T(512)S(6)} %compare.11), kind=kOutput, calls=%fused_computation.9.clone.1 | convolution fusion | flops 539230208 | bytes 9961985 | tf_op jit(solution)/shard_map/while/body/eval_jaxpr/while/body/eval_jaxpr/dot_general | solution.py:23
  227.0 8.6 %convert_reduce_fusion.2 = s32[1024,2048]{1,0:T(8,128)} fusion(s32[2048,4]{0,1:T(4,128)S(1)} %dynamic-slice_bitcast_fusion.2), kind=kLoop, calls=%fused_computation.6.clone.1 | loop fusion | flops 23068672 | bytes 8421376 | tf_op jit(solution)/shard_map/while/body/eval_jaxpr/while/body/eval_jaxpr/reduce_sum | solution.py:20
  240.5 8.6 %convert_reduce_fusion.2 = s32[1024,2048]{1,0:T(8,128)} fusion(s32[2048,4]{0,1:T(4,128)S(1)} %dynamic-slice_bitcast_fusion.2), kind=kLoop, calls=%fused_computation.6.clone.1 | loop fusion | flops 23068672 | bytes 8421376 | tf_op jit(solution)/shard_map/while/body/eval_jaxpr/while/body/eval_jaxpr/reduce_sum | solution.py:20
  253.9 8.6 %convert_reduce_fusion.2 = s32[1024,2048]{1,0:T(8,128)} fusion(s32[2048,4]{0,1:T(4,128)S(1)} %dynamic-slice_bitcast_fusion.2), kind=kLoop, calls=%fused_computation.6.clone.1 | loop fusion | flops 23068672 | bytes 8421376 | tf_op jit(solution)/shard_map/while/body/eval_jaxpr/while/body/eval_jaxpr/reduce_sum | solution.py:20
  262.5 4.8 %fusion.28 = f32[1024,128]{1,0:T(8,128)S(1)} fusion(s32[1024,2048]{1,0:T(8,128)} %convert_reduce_fusion.2, f32[1024,128]{1,0:T(8,128)S(1)} %get-tuple-element.103, bf16[16,2048,128]{2,1,0:T(8,128)(2,1)} %get-tuple-element.111, s32[]{:T(128)} %get-tuple-element.102, pred[]{:T(512)S(6)} %compare.11), kind=kOutput, calls=%fused_computation.9.clone.1 | convolution fusion | flops 539230208 | bytes 9961985 | tf_op jit(solution)/shard_map/while/body/eval_jaxpr/while/body/eval_jaxpr/dot_general | solution.py:23
  267.3 8.6 %convert_reduce_fusion.2 = s32[1024,2048]{1,0:T(8,128)} fusion(s32[2048,4]{0,1:T(4,128)S(1)} %dynamic-slice_bitcast_fusion.2), kind=kLoop, calls=%fused_computation.6.clone.1 | loop fusion | flops 23068672 | bytes 8421376 | tf_op jit(solution)/shard_map/while/body/eval_jaxpr/while/body/eval_jaxpr/reduce_sum | solution.py:20
  275.9 4.8 %fusion.28 = f32[1024,128]{1,0:T(8,128)S(1)} fusion(s32[1024,2048]{1,0:T(8,128)} %convert_reduce_fusion.2, f32[1024,128]{1,0:T(8,128)S(1)} %get-tuple-element.103, bf16[16,2048,128]{2,1,0:T(8,128)(2,1)} %get-tuple-element.111, s32[]{:T(128)} %get-tuple-element.102, pred[]{:T(512)S(6)} %compare.11), kind=kOutput, calls=%fused_computation.9.clone.1 | convolution fusion | flops 539230208 | bytes 9961985 | tf_op jit(solution)/shard_map/while/body/eval_jaxpr/while/body/eval_jaxpr/dot_general | solution.py:23
  280.8 8.6 %convert_reduce_fusion.2 = s32[1024,2048]{1,0:T(8,128)} fusion(s32[2048,4]{0,1:T(4,128)S(1)} %dynamic-slice_bitcast_fusion.2), kind=kLoop, calls=%fused_computation.6.clone.1 | loop fusion | flops 23068672 | bytes 8421376 | tf_op jit(solution)/shard_map/while/body/eval_jaxpr/while/body/eval_jaxpr/reduce_sum | solution.py:20
  294.2 8.6 %convert_reduce_fusion.2 = s32[1024,2048]{1,0:T(8,128)} fusion(s32[2048,4]{0,1:T(4,128)S(1)} %dynamic-slice_bitcast_fusion.2), kind=kLoop, calls=%fused_computation.6.clone.1 | loop fusion | flops 23068672 | bytes 8421376 | tf_op jit(solution)/shard_map/while/body/eval_jaxpr/while/body/eval_jaxpr/reduce_sum | solution.py:20
  307.6 8.6 %convert_reduce_fusion.2 = s32[1024,2048]{1,0:T(8,128)} fusion(s32[2048,4]{0,1:T(4,128)S(1)} %dynamic-slice_bitcast_fusion.2), kind=kLoop, calls=%fused_computation.6.clone.1 | loop fusion | flops 23068672 | bytes 8421376 | tf_op jit(solution)/shard_map/while/body/eval_jaxpr/while/body/eval_jaxpr/reduce_sum | solution.py:20
  321.0 8.6 %convert_reduce_fusion.2 = s32[1024,2048]{1,0:T(8,128)} fusion(s32[2048,4]{0,1:T(4,128)S(1)} %dynamic-slice_bitcast_fusion.2), kind=kLoop, calls=%fused_computation.6.clone.1 | loop fusion | flops 23068672 | bytes 8421376 | tf_op jit(solution)/shard_map/while/body/eval_jaxpr/while/body/eval_jaxpr/reduce_sum | solution.py:20
  329.6 4.8 %fusion.28 = f32[1024,128]{1,0:T(8,128)S(1)} fusion(s32[1024,2048]{1,0:T(8,128)} %convert_reduce_fusion.2, f32[1024,128]{1,0:T(8,128)S(1)} %get-tuple-element.103, bf16[16,2048,128]{2,1,0:T(8,128)(2,1)} %get-tuple-element.111, s32[]{:T(128)} %get-tuple-element.102, pred[]{:T(512)S(6)} %compare.11), kind=kOutput, calls=%fused_computation.9.clone.1 | convolution fusion | flops 539230208 | bytes 9961985 | tf_op jit(solution)/shard_map/while/body/eval_jaxpr/while/body/eval_jaxpr/dot_general | solution.py:23
  334.5 8.6 %convert_reduce_fusion.2 = s32[1024,2048]{1,0:T(8,128)} fusion(s32[2048,4]{0,1:T(4,128)S(1)} %dynamic-slice_bitcast_fusion.2), kind=kLoop, calls=%fused_computation.6.clone.1 | loop fusion | flops 23068672 | bytes 8421376 | tf_op jit(solution)/shard_map/while/body/eval_jaxpr/while/body/eval_jaxpr/reduce_sum | solution.py:20
  348.1 10.5 %psum.7 = f32[1,1024]{1,0:T(1,128)S(1)} all-reduce(f32[1,1024]{1,0:T(1,128)S(1)} %bitcast.50), channel_id=1, replica_groups=mesh['owner'=32,'col'=4] {'col'}, use_global_device_ids=true, to_apply=%region_4.5 | all-reduce | flops 1024 | bytes 8192 | tf_op jit(solution)/shard_map/psum | solution.py:44
  363.2 13.7 %scatter_custom_fusion = f32[8192,128]{1,0:T(8,128)} fusion(f32[8192,128]{1,0:T(8,128)} %copy.22, s32[1024]{0:T(1024)S(1)} %broadcast_select_fusion, f32[1024,128]{1,0:T(8,128)S(1)} %get-tuple-element.41, f32[1024]{0:T(1024)S(1)} %bitcast.51, f32[]{:T(128)} %constant.17.clone.1, f32[1,8192,128]{2,1,0:T(8,128)} %param.12, s32[1024]{0:T(1024)S(1)} %bitcast.43), kind=kCustom, calls=%fused_computation.15 | custom fusion | flops 393216 | bytes 8921600
  (45 shorter events, 51.0 us)
Async XLA Ops:
  1.4 20.2 %all-to-all-start = ((s32[1024,32,1,4]{0,3,2,1:T(4,128)}), s32[1024,32,1,4]{0,3,2,1:T(4,128)S(1)}, u32[]{:S(2)}, u32[]{:S(2)}) async-start(s32[1024,32,1,4]{0,3,2,1:T(4,128)} %bitcast.48), calls=%async_computation | async-start | bytes 1048576 | tf_op jit(solution)/shard_map/all_to_all | solution.py:72
  21.6 111.5 %all-to-all-start.1 = ((bf16[1024,32,1,128]{3,0,2,1:T(8,128)(2,1)}), bf16[1024,32,1,128]{3,0,2,1:T(8,128)(2,1)}, u32[]{:S(2)}, u32[]{:S(2)}) async-start(bf16[1024,32,1,128]{3,0,2,1:T(8,128)(2,1)} %bitcast.44), calls=%async_computation.1 | async-start | bytes 16777216 | tf_op jit(solution)/shard_map/all_to_all | solution.py:71
  27.3 5.2 %copy-start.1 = (s32[1,1024]{1,0:T(1,128)S(1)}, s32[1,1024]{1,0:T(1,128)}, u32[]{:S(2)}) copy-start(s32[1,1024]{1,0:T(1,128)} %param.10) | copy-start | bytes 12292
  27.4 11.7 %copy-start.2 = (s32[2]{0:T(128)S(1)}, s32[2]{0:T(128)}, u32[]{:S(2)}) copy-start(s32[2]{0:T(128)} %constant.48) | copy-start | bytes 28
  27.4 11.8 %copy-start.3 = (s32[2]{0:T(128)S(1)}, s32[2]{0:T(128)}, u32[]{:S(2)}) copy-start(s32[2]{0:T(128)} %constant.51) | copy-start | bytes 28
  363.2 13.8 %copy-start = (f32[8192]{0:T(1024)}, f32[8192]{0:T(1024)S(1)}, u32[]{:S(2)}) copy-start(f32[8192]{0:T(1024)S(1)} %scatter_fusion) | copy-start | bytes 98308
where the time goes:
time: 378 us; the launch traced here: 377 us
  other arithmetic  151 us (40%)
  waiting for transfers between devices  95.7 us (25%)
  matrix products  77.3 us (20%)
  local copies, waits for them, and re-layouts  26.3 us (7%)
  starting transfers between devices  14.2 us (4%)
  blocking collectives  10.5 us (3%)
    reduce_sum x16, other arithmetic, accumulate(): jnp.sum((segment_piece[None, :, :] == slot_range[:, None, None]).astype(j...  137 us
    all_to_all x1, waiting for transfers between devices, per_device(): lax.all_to_all(pooled_split, 'owner', split_axis=1, concat_axis=0, tiled=...  93.8 us
    dot_general x16, matrix products, accumulate(): jnp.dot(matches.astype(jnp.bfloat16), pooled_piece, preferred_element_typ...  77.3 us
    unnamed x12, local copies, waits for them, and re-layouts  19.7 us
    unnamed x5, other arithmetic  13.9 us
    psum x1, blocking collectives, square_sum(): return lax.psum(jnp.sum(gradient * gradient, axis=2), 'col')  10.5 us
    all_to_all x1, starting transfers between devices, per_device(): lax.all_to_all(segment_split, 'owner', split_axis=1, concat_axis=0, tiled...  8.41 us
  transfers between devices with their start and end apart: 2, of which 2 were waited for; matrix products, arithmetic and copies ran while one was open for 6% of the time, Pallas kernels for 0%

commit v1 on v0

v1 whole, which is shorter than its diff:
```python
import functools

import jax
import jax.numpy as jnp
from jax import lax
from jax.experimental import pallas as pl
from jax.experimental.pallas import tpu as pltpu
from jax.sharding import Mesh
from jax.sharding import PartitionSpec as P

learn_rate = 0.5
epsilon = 1e-08
MIB = 2**20
BF = jnp.bfloat16
F32 = jnp.float32
VMEM = pl.BlockSpec(memory_space=pltpu.VMEM)
SMEM = pl.BlockSpec(memory_space=pltpu.SMEM)
ANY = pl.BlockSpec(memory_space=pl.ANY)


def prep_body(x_ref, seg_ref, o_ref, ids_ref):
    o_ref[...] = jnp.swapaxes(x_ref[...], 0, 1)
    seg = [seg_ref[:, h, :] for h in range(4)]
    same = lambda a, b: jnp.where(seg[a] == seg[b], 1, 0)
    e01, e02, e03 = same(0, 1), same(0, 2), same(0, 3)
    e12, e13, e23 = same(1, 2), same(1, 3), same(2, 3)
    rows = [
        seg[0],
        jnp.where(e01 > 0, -1, seg[1]),
        jnp.where(e02 + e12 > 0, -1, seg[2]),
        jnp.where(e03 + e13 + e23 > 0, -1, seg[3]),
        1 + e01 + e02 + e03,
        1 + e12 + e13,
        1 + e23,
        jnp.ones_like(e01),
    ]
    for r, value in enumerate(rows):
        ids_ref[:, r, :] = value.astype(F32)


def prep(pooled, seg):
    batch, tables, columns = pooled.shape
    block = 128
    return pl.pallas_call(
        prep_body,
        grid=(batch // block,),
        in_specs=[
            pl.BlockSpec((block, tables, columns), lambda i: (i, 0, 0)),
            pl.BlockSpec((tables, 4, block), lambda i: (0, 0, i)),
        ],
        out_specs=[
            pl.BlockSpec((tables, block, columns), lambda i: (0, i, 0)),
            pl.BlockSpec((tables, 8, block), lambda i: (0, 0, i)),
        ],
        out_shape=[
            jax.ShapeDtypeStruct((tables, batch, columns), BF),
            jax.ShapeDtypeStruct((tables, 8, batch), F32),
        ],
        compiler_params=pltpu.CompilerParams(vmem_limit_bytes=40 * MIB),
        name="prep",
    )(pooled, seg)


def tile_sum(ids, weights, x, first, rows):
    batch = x.shape[0]
    number = lax.broadcasted_iota(jnp.int32, (rows, batch), 0).astype(F32).astype(BF)
    local = (ids - float(first)).astype(BF)
    hit = jnp.zeros((rows, batch), BF)
    for h in range(3, -1, -1):
        here = number == jnp.broadcast_to(local[h : h + 1], (rows, batch))
        hit = jnp.where(here, jnp.broadcast_to(weights[4 + h : 5 + h], (rows, batch)), hit)
    return jnp.dot(hit, x, preferred_element_type=F32)


def sums_body(own, first, splits, core_ref, bound_ref, ids_ref, x_ref, *refs):
    add_refs, out_ref = refs[: len(splits)], refs[-1]
    core = core_ref[0]
    side = core if own else 1 - core
    _, slots, columns = out_ref.shape
    half = slots // 2

    def table_sums(k, add):
        table = 2 * (first + k) + side

        def put(at, rows, value):
            here = pl.ds(at, rows)
            if add is not None:
                value = value + add_refs[add][k - splits[add], here, :].astype(F32)
            out_ref[k, here, :] = value.astype(BF)

        tiles = jnp.clip((bound_ref[table] - half) // 128 + 1, 0, half // 128)
        for n in range(half // 128 + 1):

            @pl.when(tiles == n)
            def _(n=n):
                ids = ids_ref[table]
                weights = ids.astype(BF)
                x = x_ref[table]
                at, end = 0, half + n * 128
                while at < end:
                    rows = min(256, end - at)
                    put(at, rows, tile_sum(ids, weights, x, at, rows))
                    at += rows
                while at < slots:
                    put(at, 128, jnp.zeros((128, columns), F32))
                    at += 128

    starts = list(splits) if splits else [0]
    ends = starts[1:] + [out_ref.shape[0]]
    for add, (begin, end) in enumerate(zip(starts, ends)):

        def step(k, carry, add=add):
            table_sums(k, add if splits else None)
            return carry

        lax.fori_loop(begin, end, step, 0)


def sums(name, core, bound, ids, xt, own, first, count, slots, adds=(), after=()):
    columns = xt.shape[2]
    splits, at = [], 0
    for add in adds:
        splits.append(at)
        at += add.shape[0]
    return pl.pallas_call(
        functools.partial(sums_body, own, first, tuple(splits)),
        in_specs=[SMEM, SMEM, VMEM, VMEM] + [VMEM] * len(adds) + [ANY] * len(after),
        out_specs=VMEM,
        out_shape=jax.ShapeDtypeStruct((count, slots, columns), BF),
        compiler_params=pltpu.CompilerParams(vmem_limit_bytes=12 * MIB),
        name=name,
    )(core, bound, ids, xt, *adds, *after)


def total_body(got_ref, grad_ref, square_ref):
    total = got_ref[0].astype(F32)
    for i in range(1, got_ref.shape[0]):
        total = total + got_ref[i].astype(F32)
    grad_ref[...] = total
    square_ref[...] = jnp.sum((total * total).T, axis=0, keepdims=True)


def total(name, got):
    _, count, columns = got.shape
    return pl.pallas_call(
        total_body,
        in_specs=[VMEM],
        out_specs=[VMEM, VMEM],
        out_shape=[
            jax.ShapeDtypeStruct((count, columns), F32),
            jax.ShapeDtypeStruct((1, count), F32),
        ],
        compiler_params=pltpu.CompilerParams(vmem_limit_bytes=8 * MIB),
        name=name,
    )(got)


def old_body(row_ref, emb_ref, acc_ref, after_ref, old_ref, old_acc_ref):
    def step(i, carry):
        for j in range(8):
            u = i * 8 + j
            row = row_ref[0, u]
            old_ref[pl.ds(u, 1), :] = emb_ref[pl.ds(row, 1), :]
            old_acc_ref[0, u] = acc_ref[0, row]
        return carry

    lax.fori_loop(0, old_ref.shape[0] // 8, step, 0)


def old_values(rows, embedding, accumulator, after):
    slots, columns = rows.shape[1], embedding.shape[1]
    return pl.pallas_call(
        old_body,
        in_specs=[SMEM, VMEM, SMEM, ANY],
        out_specs=[VMEM, SMEM],
        out_shape=[
            jax.ShapeDtypeStruct((slots, columns), F32),
            jax.ShapeDtypeStruct((1, slots), F32),
        ],
        compiler_params=pltpu.CompilerParams(vmem_limit_bytes=12 * MIB),
        name="old_values",
    )(rows, embedding, accumulator, after)


def apply_body(
    width, row_ref, live_ref, emb_in, grad_ref, old_ref, square_ref, old_acc_ref, acc_in,
    emb_out, acc_out, emb_ref, new_ref, new_acc_ref, new_acc_smem, acc_smem, sems,
):
    load = pltpu.make_async_copy(acc_in, acc_smem, sems.at[0])
    load.start()
    fetch = pltpu.make_async_copy(emb_in, emb_ref, sems.at[2])
    fetch.start()
    slots, columns = old_ref.shape
    mean_square = jnp.sum(square_ref[...], axis=0) / width
    new_acc = old_acc_ref[...] + mean_square
    new_acc_ref[...] = new_acc
    move = pltpu.make_async_copy(new_acc_ref, new_acc_smem, sems.at[1])
    move.start()
    scale = learn_rate / (jnp.sqrt(new_acc) + epsilon)
    scale = jnp.broadcast_to(scale, (columns, slots)).T
    new_ref[...] = old_ref[...] - grad_ref[...] * scale
    live = live_ref[0]
    fetch.wait()

    def step(i, carry):
        for j in range(8):
            u = jnp.minimum(i * 8 + j, live - 1)
            emb_ref[pl.ds(row_ref[0, u], 1), :] = new_ref[pl.ds(u, 1), :]
        return carry

    lax.fori_loop(0, (live + 7) // 8, step, 0)
    load.wait()
    move.wait()
    write = pltpu.make_async_copy(emb_ref, emb_out, sems.at[2])
    write.start()

    def acc_step(i, carry):
        for j in range(8):
            u = jnp.minimum(i * 8 + j, live - 1)
            acc_smem[0, row_ref[0, u]] = new_acc_smem[0, u]
        return carry

    lax.fori_loop(0, (live + 7) // 8, acc_step, 0)
    store = pltpu.make_async_copy(acc_smem, acc_out, sems.at[0])
    store.start()
    store.wait()
    write.wait()


def apply_rows(width, rows, live, embedding, gradient, old, squares, old_acc, accumulator):
    slots = rows.shape[1]
    return pl.pallas_call(
        functools.partial(apply_body, width),
        in_specs=[SMEM, SMEM, ANY, VMEM, VMEM, VMEM, VMEM, ANY],
        out_specs=[ANY, ANY],
        out_shape=[
            jax.ShapeDtypeStruct(embedding.shape, F32),
            jax.ShapeDtypeStruct(accumulator.shape, F32),
        ],
        scratch_shapes=[
            pltpu.VMEM(embedding.shape, F32),
            pltpu.VMEM(old.shape, F32),
            pltpu.VMEM((1, slots), F32),
            pltpu.SMEM((1, slots), F32),
            pltpu.SMEM(accumulator.shape, F32),
            pltpu.SemaphoreType.DMA((3,)),
        ],
        compiler_params=pltpu.CompilerParams(vmem_limit_bytes=16 * MIB),
        name="apply_rows",
    )(rows, live, embedding, gradient, old, squares, old_acc, accumulator)


def per_device(pooled_grad, segment_map, unique_rows, live_counts, embedding, accumulator):
    columns = pooled_grad.shape[2]
    slots = unique_rows.shape[1]
    cols = lax.axis_size("col")
    half = slots // 2
    core = lax.axis_index("core").astype(jnp.int32).reshape(1)
    seg = jnp.transpose(segment_map, (1, 2, 0))
    bound = jnp.max(seg, axis=(1, 2))
    xt, ids = prep(pooled_grad, seg)
    swap = lambda a: lax.ppermute(a, "core", [(0, 1), (1, 0)])
    spread = lambda a: lax.all_to_all(a, ("z", "y"), 0, 0, tiled=True)

    chips = xt.shape[0] // 2
    late = chips // 4
    sib_a = sums("sib_a", core, bound, ids, xt, False, 0, chips - late, slots)
    got_a = swap(sib_a)
    sib_b = sums("sib_b", core, bound, ids, xt, False, chips - late, late, slots, (), (sib_a,))
    got_b = swap(sib_b)
    old, old_acc = old_values(unique_rows, embedding[0], accumulator, sib_b)
    own = sums("own", core, bound, ids, xt, True, 0, chips, slots, (got_a, got_b), (old,))
    gradient, squares = total("total", spread(own))
    squares = lax.all_to_all(jnp.broadcast_to(squares[None], (cols, 1, slots)), "col", 0, 0, tiled=True)
    new_embedding, new_accumulator = apply_rows(
        columns * cols, unique_rows, live_counts, embedding[0], gradient, old, squares, old_acc, accumulator
    )
    return (new_embedding[None], new_accumulator)


def solution(mesh):
    owner = ("z", "y", "core")
    split = Mesh(mesh.devices.reshape(4, 4, 2, mesh.devices.shape[1]), owner + ("col",))
    return jax.shard_map(
        per_device,
        mesh=split,
        in_specs=(
            P(owner, None, "col"),
            P(owner, None, None),
            P(owner, None),
            P(owner),
            P(owner, None, "col"),
            P(owner, None),
        ),
        out_specs=(P(owner, None, "col"), P(owner, None)),
        check_vma=False,
    )
```

time: 378 us -> 122 us (0.32)
  other arithmetic: 151 us -> 1.72 us
  waiting for transfers between devices: 95.7 us -> 4.72 us
  matrix products: 77.3 us -> 0 us
  blocking collectives: 10.5 us -> 59.1 us
  Pallas kernels: 0 us -> 44.8 us
  local copies, waits for them, and re-layouts: 26.3 us -> 3.86 us
  starting transfers between devices: 14.2 us -> 5.04 us
    reduce_sum x17 -> x0, other arithmetic: 137 us -> none  [the longest x16 137 us: accumulate(): jnp.sum((segment_piece[None, :, :] == slot_range[:, None, None]).astype(j...]
    all_to_all x2 -> x1, waiting for transfers between devices: 95.7 us -> 4.71 us  [per_device(): lax.all_to_all(jnp.broadcast_to(squares[None], (cols, 1, slots)), 'col',...]
    dot_general x16 -> x0, matrix products: 77.3 us -> none  [accumulate(): jnp.dot(matches.astype(jnp.bfloat16), pooled_piece, preferred_element_typ...]
    all_to_all x0 -> x1, blocking collectives: none -> 59.1 us  [per_device(): spread = lambda a: lax.all_to_all(a, ('z', 'y'), 0, 0, tiled=True)]
    pallas_call x0 -> x7, Pallas kernels: none -> 44.8 us  [the longest x3 26.4 us: sums(): pl.pallas_call(functools.partial(sums_body, own, first, tuple(splits)), i...]
    unnamed x12 -> x10, local copies, waits for them, and re-layouts: 19.7 us -> 3.25 us
    unnamed x5 -> x0, other arithmetic: 13.9 us -> none
    psum x1 -> x0, blocking collectives: 10.5 us -> none  [square_sum(): return lax.psum(jnp.sum(gradient * gradient, axis=2), 'col')]
  transfers between devices with their start and end apart: 2 -> 3, of which waited for: 2 -> 1; matrix products, arithmetic and copies ran while one was open for 6% -> 0% of each run, Pallas kernels for 0% -> 6%
where the time goes in v1:
time: 122 us; the launch traced here: 121 us
  blocking collectives  59.1 us (48%)
  Pallas kernels  44.8 us (37%)
  starting transfers between devices  5.04 us (4%)
  waiting for transfers between devices  4.72 us (4%)
  local copies, waits for them, and re-layouts  3.86 us (3%)
  other arithmetic  1.72 us (1%)
  between operations  1.55 us (1%)
    all_to_all x1, blocking collectives, per_device(): spread = lambda a: lax.all_to_all(a, ('z', 'y'), 0, 0, tiled=True)  59.1 us
    pallas_call x3, Pallas kernels, sums(): pl.pallas_call(functools.partial(sums_body, own, first, tuple(splits)), i...  26.4 us
    pallas_call x1, Pallas kernels, prep(): pl.pallas_call(prep_body, grid=(batch // block,), in_specs=[pl.BlockSpec(...  8.12 us
    pallas_call x1, Pallas kernels, apply_rows(): pl.pallas_call(functools.partial(apply_body, width), in_specs=[SMEM, SMEM...  5.52 us
    all_to_all x1, waiting for transfers between devices, per_device(): lax.all_to_all(jnp.broadcast_to(squares[None], (cols, 1, slots)), 'col',...  4.71 us
    all_to_all x1, starting transfers between devices, per_device(): lax.all_to_all(jnp.broadcast_to(squares[None], (cols, 1, slots)), 'col',...  4.29 us
    pallas_call x1, Pallas kernels, old_values(): pl.pallas_call(old_body, in_specs=[SMEM, VMEM, SMEM, ANY], out_specs=[VME...  4.07 us
    unnamed x10, local copies, waits for them, and re-layouts  3.25 us
  transfers between devices with their start and end apart: 3, of which 1 were waited for; matrix products, arithmetic and copies ran while one was open for 0% of the time, Pallas kernels for 6%

profile of v1, /device:TPU:0, one launch (start us, length us, event | category | flops | bytes accessed | tf_op | source)
XLA Modules:
  0.0 120.7 jit_solution(7366053848468495592)
XLA Ops:
  0.6 1.7 %reduce_max.9.bound_ref = s32[32]{0:T(128)S(1)} reduce(s32[1024,32,4]{0,2,1:T(4,128)} %param.7, s32[]{:T(128)} %constant.7.clone.1), dimensions={2,0}, to_apply=%region_0.0 | reduce | flops 131040 | bytes 524420 | tf_op jit(solution)/shard_map/reduce_max | solution.py:260
  2.3 0.0 copy-start.2
  2.4 1.0 copy-done.2
  3.4 8.1 %prep.1 = (bf16[32,1024,128]{2,1,0:T(8,128)(2,1)S(1)}, f32[32,8,1024]{2,1,0:T(8,128)S(1)}) custom-call(bf16[1024,32,128]{2,1,0:T(8,128)(2,1)} %x_ref.1, s32[32,4,1024]{2,1,0:T(4,128)S(1)} %bitcast.7), custom_call_target="tpu_custom_call" | custom-call | tf_op jit(solution)/shard_map/prep/pallas_call | solution.py:44
  11.5 9.6 %sib_a.1.refs_0_ = bf16[12,1024,128]{2,1,0:T(8,128)(2,1)S(1)} custom-call(s32[1]{0:T(128)} %bitcast.1.core_ref, s32[32]{0:T(128)S(1)} %reduce_max.9.bound_ref, f32[32,8,1024]{2,1,0:T(8,128)S(1)} %get-tuple-element.10.ids_ref, bf16[32,1024,128]{2,1,0:T(8,128)(2,1)S(1)} %get-tuple-element.11.x_ref), custom_call_target="tpu_custom_call" | custom-call | tf_op jit(solution)/shard_map/sib_a/pallas_call | solution.py:125
  21.1 0.0 copy-start
  21.2 0.0 copy-start.3
  21.2 0.0 copy-start.4
  21.2 0.1 collective-permute-start
  21.3 3.7 %sib_b.1.after_ref = bf16[4,1024,128]{2,1,0:T(8,128)(2,1)S(1)} custom-call(s32[1]{0:T(128)} %bitcast.1.core_ref, s32[32]{0:T(128)S(1)} %reduce_max.9.bound_ref, f32[32,8,1024]{2,1,0:T(8,128)S(1)} %get-tuple-element.10.ids_ref, bf16[32,1024,128]{2,1,0:T(8,128)(2,1)S(1)} %get-tuple-element.11.x_ref, bf16[12,1024,128]{2,1,0:T(8,128)(2,1)S(1)} %sib_a.1.refs_0_), custom_call_target="tpu_custom_call" | custom-call | tf_op jit(solution)/shard_map/sib_b/pallas_call | solution.py:125
  25.0 0.7 collective-permute-start.1
  25.6 0.0 copy-done
  25.6 0.0 copy-done.3
  25.6 0.0 copy-done.4
  25.6 4.1 %old_values.1 = (f32[1024,128]{1,0:T(8,128)S(1)}, f32[1,1024]{1,0:T(1,128)S(1)}) custom-call(s32[1,1024]{1,0:T(1,128)S(1)} %copy-done.4, f32[8192,128]{1,0:T(8,128)S(1)} %bitcast.5, f32[1,8192]{1,0:T(1,128)S(1)} %copy-done.3, bf16[4,1024,128]{2,1,0:T(8,128)(2,1)S(1)} %sib_b.1.after_ref), custom_call_target="tpu_custom_call" | custom-call | tf_op jit(solution)/shard_map/old_values/pallas_call | solution.py:172
  29.7 0.0 collective-permute-done.1.refs_1_
  29.7 0.0 collective-permute-done.refs_0_
  29.7 13.1 %own.1 = bf16[16,1024,128]{2,1,0:T(8,128)(2,1)S(1)} custom-call(s32[1]{0:T(128)} %bitcast.1.core_ref, s32[32]{0:T(128)S(1)} %reduce_max.9.bound_ref, f32[32,8,1024]{2,1,0:T(8,128)S(1)} %get-tuple-element.10.ids_ref, bf16[32,1024,128]{2,1,0:T(8,128)(2,1)S(1)} %get-tuple-element.11.x_ref, bf16[12,1024,128]{2,1,0:T(8,128)(2,1)S(1)} %collective-permute-done.refs_0_, ...), custom_call_target="tpu_custom_call" | custom-call | tf_op jit(solution)/shard_map/own/pallas_call | solution.py:125
  42.9 59.1 %all_to_all.10.got_ref = bf16[16,1024,128]{2,1,0:T(8,128)(2,1)S(1)} all-to-all(bf16[16,1024,128]{2,1,0:T(8,128)(2,1)S(1)} %own.1), channel_id=1, replica_groups=mesh['z'=4,'y'=4,'core'=2,'col'=4] {'z','y'}, dimensions={0} | all-to-all | bytes 8388608 | tf_op jit(solution)/shard_map/all_to_all | solution.py:263
  101.9 0.6 total.1
  102.6 0.6 broadcast_in_dim.12
  103.2 4.3 %all-to-all-start.1 = ((f32[4,1,1024]{2,1,0:T(1,128)}), f32[4,1,1024]{2,1,0:T(1,128)S(1)}, u32[]{:S(2)}, u32[]{:S(2)}) async-start(f32[4,1,1024]{2,1,0:T(1,128)} %broadcast_in_dim.12), calls=%async_computation.1 | async-start | bytes 32768 | tf_op jit(solution)/shard_map/all_to_all | solution.py:274
  108.1 4.7 %all-to-all-done.1.square_ref = f32[4,1,1024]{2,1,0:T(1,128)S(1)} async-done(((f32[4,1,1024]{2,1,0:T(1,128)}), f32[4,1,1024]{2,1,0:T(1,128)S(1)}, u32[]{:S(2)}, u32[]{:S(2)}) %all-to-all-start.1) | async-done | bytes 16416 | tf_op jit(solution)/shard_map/all_to_all | solution.py:274
  112.9 0.0 copy-start.1
  112.9 2.2 %copy-done.1 = f32[1,8192,128]{2,1,0:T(8,128)S(1)} copy-done((f32[1,8192,128]{2,1,0:T(8,128)S(1)}, f32[1,8192,128]{2,1,0:T(8,128)}, u32[]{:S(2)}) %copy-start.1) | copy-done | bytes 4194328
  115.0 5.5 %apply_rows.1 = (f32[8192,128]{1,0:T(8,128)}, f32[1,8192]{1,0:T(1,128)}) custom-call(s32[1,1024]{1,0:T(1,128)S(1)} %copy-done.4, s32[1]{0:T(128)S(6)} %copy.8.live_ref, f32[8192,128]{1,0:T(8,128)S(1)} %bitcast.6, f32[1024,128]{1,0:T(8,128)S(1)} %get-tuple-element.13.grad_ref, f32[1024,128]{1,0:T(8,128)S(1)} %get-tuple-element.12.refs_2_.old_ref, ...), custom_call_target="tpu_custom_call" | custom-call | tf_op jit(solution)/shard_map/apply_rows/pallas_call | solution.py:232
Async XLA Ops:
  2.3 1.0 copy-start.2
  21.1 4.5 %copy-start = (f32[1,8192,128]{2,1,0:T(8,128)S(1)}, f32[1,8192,128]{2,1,0:T(8,128)}, u32[]{:S(2)}) copy-start(f32[1,8192,128]{2,1,0:T(8,128)} %param.10) | copy-start | bytes 12582916
  21.2 4.5 %copy-start.3 = (f32[1,8192]{1,0:T(1,128)S(1)}, f32[1,8192]{1,0:T(1,128)}, u32[]{:S(2)}) copy-start(f32[1,8192]{1,0:T(1,128)} %acc_in.1) | copy-start | bytes 98308
  21.2 4.5 %copy-start.4 = (s32[1,1024]{1,0:T(1,128)S(1)}, s32[1,1024]{1,0:T(1,128)}, u32[]{:S(2)}) copy-start(s32[1,1024]{1,0:T(1,128)} %row_ref.3) | copy-start | bytes 12292
  21.2 8.5 %collective-permute-start = (bf16[12,1024,128]{2,1,0:T(8,128)(2,1)S(1)}, bf16[12,1024,128]{2,1,0:T(8,128)(2,1)S(1)}, u32[]{:S(2)}, u32[]{:S(2)}) collective-permute-start(bf16[12,1024,128]{2,1,0:T(8,128)(2,1)S(1)} %sib_a.1.refs_0_), channel_id=1, source_target_pairs={{0,4},{4,0},{1,5},{5,1},{2,6},{6,2},{3,7},{7,3},{8,12},{12,8},{9,1... | collective-permute-start | bytes 9437192 | tf_op jit(solution)/shard_map/ppermute | solution.py:262
  25.0 4.8 %collective-permute-start.1 = (bf16[4,1024,128]{2,1,0:T(8,128)(2,1)S(1)}, bf16[4,1024,128]{2,1,0:T(8,128)(2,1)S(1)}, u32[]{:S(2)}, u32[]{:S(2)}) collective-permute-start(bf16[4,1024,128]{2,1,0:T(8,128)(2,1)S(1)} %sib_b.1.after_ref), channel_id=1, source_target_pairs={{0,4},{4,0},{1,5},{5,1},{2,6},{6,2},{3,7},{7,3},{8,12},{12,8},{9,1... | collective-permute-start | bytes 3145736 | tf_op jit(solution)/shard_map/ppermute | solution.py:262
  103.2 9.7 %all-to-all-start.1 = ((f32[4,1,1024]{2,1,0:T(1,128)}), f32[4,1,1024]{2,1,0:T(1,128)S(1)}, u32[]{:S(2)}, u32[]{:S(2)}) async-start(f32[4,1,1024]{2,1,0:T(1,128)} %broadcast_in_dim.12), calls=%async_computation.1 | async-start | bytes 32768 | tf_op jit(solution)/shard_map/all_to_all | solution.py:274
  112.9 2.2 %copy-start.1 = (f32[1,8192,128]{2,1,0:T(8,128)S(1)}, f32[1,8192,128]{2,1,0:T(8,128)}, u32[]{:S(2)}) copy-start(f32[1,8192,128]{2,1,0:T(8,128)} %param.10) | copy-start | bytes 12582916

commit v2 on v1

v2 whole, which is shorter than its diff:
```python
import functools

import jax
import jax.numpy as jnp
from jax import lax
from jax.experimental import pallas as pl
from jax.experimental.pallas import tpu as pltpu
from jax.sharding import Mesh
from jax.sharding import PartitionSpec as P

learn_rate = 0.5
epsilon = 1e-08
MIB = 2**20
BF = jnp.bfloat16
F32 = jnp.float32
VMEM = pl.BlockSpec(memory_space=pltpu.VMEM)
SMEM = pl.BlockSpec(memory_space=pltpu.SMEM)
ANY = pl.BlockSpec(memory_space=pl.ANY)
COST = pl.CostEstimate(flops=1000, transcendentals=0, bytes_accessed=1000)


def prep_body(x_hbm, seg_hbm, o_ref, ids_ref, bound_ref, x_ref, seg_ref, sems):
    batch = x_ref.shape[0]
    block = 128
    blocks = batch // block
    seg_copy = pltpu.make_async_copy(seg_hbm, seg_ref, sems.at[blocks])
    seg_copy.start()
    copies = []
    for i in range(blocks):
        here = pl.ds(i * block, block)
        copies.append(pltpu.make_async_copy(x_hbm.at[here], x_ref.at[here], sems.at[i]))
        copies[-1].start()
    seg_copy.wait()
    for t in range(seg_ref.shape[0]):
        bound_ref[t] = jnp.max(seg_ref[t])
    seg = [seg_ref[:, h, :] for h in range(4)]
    same = lambda a, b: jnp.where(seg[a] == seg[b], 1, 0)
    e01, e02, e03 = same(0, 1), same(0, 2), same(0, 3)
    e12, e13, e23 = same(1, 2), same(1, 3), same(2, 3)
    rows = [
        seg[0],
        jnp.where(e01 > 0, -1, seg[1]),
        jnp.where(e02 + e12 > 0, -1, seg[2]),
        jnp.where(e03 + e13 + e23 > 0, -1, seg[3]),
        1 + e01 + e02 + e03,
        1 + e12 + e13,
        1 + e23,
        jnp.ones_like(e01),
    ]
    for r, value in enumerate(rows):
        ids_ref[:, r, :] = value.astype(F32)
    for i in range(blocks):
        here = pl.ds(i * block, block)
        copies[i].wait()
        o_ref[:, here, :] = jnp.swapaxes(x_ref[here], 0, 1)


def prep(pooled, seg):
    batch, tables, columns = pooled.shape
    return pl.pallas_call(
        prep_body,
        in_specs=[ANY, ANY],
        out_specs=[VMEM, VMEM, SMEM],
        out_shape=[
            jax.ShapeDtypeStruct((tables, batch, columns), BF),
            jax.ShapeDtypeStruct((tables, 8, batch), F32),
            jax.ShapeDtypeStruct((tables,), jnp.int32),
        ],
        scratch_shapes=[
            pltpu.VMEM(pooled.shape, BF),
            pltpu.VMEM(seg.shape, jnp.int32),
            pltpu.SemaphoreType.DMA((batch // 128 + 1,)),
        ],
        compiler_params=pltpu.CompilerParams(vmem_limit_bytes=40 * MIB),
        cost_estimate=COST,
        name="prep",
    )(pooled, seg)


def tile_sum(ids, weights, x, first, rows):
    batch = x.shape[0]
    number = lax.broadcasted_iota(jnp.int32, (rows, batch), 0).astype(F32).astype(BF)
    local = (ids - first).astype(BF)
    hit = jnp.zeros((rows, batch), BF)
    for h in range(3, -1, -1):
        here = number == jnp.broadcast_to(local[h : h + 1], (rows, batch))
        hit = jnp.where(here, jnp.broadcast_to(weights[4 + h : 5 + h], (rows, batch)), hit)
    return jnp.dot(hit, x, preferred_element_type=F32)


def ring_pos(half):
    at_z, at_y = lax.axis_index("z"), lax.axis_index("y")
    return jnp.where(half == 0, at_z, at_y), jnp.where(half == 0, at_y, at_z)


def half_sums(own, step, add_ref, extra_ref, out_ref, bound_ref, ids_ref, x_ref):
    core = lax.axis_index("core")
    half = core if own else 1 - core
    place = lax.rem(ring_pos(half)[0] + step, 4)
    _, slots, columns = out_ref.shape
    tile = slots // 2

    def put(m, at, value):
        here = pl.ds(at, tile)
        if add_ref is not None:
            value = value + add_ref[m, here, :].astype(F32)
        if extra_ref is not None:
            value = value + extra_ref[m, here, :].astype(F32)
        out_ref[m, here, :] = value.astype(out_ref.dtype)

    def chip_sums(j, carry):
        chip = jnp.where(half == 0, place * 4 + j, j * 4 + place)
        later = [slots + lax.rem(half + c, 2) * tile for c in range(2)]
        filled = [bound_ref[2 * chip + c] >= later[c] for c in range(2)]
        for case in range(4):
            wanted = [bool(case & 1), bool(case & 2)]

            @pl.when(jnp.logical_and(filled[0] == wanted[0], filled[1] == wanted[1]))
            def _(wanted=wanted):
                for c in range(2):
                    ids = ids_ref[2 * chip + c]
                    weights = ids.astype(BF)
                    x = x_ref[2 * chip + c]
                    put(2 * j + c, 0, tile_sum(ids, weights, x, (half * tile).astype(F32), tile))
                    if wanted[c]:
                        value = tile_sum(ids, weights, x, later[c].astype(F32), tile)
                    else:
                        value = jnp.zeros((tile, columns), F32)
                    put(2 * j + c, tile, value)

        return carry

    lax.fori_loop(0, 4, chip_sums, 0)


def sums_body(jobs, afters, old, bound_hbm, ids_ref, x_ref, *refs):
    refs = list(refs)
    take = lambda n: [refs.pop(0) for _ in range(n)]
    inputs = [(take(adds), take(extras)) for _, _, adds, extras in jobs]
    old_in = take(3 if old else 0)
    take(afters)
    outs = take(len(jobs))
    old_out = take(3 if old else 0)
    bound_ref, sem = take(2)
    bound_copy = pltpu.make_async_copy(bound_hbm, bound_ref, sem)
    bound_copy.start()
    if old:
        row_hbm, emb_hbm, acc_hbm = old_in
        old_ref, old_acc_ref, table_ref = old_out
        row_ref, acc_ref, sems = take(3)
        loads = [
            pltpu.make_async_copy(row_hbm, row_ref, sems.at[0]),
            pltpu.make_async_copy(acc_hbm, acc_ref, sems.at[1]),
            pltpu.make_async_copy(emb_hbm, table_ref, sems.at[2]),
        ]
        for load in loads:
            load.start()
    bound_copy.wait()
    for (own, step, _, _), (add, extra), out in zip(jobs, inputs, outs):
        half_sums(own, step, add[0] if add else None, extra[0] if extra else None, out, bound_ref, ids_ref, x_ref)
    if old:
        for load in loads:
            load.wait()

        def gather(i, carry):
            for j in range(8):
                u = i * 8 + j
                row = row_ref[0, u]
                old_ref[pl.ds(u, 1), :] = table_ref[pl.ds(row, 1), :]
                old_acc_ref[0, u] = acc_ref[0, row]
            return carry

        lax.fori_loop(0, old_ref.shape[0] // 8, gather, 0)


def sums(name, bound, ids, xt, slots, jobs, after=(), old=()):
    columns = xt.shape[2]
    shapes, operands, kinds = [], [], []
    for own, step, add, extra, kind in jobs:
        operands += [a for a in (add, extra) if a is not None]
        kinds.append((own, step, int(add is not None), int(extra is not None)))
        shapes.append(jax.ShapeDtypeStruct((8, slots, columns), kind))
    out_specs = [VMEM] * len(shapes)
    scratch = [pltpu.SMEM(bound.shape, jnp.int32), pltpu.SemaphoreType.DMA]
    if old:
        rows, embedding, accumulator = old
        shapes += [
            jax.ShapeDtypeStruct((rows.shape[1], columns), F32),
            jax.ShapeDtypeStruct(rows.shape, F32),
            jax.ShapeDtypeStruct(embedding.shape, F32),
        ]
        out_specs += [VMEM, SMEM, VMEM]
        scratch += [
            pltpu.SMEM(rows.shape, jnp.int32),
            pltpu.SMEM(accumulator.shape, F32),
            pltpu.SemaphoreType.DMA((3,)),
        ]
    return pl.pallas_call(
        functools.partial(sums_body, tuple(kinds), len(after), bool(old)),
        in_specs=[ANY, VMEM, VMEM] + [VMEM] * len(operands) + [ANY] * (len(old) + len(after)),
        out_specs=out_specs,
        out_shape=shapes,
        scratch_shapes=scratch,
        compiler_params=pltpu.CompilerParams(vmem_limit_bytes=12 * MIB),
        cost_estimate=COST,
        name=name,
    )(bound, ids, xt, *operands, *old, *after)


def fold_body(here_ref, back_ref, next_ref, *out_refs):
    place = ring_pos(lax.axis_index("core"))[1]
    for d, out_ref in enumerate(out_refs):
        j = lax.rem(place + d, 4)
        for c in range(2):
            m = 2 * j + c
            value = here_ref[m] + (back_ref[m].astype(F32) + next_ref[m].astype(F32))
            out_ref[c] = value.astype(out_ref.dtype)


def fold(here, back, following):
    shape = (2,) + here.shape[1:]
    return pl.pallas_call(
        fold_body,
        in_specs=[VMEM] * 3,
        out_specs=[VMEM] * 4,
        out_shape=[jax.ShapeDtypeStruct(shape, k) for k in (F32, BF, BF, BF)],
        compiler_params=pltpu.CompilerParams(vmem_limit_bytes=12 * MIB),
        cost_estimate=COST,
        name="fold",
    )(here, back, following)


def total_body(a_ref, b_ref, c_ref, d_ref, mine_ref, other_ref):
    core = lax.axis_index("core")
    for out_ref, table in ((other_ref, 1 - core), (mine_ref, core)):
        out_ref[...] = (a_ref[table] + b_ref[table].astype(F32)) + (
            c_ref[table].astype(F32) + d_ref[table].astype(F32)
        )


def total(parts):
    return pl.pallas_call(
        total_body,
        in_specs=[VMEM] * 4,
        out_specs=[VMEM] * 2,
        out_shape=[jax.ShapeDtypeStruct(parts[0].shape[1:], F32)] * 2,
        compiler_params=pltpu.CompilerParams(vmem_limit_bytes=8 * MIB),
        cost_estimate=COST,
        name="total",
    )(*parts)


def square_body(mine_ref, got_ref, grad_ref, square_ref):
    core = lax.axis_index("core")
    slots = mine_ref.shape[0]
    tile = slots // 2
    for i, (ref, half) in enumerate(((mine_ref, core), (got_ref, 1 - core))):
        for at, first in ((0, half * tile), (tile, slots + i * tile)):
            here = pl.ds(pl.multiple_of(first, tile), tile)
            value = ref[at : at + tile, :]
            grad_ref[here, :] = value
            square_ref[:, here] = jnp.sum((value * value).T, axis=0, keepdims=True)


def square(mine, got):
    slots, columns = mine.shape
    return pl.pallas_call(
        square_body,
        in_specs=[VMEM] * 2,
        out_specs=[VMEM] * 2,
        out_shape=[
            jax.ShapeDtypeStruct((2 * slots, columns), F32),
            jax.ShapeDtypeStruct((1, 2 * slots), F32),
        ],
        compiler_params=pltpu.CompilerParams(vmem_limit_bytes=8 * MIB),
        cost_estimate=COST,
        name="square",
    )(mine, got)


def apply_body(
    width, row_ref, live_ref, emb_in, grad_ref, old_ref, s0_ref, s1_ref, old_acc_ref, acc_in,
    emb_out, acc_out, emb_ref, new_ref, new_acc_ref, new_acc_smem, acc_smem, sems,
):
    load = pltpu.make_async_copy(acc_in, acc_smem, sems.at[0])
    load.start()
    emb_ref[...] = emb_in[...]
    slots, columns = old_ref.shape
    mean_square = (s0_ref[...] + s1_ref[...]) / width
    new_acc = old_acc_ref[...] + mean_square
    new_acc_ref[...] = new_acc
    move = pltpu.make_async_copy(new_acc_ref, new_acc_smem, sems.at[1])
    move.start()
    scale = learn_rate / (jnp.sqrt(new_acc) + epsilon)
    scale = jnp.broadcast_to(scale, (columns, slots)).T
    new_ref[...] = old_ref[...] - grad_ref[...] * scale
    live = live_ref[0]

    def step(i, carry):
        for j in range(8):
            u = jnp.minimum(i * 8 + j, live - 1)
            emb_ref[pl.ds(row_ref[0, u], 1), :] = new_ref[pl.ds(u, 1), :]
        return carry

    lax.fori_loop(0, (live + 7) // 8, step, 0)
    load.wait()
    move.wait()
    write = pltpu.make_async_copy(emb_ref, emb_out, sems.at[2])
    write.start()

    def acc_step(i, carry):
        for j in range(8):
            u = jnp.minimum(i * 8 + j, live - 1)
            acc_smem[0, row_ref[0, u]] = new_acc_smem[0, u]
        return carry

    lax.fori_loop(0, (live + 7) // 8, acc_step, 0)
    store = pltpu.make_async_copy(acc_smem, acc_out, sems.at[0])
    store.start()
    store.wait()
    write.wait()


def apply_rows(width, rows, live, embedding, gradient, old, squares, old_acc, accumulator):
    slots = rows.shape[1]
    return pl.pallas_call(
        functools.partial(apply_body, width),
        in_specs=[SMEM, SMEM] + [VMEM] * 6 + [ANY],
        out_specs=[ANY, ANY],
        out_shape=[
            jax.ShapeDtypeStruct(embedding.shape, F32),
            jax.ShapeDtypeStruct(accumulator.shape, F32),
        ],
        scratch_shapes=[
            pltpu.VMEM(embedding.shape, F32),
            pltpu.VMEM(old.shape, F32),
            pltpu.VMEM((1, slots), F32),
            pltpu.SMEM((1, slots), F32),
            pltpu.SMEM(accumulator.shape, F32),
            pltpu.SemaphoreType.DMA((3,)),
        ],
        compiler_params=pltpu.CompilerParams(vmem_limit_bytes=16 * MIB),
        cost_estimate=COST,
        name="apply_rows",
    )(rows, live, embedding, gradient, old, *squares, old_acc, accumulator)


def per_device(pooled_grad, segment_map, unique_rows, live_counts, embedding, accumulator):
    columns = pooled_grad.shape[2]
    slots = unique_rows.shape[1]
    cols = lax.axis_size("col")
    half = slots // 2
    seg = jnp.transpose(segment_map, (1, 2, 0))
    xt, ids, bound = prep(pooled_grad, seg)

    chips = [(z, y) for z in range(4) for y in range(4)]
    index = lambda z, y, c: ((z % 4) * 4 + y % 4) * 2 + c
    owner = ("z", "y", "core")

    def swap(a):
        return lax.ppermute(a, "core", [(0, 1), (1, 0)])

    def shift(a, first, by):
        move = lambda z, y, c: (z + by, y, c) if (c == 0) == first else (z, y + by, c)
        return lax.ppermute(a, owner, [(index(z, y, c), index(*move(z, y, c))) for z, y in chips for c in range(2)])

    run = lambda name, *jobs, **kw: sums(name, bound, ids, xt, half, jobs, **kw)
    sib = lambda step: (False, step, None, None, BF)
    own = lambda step, add, extra=None, kind=BF: (True, step, add, extra, kind)
    (sib_far,) = run("sib_far", sib(2))
    got_far = swap(sib_far)
    sib_next, sib_back = run("sib_next", sib(1), sib(3), after=(sib_far,))
    got_next, got_back = swap(sib_next), swap(sib_back)
    (far,) = run("own_far", own(2, got_far), after=(sib_next,))
    far_got = shift(far, True, 1)
    sib_here, back = run("middle", sib(0), own(3, got_back), after=(far,))
    got_here = swap(sib_here)
    back_got = shift(back, True, -1)
    (following,) = run("own_next", own(1, got_next, far_got), after=(back,))
    next_got = shift(following, True, 1)
    here, old, old_acc, table = run(
        "own_here", own(0, got_here, None, F32), after=(following,), old=(unique_rows, embedding[0], accumulator)
    )
    parts = list(fold(here, back_got, next_got))
    for d in range(1, 4):
        parts[d] = shift(parts[d], False, d)
    mine, other = total(parts)
    gradient, squares = square(mine, swap(other))
    across = lambda a, k: lax.ppermute(a, "col", [(i, i ^ k) for i in range(cols)])
    pair = squares + across(squares, 1)
    squares = (pair, across(pair, 3))
    new_embedding, new_accumulator = apply_rows(
        columns * cols, unique_rows, live_counts, table, gradient, old, squares, old_acc, accumulator
    )
    return (new_embedding[None], new_accumulator)


def solution(mesh):
    owner = ("z", "y", "core")
    split = Mesh(mesh.devices.reshape(4, 4, 2, mesh.devices.shape[1]), owner + ("col",))
    return jax.shard_map(
        per_device,
        mesh=split,
        in_specs=(
            P(owner, None, "col"),
            P(owner, None, None),
            P(owner, None),
            P(owner),
            P(owner, None, "col"),
            P(owner, None),
        ),
        out_specs=(P(owner, None, "col"), P(owner, None)),
        check_vma=False,
    )
```

time: 122 us -> 88.4 us (0.72)
  blocking collectives: 59.1 us -> 0 us
  waiting for transfers between devices: 4.72 us -> 23 us
  starting transfers between devices: 5.04 us -> 18 us
  local copies, waits for them, and re-layouts: 3.86 us -> 1.05 us
  other arithmetic: 1.72 us -> 0.01 us
    all_to_all x1 -> x0, blocking collectives: 59.1 us -> none  [per_device(): spread = lambda a: lax.all_to_all(a, ('z', 'y'), 0, 0, tiled=True)]
    ppermute x2 -> x13, waiting for transfers between devices: 0.01 us -> 23 us  [the longest x6 17.9 us: shift(): lax.ppermute(a, owner, [(index(z, y, c), index(*move(z, y, c))) for z, y...]
    ppermute x2 -> x13, starting transfers between devices: 0.75 us -> 18 us  [the longest x6 12.2 us: shift(): lax.ppermute(a, owner, [(index(z, y, c), index(*move(z, y, c))) for z, y...]
    all_to_all x1 -> x0, waiting for transfers between devices: 4.71 us -> none  [per_device(): lax.all_to_all(jnp.broadcast_to(squares[None], (cols, 1, slots)), 'col',...]
    all_to_all x1 -> x0, starting transfers between devices: 4.29 us -> none  [per_device(): lax.all_to_all(jnp.broadcast_to(squares[None], (cols, 1, slots)), 'col',...]
    unnamed x10 -> x8, local copies, waits for them, and re-layouts: 3.25 us -> 1.05 us
    reduce_max x1 -> x0, other arithmetic: 1.72 us -> none  [per_device(): bound = jnp.max(seg, axis=(1, 2))]
    pallas_call x6 -> x10, Pallas kernels: 39.2 us -> 39 us  [the longest x6 33.9 us: sums(): pl.pallas_call(functools.partial(sums_body, tuple(kinds), len(after), boo...]
  transfers between devices with their start and end apart: 3 -> 13, of which waited for: 1 -> 7; matrix products, arithmetic and copies ran while one was open for 0% -> 0% of each run, Pallas kernels for 6% -> 34%
where the time goes in v2:
time: 88.4 us; the launch traced here: 88.3 us
  Pallas kernels  44.6 us (50%)
  waiting for transfers between devices  23 us (26%)
  starting transfers between devices  18 us (20%)
  between operations  1.64 us (2%)
  local copies, waits for them, and re-layouts  1.05 us (1%)
    pallas_call x6, Pallas kernels, sums(): pl.pallas_call(functools.partial(sums_body, tuple(kinds), len(after), boo...  33.9 us
    ppermute x6, waiting for transfers between devices, shift(): lax.ppermute(a, owner, [(index(z, y, c), index(*move(z, y, c))) for z, y...  17.9 us
    ppermute x6, starting transfers between devices, shift(): lax.ppermute(a, owner, [(index(z, y, c), index(*move(z, y, c))) for z, y...  12.2 us
    pallas_call x1, Pallas kernels, apply_rows(): pl.pallas_call(functools.partial(apply_body, width), in_specs=[SMEM, SMEM...  5.63 us
    pallas_call x1, Pallas kernels, prep(): pl.pallas_call(prep_body, in_specs=[ANY, ANY], out_specs=[VMEM, VMEM, SME...  4.35 us
    ppermute x2, starting transfers between devices, per_device(): lax.ppermute(a, 'col', [(i, i ^ k) for i in range(cols)])  4.33 us
    ppermute x2, waiting for transfers between devices, per_device(): lax.ppermute(a, 'col', [(i, i ^ k) for i in range(cols)])  3.52 us
  transfers between devices with their start and end apart: 13, of which 7 were waited for; matrix products, arithmetic and copies ran while one was open for 0% of the time, Pallas kernels for 34%

profile of v2, /device:TPU:0, one launch (start us, length us, event | category | flops | bytes accessed | tf_op | source)
XLA Modules:
  0.0 88.3 jit_solution(6961392355693411445)
XLA Ops:
  0.6 1.0 %copy-done.1 = s32[1024,32,4]{0,2,1:T(4,128)S(1)} copy-done((s32[1024,32,4]{0,2,1:T(4,128)S(1)}, s32[1024,32,4]{0,2,1:T(4,128)}, u32[]{:S(2)}) %copy-start.1) | copy-done | bytes 524312
  1.7 4.4 %prep.1 = (bf16[32,1024,128]{2,1,0:T(8,128)(2,1)S(1)}, f32[32,8,1024]{2,1,0:T(8,128)S(1)}, s32[32]{0:T(128)S(1)}) custom-call(bf16[1024,32,128]{2,1,0:T(8,128)(2,1)} %x_hbm.1, s32[32,4,1024]{2,1,0:T(4,128)S(1)} %bitcast.4), custom_call_target="tpu_custom_call" | custom-call | flops 1000 | bytes 1000 | tf_op jit(solution)/shard_map/prep/pallas_call | solution.py:60
  6.0 4.1 %sib_far.1.refs_0_ = bf16[8,512,128]{2,1,0:T(8,128)(2,1)S(1)} custom-call(s32[32]{0:T(128)S(1)} %get-tuple-element.23.bound_hbm, f32[32,8,1024]{2,1,0:T(8,128)S(1)} %get-tuple-element.24.ids_ref, bf16[32,1024,128]{2,1,0:T(8,128)(2,1)S(1)} %get-tuple-element.25.x_ref), custom_call_target="tpu_custom_call" | custom-call | flops 1000 | bytes 1000 | tf_op jit(solution)/shard_map/sib_far/pallas_call | solution.py:198
  10.1 0.3 collective-permute-start.1
  10.4 7.4 %sib_next.1 = (bf16[8,512,128]{2,1,0:T(8,128)(2,1)S(1)}, bf16[8,512,128]{2,1,0:T(8,128)(2,1)S(1)}) custom-call(s32[32]{0:T(128)S(1)} %get-tuple-element.23.bound_hbm, f32[32,8,1024]{2,1,0:T(8,128)S(1)} %get-tuple-element.24.ids_ref, bf16[32,1024,128]{2,1,0:T(8,128)(2,1)S(1)} %get-tuple-element.25.x_ref, bf16[8,512,128]{2,1,0:T(8,128)(2,1)S(1)} %sib_far.1.refs_0_), custom_call_target="tpu_custom_call" | custom-call | flops 1000 | bytes 1000 | tf_op jit(solution)/shard_map/sib_next/pallas_call | solution.py:198
  17.8 0.2 collective-permute-start
  18.0 0.4 collective-permute-start.3
  18.4 4.0 %own_far.1.refs_1_ = bf16[8,512,128]{2,1,0:T(8,128)(2,1)S(1)} custom-call(s32[32]{0:T(128)S(1)} %get-tuple-element.23.bound_hbm, f32[32,8,1024]{2,1,0:T(8,128)S(1)} %get-tuple-element.24.ids_ref, bf16[32,1024,128]{2,1,0:T(8,128)(2,1)S(1)} %get-tuple-element.25.x_ref, bf16[8,512,128]{2,1,0:T(8,128)(2,1)S(1)} %collective-permute-done.1.refs_0_, ...), custom_call_target="tpu_custom_call" | custom-call | flops 1000 | bytes 1000 | tf_op jit(solution)/shard_map/own_far/pallas_call | solution.py:198
  22.4 2.1 %collective-permute-start.4 = (bf16[8,512,128]{2,1,0:T(8,128)(2,1)S(1)}, bf16[8,512,128]{2,1,0:T(8,128)(2,1)S(1)}, u32[]{:S(2)}, u32[]{:S(2)}) collective-permute-start(bf16[8,512,128]{2,1,0:T(8,128)(2,1)S(1)} %own_far.1.refs_1_), channel_id=1, source_target_pairs={{0,32},{4,12},{8,40},{12,20},{16,48},{20,28},{24,56},{28,4},{32,64... | collective-permute-start | bytes 3145736 | tf_op jit(solution)/shard_map/ppermute | solution.py:365
  24.6 7.1 %middle.1 = (bf16[8,512,128]{2,1,0:T(8,128)(2,1)S(1)}, bf16[8,512,128]{2,1,0:T(8,128)(2,1)S(1)}) custom-call(s32[32]{0:T(128)S(1)} %get-tuple-element.23.bound_hbm, f32[32,8,1024]{2,1,0:T(8,128)S(1)} %get-tuple-element.24.ids_ref, bf16[32,1024,128]{2,1,0:T(8,128)(2,1)S(1)} %get-tuple-element.25.x_ref, bf16[8,512,128]{2,1,0:T(8,128)(2,1)S(1)} %collective-permute-done.refs_0_, ...), custom_call_target="tpu_custom_call" | custom-call | flops 1000 | bytes 1000 | tf_op jit(solution)/shard_map/middle/pallas_call | solution.py:198
  31.7 0.6 collective-permute-start.2
  32.3 4.0 %collective-permute-start.5 = (bf16[8,512,128]{2,1,0:T(8,128)(2,1)S(1)}, bf16[8,512,128]{2,1,0:T(8,128)(2,1)S(1)}, u32[]{:S(2)}, u32[]{:S(2)}) collective-permute-start(bf16[8,512,128]{2,1,0:T(8,128)(2,1)S(1)} %get-tuple-element.29.refs_2_), channel_id=1, source_target_pairs={{0,96},{4,28},{8,104},{12,4},{16,112},{20,12},{24,120},{28,20},{32... | collective-permute-start | bytes 3145736 | tf_op jit(solution)/shard_map/ppermute | solution.py:365
  36.3 3.4 %collective-permute-done.4.refs_1_ = bf16[8,512,128]{2,1,0:T(8,128)(2,1)S(1)} collective-permute-done((bf16[8,512,128]{2,1,0:T(8,128)(2,1)S(1)}, bf16[8,512,128]{2,1,0:T(8,128)(2,1)S(1)}, u32[]{:S(2)}, u32[]{:S(2)}) %collective-permute-start.4) | collective-permute-done | bytes 1048608 | tf_op jit(solution)/shard_map/ppermute | solution.py:365
  39.7 4.1 %own_next.1.refs_4_ = bf16[8,512,128]{2,1,0:T(8,128)(2,1)S(1)} custom-call(s32[32]{0:T(128)S(1)} %get-tuple-element.23.bound_hbm, f32[32,8,1024]{2,1,0:T(8,128)S(1)} %get-tuple-element.24.ids_ref, bf16[32,1024,128]{2,1,0:T(8,128)(2,1)S(1)} %get-tuple-element.25.x_ref, bf16[8,512,128]{2,1,0:T(8,128)(2,1)S(1)} %collective-permute-done.3.refs_0_, ...), custom_call_target="tpu_custom_call" | custom-call | flops 1000 | bytes 1000 | tf_op jit(solution)/shard_map/own_next/pallas_call | solution.py:198
  43.7 0.3 collective-permute-start.6
  44.1 7.2 %own_here.1 = (f32[8,512,128]{2,1,0:T(8,128)S(1)}, f32[1024,128]{1,0:T(8,128)S(1)}, f32[1,1024]{1,0:T(1,128)S(1)}, f32[8192,128]{1,0:T(8,128)S(1)}) custom-call(s32[32]{0:T(128)S(1)} %get-tuple-element.23.bound_hbm, f32[32,8,1024]{2,1,0:T(8,128)S(1)} %get-tuple-element.24.ids_ref, bf16[32,1024,128]{2,1,0:T(8,128)(2,1)S(1)} %get-tuple-element.25.x_ref, ...), custom_call_target="tpu_custom_call" | custom-call | flops 1000 | bytes 1000 | tf_op jit(solution)/shard_map/own_here/pallas_call | solution.py:198
  51.4 8.7 %collective-permute-done.6.next_ref = bf16[8,512,128]{2,1,0:T(8,128)(2,1)S(1)} collective-permute-done((bf16[8,512,128]{2,1,0:T(8,128)(2,1)S(1)}, bf16[8,512,128]{2,1,0:T(8,128)(2,1)S(1)}, u32[]{:S(2)}, u32[]{:S(2)}) %collective-permute-start.6) | collective-permute-done | bytes 1048608 | tf_op jit(solution)/shard_map/ppermute | solution.py:365
  60.1 0.4 fold.1
  60.5 1.6 %collective-permute-start.7 = (bf16[2,512,128]{2,1,0:T(8,128)(2,1)S(1)}, bf16[2,512,128]{2,1,0:T(8,128)(2,1)S(1)}, u32[]{:S(2)}, u32[]{:S(2)}) collective-permute-start(bf16[2,512,128]{2,1,0:T(8,128)(2,1)S(1)} %get-tuple-element.33), channel_id=1, source_target_pairs={{0,8},{4,36},{8,16},{12,44},{16,24},{20,52},{24,0},{28,60},{32,40}... | collective-permute-start | bytes 786440 | tf_op jit(solution)/shard_map/ppermute | solution.py:365
  62.1 2.7 %collective-permute-start.8 = (bf16[2,512,128]{2,1,0:T(8,128)(2,1)S(1)}, bf16[2,512,128]{2,1,0:T(8,128)(2,1)S(1)}, u32[]{:S(2)}, u32[]{:S(2)}) collective-permute-start(bf16[2,512,128]{2,1,0:T(8,128)(2,1)S(1)} %get-tuple-element.34), channel_id=1, source_target_pairs={{0,16},{4,68},{8,24},{12,76},{16,0},{20,84},{24,8},{28,92},{32,48}... | collective-permute-start | bytes 786440 | tf_op jit(solution)/shard_map/ppermute | solution.py:365
  64.9 1.3 %collective-permute-start.9 = (bf16[2,512,128]{2,1,0:T(8,128)(2,1)S(1)}, bf16[2,512,128]{2,1,0:T(8,128)(2,1)S(1)}, u32[]{:S(2)}, u32[]{:S(2)}) collective-permute-start(bf16[2,512,128]{2,1,0:T(8,128)(2,1)S(1)} %get-tuple-element.35), channel_id=1, source_target_pairs={{0,24},{4,100},{8,0},{12,108},{16,8},{20,116},{24,16},{28,124},{32... | collective-permute-start | bytes 786440 | tf_op jit(solution)/shard_map/ppermute | solution.py:365
  66.2 1.9 %collective-permute-done.7.b_ref = bf16[2,512,128]{2,1,0:T(8,128)(2,1)S(1)} collective-permute-done((bf16[2,512,128]{2,1,0:T(8,128)(2,1)S(1)}, bf16[2,512,128]{2,1,0:T(8,128)(2,1)S(1)}, u32[]{:S(2)}, u32[]{:S(2)}) %collective-permute-start.7) | collective-permute-done | bytes 262176 | tf_op jit(solution)/shard_map/ppermute | solution.py:365
  68.1 3.9 %collective-permute-done.8.c_ref = bf16[2,512,128]{2,1,0:T(8,128)(2,1)S(1)} collective-permute-done((bf16[2,512,128]{2,1,0:T(8,128)(2,1)S(1)}, bf16[2,512,128]{2,1,0:T(8,128)(2,1)S(1)}, u32[]{:S(2)}, u32[]{:S(2)}) %collective-permute-start.8) | collective-permute-done | bytes 262176 | tf_op jit(solution)/shard_map/ppermute | solution.py:365
  72.0 0.1 total.1
  72.1 0.1 collective-permute-start.10
  72.2 1.5 %collective-permute-done.10.got_ref = f32[512,128]{1,0:T(8,128)S(1)} collective-permute-done((f32[512,128]{1,0:T(8,128)S(1)}, f32[512,128]{1,0:T(8,128)S(1)}, u32[]{:S(2)}, u32[]{:S(2)}) %collective-permute-start.10) | collective-permute-done | bytes 262176 | tf_op jit(solution)/shard_map/ppermute | solution.py:361
  73.7 0.2 square.1
  74.0 1.6 %collective-permute-start.11 = (f32[1,1024]{1,0:T(1,128)S(1)}, f32[1,1024]{1,0:T(1,128)S(1)}, u32[]{:S(2)}, u32[]{:S(2)}) collective-permute-start(f32[1,1024]{1,0:T(1,128)S(1)} %get-tuple-element.40), channel_id=1, source_target_pairs={{0,1},{1,0},{2,3},{3,2},{4,5},{5,4},{6,7},{7,6},{8,9},{9,8},{10,11... | collective-permute-start | bytes 12296 | tf_op jit(solution)/shard_map/ppermute | solution.py:389
  75.5 2.1 %collective-permute-done.11 = f32[1,1024]{1,0:T(1,128)S(1)} collective-permute-done((f32[1,1024]{1,0:T(1,128)S(1)}, f32[1,1024]{1,0:T(1,128)S(1)}, u32[]{:S(2)}, u32[]{:S(2)}) %collective-permute-start.11) | collective-permute-done | bytes 4128 | tf_op jit(solution)/shard_map/ppermute | solution.py:389
  77.7 2.8 %collective-permute-start.12 = (f32[1,1024]{1,0:T(1,128)S(1)}, f32[1,1024]{1,0:T(1,128)S(1)}, u32[]{:S(2)}, u32[]{:S(2)}) collective-permute-start(f32[1,1024]{1,0:T(1,128)S(1)} %add.3.s0_ref), channel_id=1, source_target_pairs={{0,3},{1,2},{2,1},{3,0},{4,7},{5,6},{6,5},{7,4},{8,11},{9,10},{10,... | collective-permute-start | bytes 12296 | tf_op jit(solution)/shard_map/ppermute | solution.py:389
  81.1 1.4 %collective-permute-done.12.s1_ref = f32[1,1024]{1,0:T(1,128)S(1)} collective-permute-done((f32[1,1024]{1,0:T(1,128)S(1)}, f32[1,1024]{1,0:T(1,128)S(1)}, u32[]{:S(2)}, u32[]{:S(2)}) %collective-permute-start.12) | collective-permute-done | bytes 4128 | tf_op jit(solution)/shard_map/ppermute | solution.py:389
  82.5 5.6 %apply_rows.1 = (f32[8192,128]{1,0:T(8,128)}, f32[1,8192]{1,0:T(1,128)}) custom-call(s32[1,1024]{1,0:T(1,128)S(1)} %copy-done.3, s32[1]{0:T(128)S(6)} %copy.8.live_ref, f32[8192,128]{1,0:T(8,128)S(1)} %get-tuple-element.30.emb_in, f32[1024,128]{1,0:T(8,128)S(1)} %get-tuple-element.38.grad_ref, f32[1024,128]{1,0:T(8,128)S(1)} %get-tuple-element.39.old_ref, ...), custom_call_target="tpu_custom_call" | custom-call | flops 1000 | bytes 1000 | tf_op jit(solution)/shard_map/apply_rows/pallas_call | solution.py:326
  (14 shorter events, 0.0 us)
Async XLA Ops:
  0.6 1.0 %copy-start.1 = (s32[1024,32,4]{0,2,1:T(4,128)S(1)}, s32[1024,32,4]{0,2,1:T(4,128)}, u32[]{:S(2)}) copy-start(s32[1024,32,4]{0,2,1:T(4,128)} %param.7) | copy-start | bytes 1572868
  10.1 8.3 %collective-permute-start.1 = (bf16[8,512,128]{2,1,0:T(8,128)(2,1)S(1)}, bf16[8,512,128]{2,1,0:T(8,128)(2,1)S(1)}, u32[]{:S(2)}, u32[]{:S(2)}) collective-permute-start(bf16[8,512,128]{2,1,0:T(8,128)(2,1)S(1)} %sib_far.1.refs_0_), channel_id=1, source_target_pairs={{0,4},{4,0},{1,5},{5,1},{2,6},{6,2},{3,7},{7,3},{8,12},{12,8},{9,1... | collective-permute-start | bytes 3145736 | tf_op jit(solution)/shard_map/ppermute | solution.py:361
  17.8 6.7 %collective-permute-start = (bf16[8,512,128]{2,1,0:T(8,128)(2,1)S(1)}, bf16[8,512,128]{2,1,0:T(8,128)(2,1)S(1)}, u32[]{:S(2)}, u32[]{:S(2)}) collective-permute-start(bf16[8,512,128]{2,1,0:T(8,128)(2,1)S(1)} %get-tuple-element.26), channel_id=1, source_target_pairs={{0,4},{4,0},{1,5},{5,1},{2,6},{6,2},{3,7},{7,3},{8,12},{12,8},{9,1... | collective-permute-start | bytes 3145736 | tf_op jit(solution)/shard_map/ppermute | solution.py:361
  18.0 18.3 %collective-permute-start.3 = (bf16[8,512,128]{2,1,0:T(8,128)(2,1)S(1)}, bf16[8,512,128]{2,1,0:T(8,128)(2,1)S(1)}, u32[]{:S(2)}, u32[]{:S(2)}) collective-permute-start(bf16[8,512,128]{2,1,0:T(8,128)(2,1)S(1)} %get-tuple-element.27.refs_1_), channel_id=1, source_target_pairs={{0,4},{4,0},{1,5},{5,1},{2,6},{6,2},{3,7},{7,3},{8,12},{12,8},{9,1... | collective-permute-start | bytes 3145736 | tf_op jit(solution)/shard_map/ppermute | solution.py:361
  22.4 17.2 %collective-permute-start.4 = (bf16[8,512,128]{2,1,0:T(8,128)(2,1)S(1)}, bf16[8,512,128]{2,1,0:T(8,128)(2,1)S(1)}, u32[]{:S(2)}, u32[]{:S(2)}) collective-permute-start(bf16[8,512,128]{2,1,0:T(8,128)(2,1)S(1)} %own_far.1.refs_1_), channel_id=1, source_target_pairs={{0,32},{4,12},{8,40},{12,20},{16,48},{20,28},{24,56},{28,4},{32,64... | collective-permute-start | bytes 3145736 | tf_op jit(solution)/shard_map/ppermute | solution.py:365
  31.7 12.4 %collective-permute-start.2 = (bf16[8,512,128]{2,1,0:T(8,128)(2,1)S(1)}, bf16[8,512,128]{2,1,0:T(8,128)(2,1)S(1)}, u32[]{:S(2)}, u32[]{:S(2)}) collective-permute-start(bf16[8,512,128]{2,1,0:T(8,128)(2,1)S(1)} %get-tuple-element.28), channel_id=1, source_target_pairs={{0,4},{4,0},{1,5},{5,1},{2,6},{6,2},{3,7},{7,3},{8,12},{12,8},{9,1... | collective-permute-start | bytes 3145736 | tf_op jit(solution)/shard_map/ppermute | solution.py:361
  32.3 11.8 %copy-start = (f32[1,8192,128]{2,1,0:T(8,128)S(1)}, f32[1,8192,128]{2,1,0:T(8,128)}, u32[]{:S(2)}) copy-start(f32[1,8192,128]{2,1,0:T(8,128)} %param.10) | copy-start | bytes 12582916
  32.3 11.9 %copy-start.2 = (f32[1,8192]{1,0:T(1,128)S(1)}, f32[1,8192]{1,0:T(1,128)}, u32[]{:S(2)}) copy-start(f32[1,8192]{1,0:T(1,128)} %acc_in.1) | copy-start | bytes 98308
  32.3 11.9 %copy-start.3 = (s32[1,1024]{1,0:T(1,128)S(1)}, s32[1,1024]{1,0:T(1,128)}, u32[]{:S(2)}) copy-start(s32[1,1024]{1,0:T(1,128)} %row_ref.1) | copy-start | bytes 12292
  32.3 19.1 %collective-permute-start.5 = (bf16[8,512,128]{2,1,0:T(8,128)(2,1)S(1)}, bf16[8,512,128]{2,1,0:T(8,128)(2,1)S(1)}, u32[]{:S(2)}, u32[]{:S(2)}) collective-permute-start(bf16[8,512,128]{2,1,0:T(8,128)(2,1)S(1)} %get-tuple-element.29.refs_2_), channel_id=1, source_target_pairs={{0,96},{4,28},{8,104},{12,4},{16,112},{20,12},{24,120},{28,20},{32... | collective-permute-start | bytes 3145736 | tf_op jit(solution)/shard_map/ppermute | solution.py:365
  43.7 16.3 %collective-permute-start.6 = (bf16[8,512,128]{2,1,0:T(8,128)(2,1)S(1)}, bf16[8,512,128]{2,1,0:T(8,128)(2,1)S(1)}, u32[]{:S(2)}, u32[]{:S(2)}) collective-permute-start(bf16[8,512,128]{2,1,0:T(8,128)(2,1)S(1)} %own_next.1.refs_4_), channel_id=1, source_target_pairs={{0,32},{4,12},{8,40},{12,20},{16,48},{20,28},{24,56},{28,4},{32,64... | collective-permute-start | bytes 3145736 | tf_op jit(solution)/shard_map/ppermute | solution.py:365
  60.5 7.7 %collective-permute-start.7 = (bf16[2,512,128]{2,1,0:T(8,128)(2,1)S(1)}, bf16[2,512,128]{2,1,0:T(8,128)(2,1)S(1)}, u32[]{:S(2)}, u32[]{:S(2)}) collective-permute-start(bf16[2,512,128]{2,1,0:T(8,128)(2,1)S(1)} %get-tuple-element.33), channel_id=1, source_target_pairs={{0,8},{4,36},{8,16},{12,44},{16,24},{20,52},{24,0},{28,60},{32,40}... | collective-permute-start | bytes 786440 | tf_op jit(solution)/shard_map/ppermute | solution.py:365
  62.1 9.9 %collective-permute-start.8 = (bf16[2,512,128]{2,1,0:T(8,128)(2,1)S(1)}, bf16[2,512,128]{2,1,0:T(8,128)(2,1)S(1)}, u32[]{:S(2)}, u32[]{:S(2)}) collective-permute-start(bf16[2,512,128]{2,1,0:T(8,128)(2,1)S(1)} %get-tuple-element.34), channel_id=1, source_target_pairs={{0,16},{4,68},{8,24},{12,76},{16,0},{20,84},{24,8},{28,92},{32,48}... | collective-permute-start | bytes 786440 | tf_op jit(solution)/shard_map/ppermute | solution.py:365
  64.9 7.2 %collective-permute-start.9 = (bf16[2,512,128]{2,1,0:T(8,128)(2,1)S(1)}, bf16[2,512,128]{2,1,0:T(8,128)(2,1)S(1)}, u32[]{:S(2)}, u32[]{:S(2)}) collective-permute-start(bf16[2,512,128]{2,1,0:T(8,128)(2,1)S(1)} %get-tuple-element.35), channel_id=1, source_target_pairs={{0,24},{4,100},{8,0},{12,108},{16,8},{20,116},{24,16},{28,124},{32... | collective-permute-start | bytes 786440 | tf_op jit(solution)/shard_map/ppermute | solution.py:365
  72.1 1.6 %collective-permute-start.10 = (f32[512,128]{1,0:T(8,128)S(1)}, f32[512,128]{1,0:T(8,128)S(1)}, u32[]{:S(2)}, u32[]{:S(2)}) collective-permute-start(f32[512,128]{1,0:T(8,128)S(1)} %get-tuple-element.37), channel_id=1, source_target_pairs={{0,4},{4,0},{1,5},{5,1},{2,6},{6,2},{3,7},{7,3},{8,12},{12,8},{9,1... | collective-permute-start | bytes 786440 | tf_op jit(solution)/shard_map/ppermute | solution.py:361
  74.0 3.7 %collective-permute-start.11 = (f32[1,1024]{1,0:T(1,128)S(1)}, f32[1,1024]{1,0:T(1,128)S(1)}, u32[]{:S(2)}, u32[]{:S(2)}) collective-permute-start(f32[1,1024]{1,0:T(1,128)S(1)} %get-tuple-element.40), channel_id=1, source_target_pairs={{0,1},{1,0},{2,3},{3,2},{4,5},{5,4},{6,7},{7,6},{8,9},{9,8},{10,11... | collective-permute-start | bytes 12296 | tf_op jit(solution)/shard_map/ppermute | solution.py:389
  77.7 4.8 %collective-permute-start.12 = (f32[1,1024]{1,0:T(1,128)S(1)}, f32[1,1024]{1,0:T(1,128)S(1)}, u32[]{:S(2)}, u32[]{:S(2)}) collective-permute-start(f32[1,1024]{1,0:T(1,128)S(1)} %add.3.s0_ref), channel_id=1, source_target_pairs={{0,3},{1,2},{2,1},{3,0},{4,7},{5,6},{6,5},{7,4},{8,11},{9,10},{10,... | collective-permute-start | bytes 12296 | tf_op jit(solution)/shard_map/ppermute | solution.py:389

commit v3 on v2

v3 whole, which is shorter than its diff:
```python
import functools

import jax
import jax.numpy as jnp
from jax import lax
from jax.experimental import pallas as pl
from jax.experimental.pallas import tpu as pltpu
from jax.sharding import Mesh
from jax.sharding import PartitionSpec as P

learn_rate = 0.5
epsilon = 1e-08
MIB = 2**20
SCALE = 2.0
BF = jnp.bfloat16
F32 = jnp.float32
VMEM = pl.BlockSpec(memory_space=pltpu.VMEM)
SMEM = pl.BlockSpec(memory_space=pltpu.SMEM)
ANY = pl.BlockSpec(memory_space=pl.ANY)


def cost(us):
    return pl.CostEstimate(flops=int(us * SCALE * 1.15e9), transcendentals=0, bytes_accessed=int(us * SCALE * 3.6e6))


def prep_body(x_hbm, seg_hbm, o_ref, ids_ref, bound_ref, x_ref, seg_ref, sems):
    batch = x_ref.shape[0]
    block = 128
    blocks = batch // block
    seg_copy = pltpu.make_async_copy(seg_hbm, seg_ref, sems.at[blocks])
    seg_copy.start()
    copies = []
    for i in range(blocks):
        here = pl.ds(i * block, block)
        copies.append(pltpu.make_async_copy(x_hbm.at[here], x_ref.at[here], sems.at[i]))
        copies[-1].start()
    seg_copy.wait()
    for t in range(seg_ref.shape[0]):
        last = jnp.max(seg_ref[t], axis=(0, 1), keepdims=True)
        bound_ref[t : t + 1, :] = jnp.broadcast_to(last, (1, bound_ref.shape[1]))
    seg = [seg_ref[:, h, :] for h in range(4)]
    same = lambda a, b: jnp.where(seg[a] == seg[b], 1, 0)
    e01, e02, e03 = same(0, 1), same(0, 2), same(0, 3)
    e12, e13, e23 = same(1, 2), same(1, 3), same(2, 3)
    rows = [
        seg[0],
        jnp.where(e01 > 0, -1, seg[1]),
        jnp.where(e02 + e12 > 0, -1, seg[2]),
        jnp.where(e03 + e13 + e23 > 0, -1, seg[3]),
        1 + e01 + e02 + e03,
        1 + e12 + e13,
        1 + e23,
        jnp.ones_like(e01),
    ]
    for r, value in enumerate(rows):
        ids_ref[:, r, :] = value.astype(F32)
    for i in range(blocks):
        here = pl.ds(i * block, block)
        copies[i].wait()
        o_ref[:, here, :] = jnp.swapaxes(x_ref[here], 0, 1)


def prep(pooled, seg):
    batch, tables, columns = pooled.shape
    return pl.pallas_call(
        prep_body,
        in_specs=[pl.BlockSpec(memory_space=pltpu.HBM)] * 2,
        out_specs=[VMEM] * 3,
        out_shape=[
            jax.ShapeDtypeStruct((tables, batch, columns), BF),
            jax.ShapeDtypeStruct((tables, 8, batch), F32),
            jax.ShapeDtypeStruct((tables, 128), jnp.int32),
        ],
        scratch_shapes=[
            pltpu.VMEM(pooled.shape, BF),
            pltpu.VMEM(seg.shape, jnp.int32),
            pltpu.SemaphoreType.DMA((batch // 128 + 1,)),
        ],
        compiler_params=pltpu.CompilerParams(vmem_limit_bytes=40 * MIB),
        cost_estimate=cost(4),
        name="prep",
    )(pooled, seg)


def tile_sum(ids, weights, x, first, rows):
    batch = x.shape[0]
    number = lax.broadcasted_iota(jnp.int32, (rows, batch), 0).astype(F32).astype(BF)
    local = (ids - first).astype(BF)
    hit = jnp.zeros((rows, batch), BF)
    for h in range(3, -1, -1):
        here = number == jnp.broadcast_to(local[h : h + 1], (rows, batch))
        hit = jnp.where(here, jnp.broadcast_to(weights[4 + h : 5 + h], (rows, batch)), hit)
    return jnp.dot(hit, x, preferred_element_type=F32)


def ring_pos(half):
    at_z, at_y = lax.axis_index("z"), lax.axis_index("y")
    return jnp.where(half == 0, at_z, at_y), jnp.where(half == 0, at_y, at_z)


def half_sums(own, step, parts, add_ref, extra_ref, out_refs, bound_ref, flag_ref, ids_ref, x_ref):
    core = lax.axis_index("core")
    half = core if own else 1 - core
    place = lax.rem(ring_pos(half)[0] + step, 4)
    columns = out_refs[0].shape[2]
    tile = 256
    slots = 2 * tile

    def put(m, part, value):
        here = pl.ds(part * tile, tile)
        if add_ref is not None:
            value = value + add_ref[m, here, :].astype(F32)
        if extra_ref is not None:
            value = value + extra_ref[m].astype(F32)
        if len(out_refs) == len(parts):
            out_refs[parts.index(part)][m] = value.astype(BF)
        else:
            out_refs[0][m, here, :] = value.astype(out_refs[0].dtype)

    def chip_of(j):
        return jnp.where(half == 0, place * 4 + j, j * 4 + place)

    later = [slots + lax.rem(half + c, 2) * tile for c in range(2)]
    if 1 in parts:
        for j in range(4):
            for c in range(2):
                last = jnp.max(bound_ref[pl.ds(2 * chip_of(j) + c, 1), :])
                flag_ref[2 * j + c] = (last >= later[c]).astype(jnp.int32)

    def chip_sums(j, carry):
        chip = chip_of(j)

        def table_sums(wanted):
            for c in range(2):
                ids = ids_ref[2 * chip + c]
                weights = ids.astype(BF)
                x = x_ref[2 * chip + c]
                if 0 in parts:
                    put(2 * j + c, 0, tile_sum(ids, weights, x, (half * tile).astype(F32), tile))
                if 1 in parts:
                    if wanted[c]:
                        value = tile_sum(ids, weights, x, later[c].astype(F32), tile)
                    else:
                        value = jnp.zeros((tile, columns), F32)
                    put(2 * j + c, 1, value)

        if 1 not in parts:
            table_sums((False, False))
            return carry
        filled = [flag_ref[2 * j + c] == 1 for c in range(2)]
        for case in range(4):
            wanted = (bool(case & 1), bool(case & 2))
            here = jnp.logical_and(filled[0] == wanted[0], filled[1] == wanted[1])
            pl.when(here)(functools.partial(table_sums, wanted))
        return carry

    lax.fori_loop(0, 4, chip_sums, 0)


def sums_body(jobs, afters, bound_ref, ids_ref, x_ref, *refs):
    refs = list(refs)
    take = lambda n: [refs.pop(0) for _ in range(n)]
    inputs = [[take(1)[0] if has else None for has in given] for _, _, _, given, _ in jobs]
    take(afters)
    outs = [take(count) for _, _, _, _, count in jobs]
    (flag_ref,) = take(1)
    for (own, step, parts, _, _), (add, extra), out in zip(jobs, inputs, outs):
        half_sums(own, step, parts, add, extra, out, bound_ref, flag_ref, ids_ref, x_ref)


def sums(name, bound, ids, xt, slots, jobs, after=()):
    columns = xt.shape[2]
    shapes, operands, kinds = [], [], []
    for own, step, parts, given, split, kind in jobs:
        operands += [a for a in given if a is not None]
        count = len(parts) if split else 1
        kinds.append((own, step, parts, tuple(a is not None for a in given), count))
        shapes += [jax.ShapeDtypeStruct((8, slots * len(parts) // (2 * count), columns), kind)] * count
    work = sum(len(job[2]) for job in jobs)
    return pl.pallas_call(
        functools.partial(sums_body, tuple(kinds), len(after)),
        in_specs=[VMEM] * (3 + len(operands)) + [ANY] * len(after),
        out_specs=[VMEM] * len(shapes),
        out_shape=shapes,
        scratch_shapes=[pltpu.SMEM((8,), jnp.int32)],
        compiler_params=pltpu.CompilerParams(vmem_limit_bytes=12 * MIB),
        cost_estimate=cost(2 * work),
        name=name,
    )(bound, ids, xt, *operands, *after)


def old_body(row_hbm, emb_hbm, acc_hbm, after_ref, old_ref, old_acc_ref, table_ref, row_ref, acc_ref, sems):
    loads = [
        pltpu.make_async_copy(row_hbm, row_ref, sems.at[0]),
        pltpu.make_async_copy(acc_hbm, acc_ref, sems.at[1]),
        pltpu.make_async_copy(emb_hbm, table_ref, sems.at[2]),
    ]
    for load in loads:
        load.start()
    for load in loads:
        load.wait()

    def gather(i, carry):
        for j in range(8):
            u = i * 8 + j
            row = row_ref[0, u]
            old_ref[pl.ds(u, 1), :] = table_ref[pl.ds(row, 1), :]
            old_acc_ref[0, u] = acc_ref[0, row]
        return carry

    lax.fori_loop(0, old_ref.shape[0] // 8, gather, 0)


def old_values(rows, embedding, accumulator, after):
    return pl.pallas_call(
        old_body,
        in_specs=[ANY] * 4,
        out_specs=[VMEM, SMEM, VMEM],
        out_shape=[
            jax.ShapeDtypeStruct((rows.shape[1], embedding.shape[1]), F32),
            jax.ShapeDtypeStruct(rows.shape, F32),
            jax.ShapeDtypeStruct(embedding.shape, F32),
        ],
        scratch_shapes=[
            pltpu.SMEM(rows.shape, jnp.int32),
            pltpu.SMEM(accumulator.shape, F32),
            pltpu.SemaphoreType.DMA((3,)),
        ],
        compiler_params=pltpu.CompilerParams(vmem_limit_bytes=12 * MIB),
        cost_estimate=cost(4),
        name="old_values",
    )(rows, embedding, accumulator, after)


def fold_body(here_ref, next_low, next_high, back_low, back_high, *out_refs):
    place = ring_pos(lax.axis_index("core"))[1]
    tile = next_low.shape[1]
    for d, out_ref in enumerate(out_refs):
        j = lax.rem(place + d, 4)
        for c in range(2):
            m = 2 * j + c
            for part, (next_ref, back_ref) in enumerate(((next_low, back_low), (next_high, back_high))):
                here = pl.ds(part * tile, tile)
                value = here_ref[m, here, :] + (next_ref[m].astype(F32) + back_ref[m].astype(F32))
                out_ref[c, here, :] = value.astype(out_ref.dtype)


def fold(here, *pieces):
    shape = (2,) + here.shape[1:]
    return pl.pallas_call(
        fold_body,
        in_specs=[VMEM] * 5,
        out_specs=[VMEM] * 4,
        out_shape=[jax.ShapeDtypeStruct(shape, k) for k in (F32, BF, BF, BF)],
        compiler_params=pltpu.CompilerParams(vmem_limit_bytes=12 * MIB),
        cost_estimate=cost(0.4),
        name="fold",
    )(here, *pieces)


def total_body(a_ref, b_ref, c_ref, d_ref, after_ref, mine_ref, other_ref):
    core = lax.axis_index("core")
    for out_ref, table in ((other_ref, 1 - core), (mine_ref, core)):
        out_ref[...] = (a_ref[table] + b_ref[table].astype(F32)) + (
            c_ref[table].astype(F32) + d_ref[table].astype(F32)
        )


def total(parts, after):
    return pl.pallas_call(
        total_body,
        in_specs=[VMEM] * 4 + [ANY],
        out_specs=[VMEM] * 2,
        out_shape=[jax.ShapeDtypeStruct(parts[0].shape[1:], F32)] * 2,
        compiler_params=pltpu.CompilerParams(vmem_limit_bytes=8 * MIB),
        cost_estimate=cost(0.3),
        name="total",
    )(*parts, after)


def square_body(mine_ref, got_ref, grad_ref, square_ref):
    core = lax.axis_index("core")
    slots = mine_ref.shape[0]
    tile = slots // 2
    for i, (ref, half) in enumerate(((mine_ref, core), (got_ref, 1 - core))):
        for at, first in ((0, half * tile), (tile, slots + i * tile)):
            here = pl.ds(pl.multiple_of(first, tile), tile)
            value = ref[at : at + tile, :]
            grad_ref[here, :] = value
            square_ref[:, here] = jnp.sum((value * value).T, axis=0, keepdims=True)


def square(mine, got):
    slots, columns = mine.shape
    return pl.pallas_call(
        square_body,
        in_specs=[VMEM] * 2,
        out_specs=[VMEM] * 2,
        out_shape=[
            jax.ShapeDtypeStruct((2 * slots, columns), F32),
            jax.ShapeDtypeStruct((1, 2 * slots), F32),
        ],
        compiler_params=pltpu.CompilerParams(vmem_limit_bytes=8 * MIB),
        cost_estimate=cost(0.3),
        name="square",
    )(mine, got)


def apply_body(
    width, row_hbm, live_hbm, emb_in, grad_ref, old_ref, s0_ref, s1_ref, old_acc_ref, acc_in,
    emb_out, acc_out, emb_ref, new_ref, new_acc_ref, new_acc_smem, acc_ref, row_ref, live_ref, sems,
):
    loads = [
        pltpu.make_async_copy(row_hbm, row_ref, sems.at[0]),
        pltpu.make_async_copy(live_hbm, live_ref, sems.at[1]),
        pltpu.make_async_copy(acc_in, acc_ref, sems.at[2]),
    ]
    for load in loads:
        load.start()
    slots, columns = old_ref.shape
    new_acc = old_acc_ref[...] + (s0_ref[...] + s1_ref[...]) / width
    new_acc_ref[...] = new_acc
    loads.append(pltpu.make_async_copy(new_acc_ref, new_acc_smem, sems.at[3]))
    loads[-1].start()
    emb_ref[...] = emb_in[...]
    scale = learn_rate / (jnp.sqrt(new_acc) + epsilon)
    scale = jnp.broadcast_to(scale, (columns, slots)).T
    new_ref[...] = old_ref[...] - grad_ref[...] * scale
    for load in loads:
        load.wait()
    live = live_ref[0]

    def put(u):
        row = row_ref[0, u]
        emb_ref[pl.ds(row, 1), :] = new_ref[pl.ds(u, 1), :]
        acc_ref[0, row] = new_acc_smem[0, u]

    def step(i, carry):
        for j in range(8):
            put(i * 8 + j)
        return carry

    def last(u, carry):
        put(u)
        return carry

    lax.fori_loop(0, live // 8, step, 0)
    lax.fori_loop(live // 8 * 8, live, last, 0)
    stores = [
        pltpu.make_async_copy(emb_ref, emb_out, sems.at[0]),
        pltpu.make_async_copy(acc_ref, acc_out, sems.at[1]),
    ]
    for store in stores:
        store.start()
    for store in stores:
        store.wait()


def apply_rows(width, rows, live, embedding, gradient, old, squares, old_acc, accumulator):
    return pl.pallas_call(
        functools.partial(apply_body, width),
        in_specs=[ANY, ANY] + [VMEM] * 6 + [ANY],
        out_specs=[ANY, ANY],
        out_shape=[
            jax.ShapeDtypeStruct(embedding.shape, F32),
            jax.ShapeDtypeStruct(accumulator.shape, F32),
        ],
        scratch_shapes=[
            pltpu.VMEM(embedding.shape, F32),
            pltpu.VMEM(old.shape, F32),
            pltpu.VMEM(rows.shape, F32),
            pltpu.SMEM(rows.shape, F32),
            pltpu.SMEM(accumulator.shape, F32),
            pltpu.SMEM(rows.shape, jnp.int32),
            pltpu.SMEM(live.shape, jnp.int32),
            pltpu.SemaphoreType.DMA((4,)),
        ],
        compiler_params=pltpu.CompilerParams(vmem_limit_bytes=16 * MIB),
        cost_estimate=cost(6),
        name="apply_rows",
    )(rows, live, embedding, gradient, old, *squares, old_acc, accumulator)


def per_device(pooled_grad, segment_map, unique_rows, live_counts, embedding, accumulator):
    columns = pooled_grad.shape[2]
    slots = unique_rows.shape[1]
    cols = lax.axis_size("col")
    half = slots // 2
    seg = jnp.transpose(segment_map, (1, 2, 0))
    xt, ids, bound = prep(pooled_grad, seg)

    chips = [(z, y) for z in range(4) for y in range(4)]
    index = lambda z, y, c: ((z % 4) * 4 + y % 4) * 2 + c
    owner = ("z", "y", "core")

    def swap(a):
        return lax.ppermute(a, "core", [(0, 1), (1, 0)])

    def shift(a, first, by):
        move = lambda z, y, c: (z + by, y, c) if (c == 0) == first else (z, y + by, c)
        return lax.ppermute(a, owner, [(index(z, y, c), index(*move(z, y, c))) for z, y in chips for c in range(2)])

    run = lambda name, *jobs, **kw: sums(name, bound, ids, xt, half, jobs, **kw)
    both = (0, 1)
    sib = lambda step: (False, step, both, (None, None), False, BF)
    own = lambda step, parts, add, extra=None, split=True, kind=BF: (True, step, parts, (add, extra), split, kind)
    (sib_far,) = run("sib_far", sib(2))
    got_far = swap(sib_far)
    sib_next, sib_back, sib_here = run("sib_next", sib(1), sib(3), sib(0), after=(sib_far,))
    got_next, got_back = swap(sib_next), swap(sib_back)
    far_low, far_high = run("own_far", own(2, both, got_far), after=(sib_next,))
    low_got, high_got = shift(far_low, True, 1), shift(far_high, True, -1)
    next_high, back_low = run("free", own(1, (1,), got_next), own(3, (0,), got_back), after=(far_low,))
    next_high_got, back_low_got = shift(next_high, True, 1), shift(back_low, True, -1)
    next_low, back_high = run(
        "bound", own(1, (0,), got_next, low_got), own(3, (1,), got_back, high_got), after=(next_high,)
    )
    next_low_got, back_high_got = shift(next_low, True, 1), shift(back_high, True, -1)
    got_here = swap(sib_here)
    (here,) = run("own_here", own(0, both, got_here, None, False, F32), after=(next_low,))
    parts = list(fold(here, next_low_got, next_high_got, back_low_got, back_high_got))
    old, old_acc, table = old_values(unique_rows, embedding[0], accumulator, parts[1])
    for d in (3, 1, 2):
        parts[d] = shift(parts[d], False, d)
    mine, other = total(parts, old)
    gradient, squares = square(mine, swap(other))
    across = lambda a, k: lax.ppermute(a, "col", [(i, i ^ k) for i in range(cols)])
    pair = squares + across(squares, 1)
    squares = (pair, across(pair, 3))
    new_embedding, new_accumulator = apply_rows(
        columns * cols, unique_rows, live_counts, table, gradient, old, squares, old_acc, accumulator
    )
    return (new_embedding[None], new_accumulator)


def solution(mesh):
    owner = ("z", "y", "core")
    split = Mesh(mesh.devices.reshape(4, 4, 2, mesh.devices.shape[1]), owner + ("col",))
    return jax.shard_map(
        per_device,
        mesh=split,
        in_specs=(
            P(owner, None, "col"),
            P(owner, None, None),
            P(owner, None),
            P(owner),
            P(owner, None, "col"),
            P(owner, None),
        ),
        out_specs=(P(owner, None, "col"), P(owner, None)),
        check_vma=False,
    )
```

time: 88.4 us -> 79 us (0.89)
  waiting for transfers between devices: 23 us -> 10.9 us
  starting transfers between devices: 18 us -> 22.3 us
  Pallas kernels: 44.6 us -> 42.5 us
    ppermute x6 -> x9, waiting for transfers between devices: 17.9 us -> 5.83 us  [shift(): lax.ppermute(a, owner, [(index(z, y, c), index(*move(z, y, c))) for z, y...]
    ppermute x6 -> x9, starting transfers between devices: 12.2 us -> 16.8 us  [shift(): lax.ppermute(a, owner, [(index(z, y, c), index(*move(z, y, c))) for z, y...]
    pallas_call x10 -> x11, Pallas kernels: 44.4 us -> 42.3 us  [the longest x6 29 us: sums(): pl.pallas_call(functools.partial(sums_body, tuple(kinds), len(after)), in...]
  transfers between devices with their start and end apart: 13 -> 16, of which waited for: 7 -> 6; matrix products, arithmetic and copies ran while one was open for 0% -> 0% of each run, Pallas kernels for 34% -> 38%
where the time goes in v3:
time: 79 us; the launch traced here: 78.3 us
  Pallas kernels  42.5 us (54%)
  starting transfers between devices  22.3 us (28%)
  waiting for transfers between devices  10.9 us (14%)
  between operations  1.63 us (2%)
  local copies, waits for them, and re-layouts  1.05 us (1%)
    pallas_call x6, Pallas kernels, sums(): pl.pallas_call(functools.partial(sums_body, tuple(kinds), len(after)), in...  29 us
    ppermute x9, starting transfers between devices, shift(): lax.ppermute(a, owner, [(index(z, y, c), index(*move(z, y, c))) for z, y...  16.8 us
    ppermute x9, waiting for transfers between devices, shift(): lax.ppermute(a, owner, [(index(z, y, c), index(*move(z, y, c))) for z, y...  5.83 us
    pallas_call x1, Pallas kernels, apply_rows(): pl.pallas_call(functools.partial(apply_body, width), in_specs=[ANY, ANY]...  4.67 us
    ppermute x2, starting transfers between devices, per_device(): lax.ppermute(a, 'col', [(i, i ^ k) for i in range(cols)])  4.33 us
    pallas_call x1, Pallas kernels, old_values(): pl.pallas_call(old_body, in_specs=[ANY] * 4, out_specs=[VMEM, SMEM, VMEM]...  4.1 us
    pallas_call x1, Pallas kernels, prep(): pl.pallas_call(prep_body, in_specs=[pl.BlockSpec(memory_space=pltpu.HBM)]...  4.1 us
    ppermute x2, waiting for transfers between devices, per_device(): lax.ppermute(a, 'col', [(i, i ^ k) for i in range(cols)])  3.52 us
  transfers between devices with their start and end apart: 16, of which 6 were waited for; matrix products, arithmetic and copies ran while one was open for 0% of the time, Pallas kernels for 38%

profile of v3, /device:TPU:0, one launch (start us, length us, event | category | flops | bytes accessed | tf_op | source)
XLA Modules:
  0.0 78.3 jit_solution(9748827985021613760)
XLA Ops:
  0.6 1.0 %copy-done.1 = s32[1024,32,4]{0,2,1:T(4,128)S(1)} copy-done((s32[1024,32,4]{0,2,1:T(4,128)S(1)}, s32[1024,32,4]{0,2,1:T(4,128)}, u32[]{:S(2)}) %copy-start.1) | copy-done | bytes 524312
  1.7 4.1 %prep.1 = (bf16[32,1024,128]{2,1,0:T(8,128)(2,1)S(1)}, f32[32,8,1024]{2,1,0:T(8,128)S(1)}, s32[32,128]{1,0:T(8,128)S(1)}) custom-call(bf16[1024,32,128]{2,1,0:T(8,128)(2,1)} %x_hbm.1, s32[32,4,1024]{2,1,0:T(4,128)S(1)} %bitcast.4), custom_call_target="tpu_custom_call" | custom-call | flops 9200000000 | bytes 28800000 | tf_op jit(solution)/shard_map/prep/pallas_call | solution.py:65
  5.8 3.4 %sib_far.1.refs_0_ = bf16[8,512,128]{2,1,0:T(8,128)(2,1)S(1)} custom-call(s32[32,128]{1,0:T(8,128)S(1)} %get-tuple-element.27.bound_ref, f32[32,8,1024]{2,1,0:T(8,128)S(1)} %get-tuple-element.28.ids_ref, bf16[32,1024,128]{2,1,0:T(8,128)(2,1)S(1)} %get-tuple-element.29.x_ref), custom_call_target="tpu_custom_call" | custom-call | flops 9200000000 | bytes 28800000 | tf_op jit(solution)/shard_map/sib_far/pallas_call | solution.py:180
  9.2 0.3 collective-permute-start.2
  9.5 10.5 %sib_next.1 = (bf16[8,512,128]{2,1,0:T(8,128)(2,1)S(1)}, bf16[8,512,128]{2,1,0:T(8,128)(2,1)S(1)}, bf16[8,512,128]{2,1,0:T(8,128)(2,1)S(1)}) custom-call(s32[32,128]{1,0:T(8,128)S(1)} %get-tuple-element.27.bound_ref, f32[32,8,1024]{2,1,0:T(8,128)S(1)} %get-tuple-element.28.ids_ref, bf16[32,1024,128]{2,1,0:T(8,128)(2,1)S(1)} %get-tuple-element.29.x_ref, ...), custom_call_target="tpu_custom_call" | custom-call | flops 27599998976 | bytes 86400000 | tf_op jit(solution)/shard_map/sib_next/pallas_call | solution.py:180
  20.0 0.2 collective-permute-start.1
  20.2 0.3 collective-permute-start.4
  20.6 0.2 collective-permute-start
  20.8 3.4 %own_far.1 = (bf16[8,256,128]{2,1,0:T(8,128)(2,1)S(1)}, bf16[8,256,128]{2,1,0:T(8,128)(2,1)S(1)}) custom-call(s32[32,128]{1,0:T(8,128)S(1)} %get-tuple-element.27.bound_ref, f32[32,8,1024]{2,1,0:T(8,128)S(1)} %get-tuple-element.28.ids_ref, bf16[32,1024,128]{2,1,0:T(8,128)(2,1)S(1)} %get-tuple-element.29.x_ref, ...), custom_call_target="tpu_custom_call" | custom-call | flops 9200000000 | bytes 28800000 | tf_op jit(solution)/shard_map/own_far/pallas_call | solution.py:180
  24.2 2.1 %collective-permute-start.3 = (bf16[8,256,128]{2,1,0:T(8,128)(2,1)S(1)}, bf16[8,256,128]{2,1,0:T(8,128)(2,1)S(1)}, u32[]{:S(2)}, u32[]{:S(2)}) collective-permute-start(bf16[8,256,128]{2,1,0:T(8,128)(2,1)S(1)} %get-tuple-element.32.refs_2_), channel_id=1, source_target_pairs={{0,32},{4,12},{8,40},{12,20},{16,48},{20,28},{24,56},{28,4},{32,64... | collective-permute-start | bytes 1572872 | tf_op jit(solution)/shard_map/ppermute | solution.py:401
  26.3 2.2 %collective-permute-start.5 = (bf16[8,256,128]{2,1,0:T(8,128)(2,1)S(1)}, bf16[8,256,128]{2,1,0:T(8,128)(2,1)S(1)}, u32[]{:S(2)}, u32[]{:S(2)}) collective-permute-start(bf16[8,256,128]{2,1,0:T(8,128)(2,1)S(1)} %get-tuple-element.34), channel_id=1, source_target_pairs={{0,96},{4,28},{8,104},{12,4},{16,112},{20,12},{24,120},{28,20},{32... | collective-permute-start | bytes 1572872 | tf_op jit(solution)/shard_map/ppermute | solution.py:401
  28.5 4.0 %free.1 = (bf16[8,256,128]{2,1,0:T(8,128)(2,1)S(1)}, bf16[8,256,128]{2,1,0:T(8,128)(2,1)S(1)}) custom-call(s32[32,128]{1,0:T(8,128)S(1)} %get-tuple-element.27.bound_ref, f32[32,8,1024]{2,1,0:T(8,128)S(1)} %get-tuple-element.28.ids_ref, bf16[32,1024,128]{2,1,0:T(8,128)(2,1)S(1)} %get-tuple-element.29.x_ref, ...), custom_call_target="tpu_custom_call" | custom-call | flops 9200000000 | bytes 28800000 | tf_op jit(solution)/shard_map/free/pallas_call | solution.py:180
  32.5 3.2 %collective-permute-start.8 = (bf16[8,256,128]{2,1,0:T(8,128)(2,1)S(1)}, bf16[8,256,128]{2,1,0:T(8,128)(2,1)S(1)}, u32[]{:S(2)}, u32[]{:S(2)}) collective-permute-start(bf16[8,256,128]{2,1,0:T(8,128)(2,1)S(1)} %get-tuple-element.37), channel_id=1, source_target_pairs={{0,96},{4,28},{8,104},{12,4},{16,112},{20,12},{24,120},{28,20},{32... | collective-permute-start | bytes 1572872 | tf_op jit(solution)/shard_map/ppermute | solution.py:401
  35.8 4.0 %bound.1 = (bf16[8,256,128]{2,1,0:T(8,128)(2,1)S(1)}, bf16[8,256,128]{2,1,0:T(8,128)(2,1)S(1)}) custom-call(s32[32,128]{1,0:T(8,128)S(1)} %get-tuple-element.27.bound_ref, f32[32,8,1024]{2,1,0:T(8,128)S(1)} %get-tuple-element.28.ids_ref, bf16[32,1024,128]{2,1,0:T(8,128)(2,1)S(1)} %get-tuple-element.29.x_ref, ...), custom_call_target="tpu_custom_call" | custom-call | flops 9200000000 | bytes 28800000 | tf_op jit(solution)/shard_map/bound/pallas_call | solution.py:180
  39.8 2.0 %collective-permute-start.6 = (bf16[8,256,128]{2,1,0:T(8,128)(2,1)S(1)}, bf16[8,256,128]{2,1,0:T(8,128)(2,1)S(1)}, u32[]{:S(2)}, u32[]{:S(2)}) collective-permute-start(bf16[8,256,128]{2,1,0:T(8,128)(2,1)S(1)} %get-tuple-element.36.refs_1_), channel_id=1, source_target_pairs={{0,32},{4,12},{8,40},{12,20},{16,48},{20,28},{24,56},{28,4},{32,64... | collective-permute-start | bytes 1572872 | tf_op jit(solution)/shard_map/ppermute | solution.py:401
  41.8 1.3 %collective-permute-start.9 = (bf16[8,256,128]{2,1,0:T(8,128)(2,1)S(1)}, bf16[8,256,128]{2,1,0:T(8,128)(2,1)S(1)}, u32[]{:S(2)}, u32[]{:S(2)}) collective-permute-start(bf16[8,256,128]{2,1,0:T(8,128)(2,1)S(1)} %get-tuple-element.38), channel_id=1, source_target_pairs={{0,96},{4,28},{8,104},{12,4},{16,112},{20,12},{24,120},{28,20},{32... | collective-permute-start | bytes 1572872 | tf_op jit(solution)/shard_map/ppermute | solution.py:401
  43.1 3.6 %own_here.1.here_ref = f32[8,512,128]{2,1,0:T(8,128)S(1)} custom-call(s32[32,128]{1,0:T(8,128)S(1)} %get-tuple-element.27.bound_ref, f32[32,8,1024]{2,1,0:T(8,128)S(1)} %get-tuple-element.28.ids_ref, bf16[32,1024,128]{2,1,0:T(8,128)(2,1)S(1)} %get-tuple-element.29.x_ref, bf16[8,512,128]{2,1,0:T(8,128)(2,1)S(1)} %collective-permute-done.refs_0_, ...), custom_call_target="tpu_custom_call" | custom-call | flops 9200000000 | bytes 28800000 | tf_op jit(solution)/shard_map/own_here/pallas_call | solution.py:180
  46.8 3.5 %collective-permute-done.6.next_low = bf16[8,256,128]{2,1,0:T(8,128)(2,1)S(1)} collective-permute-done((bf16[8,256,128]{2,1,0:T(8,128)(2,1)S(1)}, bf16[8,256,128]{2,1,0:T(8,128)(2,1)S(1)}, u32[]{:S(2)}, u32[]{:S(2)}) %collective-permute-start.6) | collective-permute-done | bytes 524320 | tf_op jit(solution)/shard_map/ppermute | solution.py:401
  50.3 0.7 collective-permute-done.9.back_high
  50.9 0.3 fold.1
  51.2 1.7 %collective-permute-start.10 = (bf16[2,512,128]{2,1,0:T(8,128)(2,1)S(1)}, bf16[2,512,128]{2,1,0:T(8,128)(2,1)S(1)}, u32[]{:S(2)}, u32[]{:S(2)}) collective-permute-start(bf16[2,512,128]{2,1,0:T(8,128)(2,1)S(1)} %get-tuple-element.39.after_ref), channel_id=1, source_target_pairs={{0,8},{4,36},{8,16},{12,44},{16,24},{20,52},{24,0},{28,60},{32,40}... | collective-permute-start | bytes 786440 | tf_op jit(solution)/shard_map/ppermute | solution.py:401
  52.9 2.9 %collective-permute-start.11 = (bf16[2,512,128]{2,1,0:T(8,128)(2,1)S(1)}, bf16[2,512,128]{2,1,0:T(8,128)(2,1)S(1)}, u32[]{:S(2)}, u32[]{:S(2)}) collective-permute-start(bf16[2,512,128]{2,1,0:T(8,128)(2,1)S(1)} %get-tuple-element.42), channel_id=1, source_target_pairs={{0,16},{4,68},{8,24},{12,76},{16,0},{20,84},{24,8},{28,92},{32,48}... | collective-permute-start | bytes 786440 | tf_op jit(solution)/shard_map/ppermute | solution.py:401
  55.8 1.4 %collective-permute-start.12 = (bf16[2,512,128]{2,1,0:T(8,128)(2,1)S(1)}, bf16[2,512,128]{2,1,0:T(8,128)(2,1)S(1)}, u32[]{:S(2)}, u32[]{:S(2)}) collective-permute-start(bf16[2,512,128]{2,1,0:T(8,128)(2,1)S(1)} %get-tuple-element.43), channel_id=1, source_target_pairs={{0,24},{4,100},{8,0},{12,108},{16,8},{20,116},{24,16},{28,124},{32... | collective-permute-start | bytes 786440 | tf_op jit(solution)/shard_map/ppermute | solution.py:401
  57.2 4.1 %old_values.1 = (f32[1024,128]{1,0:T(8,128)S(1)}, f32[1,1024]{1,0:T(1,128)S(1)}, f32[8192,128]{1,0:T(8,128)S(1)}) custom-call(s32[1,1024]{1,0:T(1,128)S(1)} %copy-done.3, f32[8192,128]{1,0:T(8,128)S(1)} %bitcast.3, f32[1,8192]{1,0:T(1,128)S(1)} %copy-done.2, bf16[2,512,128]{2,1,0:T(8,128)(2,1)S(1)} %get-tuple-element.39.after_ref), custom_call_target="tpu_custom_call" | custom-call | flops 9200000000 | bytes 28800000 | tf_op jit(solution)/shard_map/old_values/pallas_call | solution.py:215
  61.3 1.6 %collective-permute-done.11.c_ref = bf16[2,512,128]{2,1,0:T(8,128)(2,1)S(1)} collective-permute-done((bf16[2,512,128]{2,1,0:T(8,128)(2,1)S(1)}, bf16[2,512,128]{2,1,0:T(8,128)(2,1)S(1)}, u32[]{:S(2)}, u32[]{:S(2)}) %collective-permute-start.11) | collective-permute-done | bytes 262176 | tf_op jit(solution)/shard_map/ppermute | solution.py:401
  63.2 1.5 %collective-permute-done.13.got_ref = f32[512,128]{1,0:T(8,128)S(1)} collective-permute-done((f32[512,128]{1,0:T(8,128)S(1)}, f32[512,128]{1,0:T(8,128)S(1)}, u32[]{:S(2)}, u32[]{:S(2)}) %collective-permute-start.13) | collective-permute-done | bytes 262176 | tf_op jit(solution)/shard_map/ppermute | solution.py:397
  64.7 0.2 square.1
  65.0 1.6 %collective-permute-start.14 = (f32[1,1024]{1,0:T(1,128)S(1)}, f32[1,1024]{1,0:T(1,128)S(1)}, u32[]{:S(2)}, u32[]{:S(2)}) collective-permute-start(f32[1,1024]{1,0:T(1,128)S(1)} %get-tuple-element.48), channel_id=1, source_target_pairs={{0,1},{1,0},{2,3},{3,2},{4,5},{5,4},{6,7},{7,6},{8,9},{9,8},{10,11... | collective-permute-start | bytes 12296 | tf_op jit(solution)/shard_map/ppermute | solution.py:427
  66.5 2.1 %collective-permute-done.14 = f32[1,1024]{1,0:T(1,128)S(1)} collective-permute-done((f32[1,1024]{1,0:T(1,128)S(1)}, f32[1,1024]{1,0:T(1,128)S(1)}, u32[]{:S(2)}, u32[]{:S(2)}) %collective-permute-start.14) | collective-permute-done | bytes 4128 | tf_op jit(solution)/shard_map/ppermute | solution.py:427
  68.6 2.8 %collective-permute-start.15 = (f32[1,1024]{1,0:T(1,128)S(1)}, f32[1,1024]{1,0:T(1,128)S(1)}, u32[]{:S(2)}, u32[]{:S(2)}) collective-permute-start(f32[1,1024]{1,0:T(1,128)S(1)} %add.3.s0_ref), channel_id=1, source_target_pairs={{0,3},{1,2},{2,1},{3,0},{4,7},{5,6},{6,5},{7,4},{8,11},{9,10},{10,... | collective-permute-start | bytes 12296 | tf_op jit(solution)/shard_map/ppermute | solution.py:427
  72.1 1.4 %collective-permute-done.15.s1_ref = f32[1,1024]{1,0:T(1,128)S(1)} collective-permute-done((f32[1,1024]{1,0:T(1,128)S(1)}, f32[1,1024]{1,0:T(1,128)S(1)}, u32[]{:S(2)}, u32[]{:S(2)}) %collective-permute-start.15) | collective-permute-done | bytes 4128 | tf_op jit(solution)/shard_map/ppermute | solution.py:427
  73.5 4.7 %apply_rows.1 = (f32[8192,128]{1,0:T(8,128)}, f32[1,8192]{1,0:T(1,128)}) custom-call(s32[1,1024]{1,0:T(1,128)S(1)} %copy-done.3, s32[1]{0:T(128)S(6)} %copy.8.live_hbm, f32[8192,128]{1,0:T(8,128)S(1)} %get-tuple-element.40.emb_in, f32[1024,128]{1,0:T(8,128)S(1)} %get-tuple-element.47.grad_ref, f32[1024,128]{1,0:T(8,128)S(1)} %get-tuple-element.44.after_ref.old_ref, ...), custom_call_target="tpu_custom_call" | custom-call | flops 13799999488 | bytes 43200000 | tf_op jit(solution)/shard_map/apply_rows/pallas_call | solution.py:360
  (21 shorter events, 0.4 us)
Async XLA Ops:
  0.6 1.0 %copy-start.1 = (s32[1024,32,4]{0,2,1:T(4,128)S(1)}, s32[1024,32,4]{0,2,1:T(4,128)}, u32[]{:S(2)}) copy-start(s32[1024,32,4]{0,2,1:T(4,128)} %param.7) | copy-start | bytes 1572868
  9.2 11.6 %collective-permute-start.2 = (bf16[8,512,128]{2,1,0:T(8,128)(2,1)S(1)}, bf16[8,512,128]{2,1,0:T(8,128)(2,1)S(1)}, u32[]{:S(2)}, u32[]{:S(2)}) collective-permute-start(bf16[8,512,128]{2,1,0:T(8,128)(2,1)S(1)} %sib_far.1.refs_0_), channel_id=1, source_target_pairs={{0,4},{4,0},{1,5},{5,1},{2,6},{6,2},{3,7},{7,3},{8,12},{12,8},{9,1... | collective-permute-start | bytes 3145736 | tf_op jit(solution)/shard_map/ppermute | solution.py:397
  20.0 8.5 %collective-permute-start.1 = (bf16[8,512,128]{2,1,0:T(8,128)(2,1)S(1)}, bf16[8,512,128]{2,1,0:T(8,128)(2,1)S(1)}, u32[]{:S(2)}, u32[]{:S(2)}) collective-permute-start(bf16[8,512,128]{2,1,0:T(8,128)(2,1)S(1)} %get-tuple-element.31.refs_1_), channel_id=1, source_target_pairs={{0,4},{4,0},{1,5},{5,1},{2,6},{6,2},{3,7},{7,3},{8,12},{12,8},{9,1... | collective-permute-start | bytes 3145736 | tf_op jit(solution)/shard_map/ppermute | solution.py:397
  20.2 8.2 %collective-permute-start.4 = (bf16[8,512,128]{2,1,0:T(8,128)(2,1)S(1)}, bf16[8,512,128]{2,1,0:T(8,128)(2,1)S(1)}, u32[]{:S(2)}, u32[]{:S(2)}) collective-permute-start(bf16[8,512,128]{2,1,0:T(8,128)(2,1)S(1)} %get-tuple-element.33), channel_id=1, source_target_pairs={{0,4},{4,0},{1,5},{5,1},{2,6},{6,2},{3,7},{7,3},{8,12},{12,8},{9,1... | collective-permute-start | bytes 3145736 | tf_op jit(solution)/shard_map/ppermute | solution.py:397
  20.6 22.5 %collective-permute-start = (bf16[8,512,128]{2,1,0:T(8,128)(2,1)S(1)}, bf16[8,512,128]{2,1,0:T(8,128)(2,1)S(1)}, u32[]{:S(2)}, u32[]{:S(2)}) collective-permute-start(bf16[8,512,128]{2,1,0:T(8,128)(2,1)S(1)} %get-tuple-element.30), channel_id=1, source_target_pairs={{0,4},{4,0},{1,5},{5,1},{2,6},{6,2},{3,7},{7,3},{8,12},{12,8},{9,1... | collective-permute-start | bytes 3145736 | tf_op jit(solution)/shard_map/ppermute | solution.py:397
  24.2 11.6 %collective-permute-start.3 = (bf16[8,256,128]{2,1,0:T(8,128)(2,1)S(1)}, bf16[8,256,128]{2,1,0:T(8,128)(2,1)S(1)}, u32[]{:S(2)}, u32[]{:S(2)}) collective-permute-start(bf16[8,256,128]{2,1,0:T(8,128)(2,1)S(1)} %get-tuple-element.32.refs_2_), channel_id=1, source_target_pairs={{0,32},{4,12},{8,40},{12,20},{16,48},{20,28},{24,56},{28,4},{32,64... | collective-permute-start | bytes 1572872 | tf_op jit(solution)/shard_map/ppermute | solution.py:401
  26.3 9.5 %collective-permute-start.5 = (bf16[8,256,128]{2,1,0:T(8,128)(2,1)S(1)}, bf16[8,256,128]{2,1,0:T(8,128)(2,1)S(1)}, u32[]{:S(2)}, u32[]{:S(2)}) collective-permute-start(bf16[8,256,128]{2,1,0:T(8,128)(2,1)S(1)} %get-tuple-element.34), channel_id=1, source_target_pairs={{0,96},{4,28},{8,104},{12,4},{16,112},{20,12},{24,120},{28,20},{32... | collective-permute-start | bytes 1572872 | tf_op jit(solution)/shard_map/ppermute | solution.py:401
  32.5 14.3 %collective-permute-start.7 = (bf16[8,256,128]{2,1,0:T(8,128)(2,1)S(1)}, bf16[8,256,128]{2,1,0:T(8,128)(2,1)S(1)}, u32[]{:S(2)}, u32[]{:S(2)}) collective-permute-start(bf16[8,256,128]{2,1,0:T(8,128)(2,1)S(1)} %get-tuple-element.35.refs_4_), channel_id=1, source_target_pairs={{0,32},{4,12},{8,40},{12,20},{16,48},{20,28},{24,56},{28,4},{32,64... | collective-permute-start | bytes 1572872 | tf_op jit(solution)/shard_map/ppermute | solution.py:401
  32.5 14.2 %collective-permute-start.8 = (bf16[8,256,128]{2,1,0:T(8,128)(2,1)S(1)}, bf16[8,256,128]{2,1,0:T(8,128)(2,1)S(1)}, u32[]{:S(2)}, u32[]{:S(2)}) collective-permute-start(bf16[8,256,128]{2,1,0:T(8,128)(2,1)S(1)} %get-tuple-element.37), channel_id=1, source_target_pairs={{0,96},{4,28},{8,104},{12,4},{16,112},{20,12},{24,120},{28,20},{32... | collective-permute-start | bytes 1572872 | tf_op jit(solution)/shard_map/ppermute | solution.py:401
  39.8 10.5 %collective-permute-start.6 = (bf16[8,256,128]{2,1,0:T(8,128)(2,1)S(1)}, bf16[8,256,128]{2,1,0:T(8,128)(2,1)S(1)}, u32[]{:S(2)}, u32[]{:S(2)}) collective-permute-start(bf16[8,256,128]{2,1,0:T(8,128)(2,1)S(1)} %get-tuple-element.36.refs_1_), channel_id=1, source_target_pairs={{0,32},{4,12},{8,40},{12,20},{16,48},{20,28},{24,56},{28,4},{32,64... | collective-permute-start | bytes 1572872 | tf_op jit(solution)/shard_map/ppermute | solution.py:401
  41.8 9.2 %collective-permute-start.9 = (bf16[8,256,128]{2,1,0:T(8,128)(2,1)S(1)}, bf16[8,256,128]{2,1,0:T(8,128)(2,1)S(1)}, u32[]{:S(2)}, u32[]{:S(2)}) collective-permute-start(bf16[8,256,128]{2,1,0:T(8,128)(2,1)S(1)} %get-tuple-element.38), channel_id=1, source_target_pairs={{0,96},{4,28},{8,104},{12,4},{16,112},{20,12},{24,120},{28,20},{32... | collective-permute-start | bytes 1572872 | tf_op jit(solution)/shard_map/ppermute | solution.py:401
  43.1 14.1 %copy-start.2 = (f32[1,8192]{1,0:T(1,128)S(1)}, f32[1,8192]{1,0:T(1,128)}, u32[]{:S(2)}) copy-start(f32[1,8192]{1,0:T(1,128)} %acc_in.1) | copy-start | bytes 98308
  46.7 10.5 %copy-start = (f32[1,8192,128]{2,1,0:T(8,128)S(1)}, f32[1,8192,128]{2,1,0:T(8,128)}, u32[]{:S(2)}) copy-start(f32[1,8192,128]{2,1,0:T(8,128)} %param.10) | copy-start | bytes 12582916
  46.7 10.5 %copy-start.3 = (s32[1,1024]{1,0:T(1,128)S(1)}, s32[1,1024]{1,0:T(1,128)}, u32[]{:S(2)}) copy-start(s32[1,1024]{1,0:T(1,128)} %row_hbm.3) | copy-start | bytes 12292
  51.2 10.1 %collective-permute-start.10 = (bf16[2,512,128]{2,1,0:T(8,128)(2,1)S(1)}, bf16[2,512,128]{2,1,0:T(8,128)(2,1)S(1)}, u32[]{:S(2)}, u32[]{:S(2)}) collective-permute-start(bf16[2,512,128]{2,1,0:T(8,128)(2,1)S(1)} %get-tuple-element.39.after_ref), channel_id=1, source_target_pairs={{0,8},{4,36},{8,16},{12,44},{16,24},{20,52},{24,0},{28,60},{32,40}... | collective-permute-start | bytes 786440 | tf_op jit(solution)/shard_map/ppermute | solution.py:401
  52.9 10.0 %collective-permute-start.11 = (bf16[2,512,128]{2,1,0:T(8,128)(2,1)S(1)}, bf16[2,512,128]{2,1,0:T(8,128)(2,1)S(1)}, u32[]{:S(2)}, u32[]{:S(2)}) collective-permute-start(bf16[2,512,128]{2,1,0:T(8,128)(2,1)S(1)} %get-tuple-element.42), channel_id=1, source_target_pairs={{0,16},{4,68},{8,24},{12,76},{16,0},{20,84},{24,8},{28,92},{32,48}... | collective-permute-start | bytes 786440 | tf_op jit(solution)/shard_map/ppermute | solution.py:401
  55.8 7.2 %collective-permute-start.12 = (bf16[2,512,128]{2,1,0:T(8,128)(2,1)S(1)}, bf16[2,512,128]{2,1,0:T(8,128)(2,1)S(1)}, u32[]{:S(2)}, u32[]{:S(2)}) collective-permute-start(bf16[2,512,128]{2,1,0:T(8,128)(2,1)S(1)} %get-tuple-element.43), channel_id=1, source_target_pairs={{0,24},{4,100},{8,0},{12,108},{16,8},{20,116},{24,16},{28,124},{32... | collective-permute-start | bytes 786440 | tf_op jit(solution)/shard_map/ppermute | solution.py:401
  63.1 1.6 %collective-permute-start.13 = (f32[512,128]{1,0:T(8,128)S(1)}, f32[512,128]{1,0:T(8,128)S(1)}, u32[]{:S(2)}, u32[]{:S(2)}) collective-permute-start(f32[512,128]{1,0:T(8,128)S(1)} %get-tuple-element.46), channel_id=1, source_target_pairs={{0,4},{4,0},{1,5},{5,1},{2,6},{6,2},{3,7},{7,3},{8,12},{12,8},{9,1... | collective-permute-start | bytes 786440 | tf_op jit(solution)/shard_map/ppermute | solution.py:397
  65.0 3.7 %collective-permute-start.14 = (f32[1,1024]{1,0:T(1,128)S(1)}, f32[1,1024]{1,0:T(1,128)S(1)}, u32[]{:S(2)}, u32[]{:S(2)}) collective-permute-start(f32[1,1024]{1,0:T(1,128)S(1)} %get-tuple-element.48), channel_id=1, source_target_pairs={{0,1},{1,0},{2,3},{3,2},{4,5},{5,4},{6,7},{7,6},{8,9},{9,8},{10,11... | collective-permute-start | bytes 12296 | tf_op jit(solution)/shard_map/ppermute | solution.py:427
  68.6 4.8 %collective-permute-start.15 = (f32[1,1024]{1,0:T(1,128)S(1)}, f32[1,1024]{1,0:T(1,128)S(1)}, u32[]{:S(2)}, u32[]{:S(2)}) collective-permute-start(f32[1,1024]{1,0:T(1,128)S(1)} %add.3.s0_ref), channel_id=1, source_target_pairs={{0,3},{1,2},{2,1},{3,0},{4,7},{5,6},{6,5},{7,4},{8,11},{9,10},{10,... | collective-permute-start | bytes 12296 | tf_op jit(solution)/shard_map/ppermute | solution.py:427

commit v4 on v3

--- a/solution.py
+++ b/solution.py
@@ -11,6 +11,8 @@
 learn_rate = 0.5
 epsilon = 1e-08
 MIB = 2**20
+GATHER = 20
+LAST = 1
 SCALE = 2.0
 BF = jnp.bfloat16
 F32 = jnp.float32
@@ -184,7 +186,7 @@
         out_shape=shapes,
         scratch_shapes=[pltpu.SMEM((8,), jnp.int32)],
         compiler_params=pltpu.CompilerParams(vmem_limit_bytes=12 * MIB),
-        cost_estimate=cost(2 * work),
+        cost_estimate=cost(2 * work if name != "own_here" else LAST),
         name=name,
     )(bound, ids, xt, *operands, *after)
 
@@ -219,7 +221,7 @@
         out_shape=[
             jax.ShapeDtypeStruct((rows.shape[1], embedding.shape[1]), F32),
             jax.ShapeDtypeStruct(rows.shape, F32),
-            jax.ShapeDtypeStruct(embedding.shape, F32),
+            pltpu.VMEM(embedding.shape, F32),
         ],
         scratch_shapes=[
             pltpu.SMEM(rows.shape, jnp.int32),
@@ -232,30 +234,45 @@
     )(rows, embedding, accumulator, after)
 
 
-def fold_body(here_ref, next_low, next_high, back_low, back_high, *out_refs):
+def gather_body(here_ref, next_low, next_high, back_low, back_high, out_ref):
+    tile = next_low.shape[1]
+    for part, (next_ref, back_ref) in enumerate(((next_low, back_low), (next_high, back_high))):
+        here = pl.ds(part * tile, tile)
+        out_ref[:, here, :] = here_ref[:, here, :] + (next_ref[...].astype(F32) + back_ref[...].astype(F32))
+
+
+def gather(here, *pieces):
+    return pl.pallas_call(
+        gather_body,
+        in_specs=[VMEM] * 5,
+        out_specs=VMEM,
+        out_shape=jax.ShapeDtypeStruct(here.shape, F32),
+        compiler_params=pltpu.CompilerParams(vmem_limit_bytes=12 * MIB),
+        cost_estimate=cost(GATHER),
+        name="gather",
+    )(here, *pieces)
+
+
+def fold_body(here_ref, got_ref, *out_refs):
     place = ring_pos(lax.axis_index("core"))[1]
-    tile = next_low.shape[1]
     for d, out_ref in enumerate(out_refs):
         j = lax.rem(place + d, 4)
         for c in range(2):
             m = 2 * j + c
-            for part, (next_ref, back_ref) in enumerate(((next_low, back_low), (next_high, back_high))):
-                here = pl.ds(part * tile, tile)
-                value = here_ref[m, here, :] + (next_ref[m].astype(F32) + back_ref[m].astype(F32))
-                out_ref[c, here, :] = value.astype(out_ref.dtype)
-
-
-def fold(here, *pieces):
+            out_ref[c] = (here_ref[m] + got_ref[m].astype(F32)).astype(out_ref.dtype)
+
+
+def fold(here, got):
     shape = (2,) + here.shape[1:]
     return pl.pallas_call(
         fold_body,
-        in_specs=[VMEM] * 5,
+        in_specs=[VMEM] * 2,
         out_specs=[VMEM] * 4,
         out_shape=[jax.ShapeDtypeStruct(shape, k) for k in (F32, BF, BF, BF)],
         compiler_params=pltpu.CompilerParams(vmem_limit_bytes=12 * MIB),
         cost_estimate=cost(0.4),
         name="fold",
-    )(here, *pieces)
+    )(here, got)
 
 
 def total_body(a_ref, b_ref, c_ref, d_ref, after_ref, mine_ref, other_ref):
@@ -322,51 +339,58 @@
     new_acc_ref[...] = new_acc
     loads.append(pltpu.make_async_copy(new_acc_ref, new_acc_smem, sems.at[3]))
     loads[-1].start()
-    emb_ref[...] = emb_in[...]
     scale = learn_rate / (jnp.sqrt(new_acc) + epsilon)
     scale = jnp.broadcast_to(scale, (columns, slots)).T
     new_ref[...] = old_ref[...] - grad_ref[...] * scale
-    for load in loads:
-        load.wait()
+    row_load, live_load, acc_load, new_load = loads
+    row_load.wait()
+    live_load.wait()
     live = live_ref[0]
-
-    def put(u):
-        row = row_ref[0, u]
-        emb_ref[pl.ds(row, 1), :] = new_ref[pl.ds(u, 1), :]
-        acc_ref[0, row] = new_acc_smem[0, u]
-
-    def step(i, carry):
-        for j in range(8):
-            put(i * 8 + j)
-        return carry
-
-    def last(u, carry):
-        put(u)
-        return carry
-
-    lax.fori_loop(0, live // 8, step, 0)
-    lax.fori_loop(live // 8 * 8, live, last, 0)
-    stores = [
-        pltpu.make_async_copy(emb_ref, emb_out, sems.at[0]),
-        pltpu.make_async_copy(acc_ref, acc_out, sems.at[1]),
-    ]
-    for store in stores:
-        store.start()
-    for store in stores:
-        store.wait()
+    block = 16
+
+    def scatter(put):
+        def step(i, carry):
+            for j in range(block):
+                put(i * block + j)
+            return carry
+
+        def last(u, carry):
+            put(u)
+            return carry
+
+        lax.fori_loop(0, live // block, step, 0)
+        lax.fori_loop(live // block * block, live, last, 0)
+
+    def put_row(u):
+        emb_ref[pl.ds(row_ref[0, u], 1), :] = new_ref[pl.ds(u, 1), :]
+
+    def put_acc(u):
+        acc_ref[0, row_ref[0, u]] = new_acc_smem[0, u]
+
+    scatter(put_row)
+    emb_store = pltpu.make_async_copy(emb_ref, emb_out, sems.at[0])
+    emb_store.start()
+    acc_load.wait()
+    new_load.wait()
+    scatter(put_acc)
+    acc_store = pltpu.make_async_copy(acc_ref, acc_out, sems.at[1])
+    acc_store.start()
+    acc_store.wait()
+    emb_store.wait()
 
 
 def apply_rows(width, rows, live, embedding, gradient, old, squares, old_acc, accumulator):
     return pl.pallas_call(
         functools.partial(apply_body, width),
         in_specs=[ANY, ANY] + [VMEM] * 6 + [ANY],
-        out_specs=[ANY, ANY],
+        out_specs=[ANY, ANY, VMEM],
         out_shape=[
             jax.ShapeDtypeStruct(embedding.shape, F32),
             jax.ShapeDtypeStruct(accumulator.shape, F32),
-        ],
+            pltpu.VMEM(embedding.shape, F32),
+        ],
+        input_output_aliases={2: 2},
         scratch_shapes=[
-            pltpu.VMEM(embedding.shape, F32),
             pltpu.VMEM(old.shape, F32),
             pltpu.VMEM(rows.shape, F32),
             pltpu.SMEM(rows.shape, F32),
@@ -378,7 +402,7 @@
         compiler_params=pltpu.CompilerParams(vmem_limit_bytes=16 * MIB),
         cost_estimate=cost(6),
         name="apply_rows",
-    )(rows, live, embedding, gradient, old, *squares, old_acc, accumulator)
+    )(rows, live, pltpu.with_memory_space_constraint(embedding, pltpu.VMEM), gradient, old, *squares, old_acc, accumulator)
 
 
 def per_device(pooled_grad, segment_map, unique_rows, live_counts, embedding, accumulator):
@@ -387,6 +411,7 @@
     cols = lax.axis_size("col")
     half = slots // 2
     seg = jnp.transpose(segment_map, (1, 2, 0))
+    seg = pltpu.with_memory_space_constraint(seg, pltpu.HBM)
     xt, ids, bound = prep(pooled_grad, seg)
 
     chips = [(z, y) for z in range(4) for y in range(4)]
@@ -406,7 +431,7 @@
     own = lambda step, parts, add, extra=None, split=True, kind=BF: (True, step, parts, (add, extra), split, kind)
     (sib_far,) = run("sib_far", sib(2))
     got_far = swap(sib_far)
-    sib_next, sib_back, sib_here = run("sib_next", sib(1), sib(3), sib(0), after=(sib_far,))
+    sib_next, sib_back = run("sib_next", sib(1), sib(3), after=(sib_far,))
     got_next, got_back = swap(sib_next), swap(sib_back)
     far_low, far_high = run("own_far", own(2, both, got_far), after=(sib_next,))
     low_got, high_got = shift(far_low, True, 1), shift(far_high, True, -1)
@@ -416,9 +441,11 @@
         "bound", own(1, (0,), got_next, low_got), own(3, (1,), got_back, high_got), after=(next_high,)
     )
     next_low_got, back_high_got = shift(next_low, True, 1), shift(back_high, True, -1)
+    (sib_here,) = run("sib_here", sib(0), after=(next_low,))
     got_here = swap(sib_here)
-    (here,) = run("own_here", own(0, both, got_here, None, False, F32), after=(next_low,))
-    parts = list(fold(here, next_low_got, next_high_got, back_low_got, back_high_got))
+    (here,) = run("own_here", own(0, both, None, None, False, F32), after=(sib_here,))
+    gathered = gather(here, next_low_got, next_high_got, back_low_got, back_high_got)
+    parts = list(fold(gathered, got_here))
     old, old_acc, table = old_values(unique_rows, embedding[0], accumulator, parts[1])
     for d in (3, 1, 2):
         parts[d] = shift(parts[d], False, d)
@@ -427,7 +454,7 @@
     across = lambda a, k: lax.ppermute(a, "col", [(i, i ^ k) for i in range(cols)])
     pair = squares + across(squares, 1)
     squares = (pair, across(pair, 3))
-    new_embedding, new_accumulator = apply_rows(
+    new_embedding, new_accumulator, _ = apply_rows(
         columns * cols, unique_rows, live_counts, table, gradient, old, squares, old_acc, accumulator
     )
     return (new_embedding[None], new_accumulator)

time: 79 us -> 75.7 us (0.958); the launches traced: 78.3 us -> 75.9 us
  waiting for transfers between devices: 10.9 us -> 7.56 us
  Pallas kernels: 42.5 us -> 44 us
  local copies, waits for them, and re-layouts: 1.05 us -> 0.02 us
    ppermute x9, waiting for transfers between devices: 5.83 us -> 2.5 us  [shift(): lax.ppermute(a, owner, [(index(z, y, c), index(*move(z, y, c))) for z, y...]
    unnamed x8 -> x6, local copies, waits for them, and re-layouts: 1.05 us -> 0.02 us
    pallas_call x6 -> x7, Pallas kernels: 29 us -> 29.5 us  [sums(): pl.pallas_call(functools.partial(sums_body, tuple(kinds), len(after)), in...]
  transfers between devices with their start and end apart: 16 -> 16, of which waited for: 6 -> 5; matrix products, arithmetic and copies ran while one was open for 0% -> 0% of each run, Pallas kernels for 38% -> 40%
where the time goes in v4:
time: 75.7 us; the launch traced here: 75.9 us
  Pallas kernels  44 us (58%)
  starting transfers between devices  22.7 us (30%)
  waiting for transfers between devices  7.56 us (10%)
  between operations  1.65 us (2%)
    pallas_call x7, Pallas kernels, sums(): pl.pallas_call(functools.partial(sums_body, tuple(kinds), len(after)), in...  29.5 us
    ppermute x9, starting transfers between devices, shift(): lax.ppermute(a, owner, [(index(z, y, c), index(*move(z, y, c))) for z, y...  17 us
    pallas_call x1, Pallas kernels, prep(): pl.pallas_call(prep_body, in_specs=[pl.BlockSpec(memory_space=pltpu.HBM)]...  4.72 us
    pallas_call x1, Pallas kernels, apply_rows(): pl.pallas_call(functools.partial(apply_body, width), in_specs=[ANY, ANY]...  4.67 us
    ppermute x2, starting transfers between devices, per_device(): lax.ppermute(a, 'col', [(i, i ^ k) for i in range(cols)])  4.33 us
    pallas_call x1, Pallas kernels, old_values(): pl.pallas_call(old_body, in_specs=[ANY] * 4, out_specs=[VMEM, SMEM, VMEM]...  4.1 us
    ppermute x2, waiting for transfers between devices, per_device(): lax.ppermute(a, 'col', [(i, i ^ k) for i in range(cols)])  3.52 us
    ppermute x9, waiting for transfers between devices, shift(): lax.ppermute(a, owner, [(index(z, y, c), index(*move(z, y, c))) for z, y...  2.5 us
  transfers between devices with their start and end apart: 16, of which 5 were waited for; matrix products, arithmetic and copies ran while one was open for 0% of the time, Pallas kernels for 40%

profile of v4, /device:TPU:0, one launch (start us, length us, event | category | flops | bytes accessed | tf_op | source)
XLA Modules:
  0.0 75.9 jit_solution(8236602963983005196)
XLA Ops:
  0.6 4.7 %prep.1 = (bf16[32,1024,128]{2,1,0:T(8,128)(2,1)S(1)}, f32[32,8,1024]{2,1,0:T(8,128)S(1)}, s32[32,128]{1,0:T(8,128)S(1)}) custom-call(bf16[1024,32,128]{2,1,0:T(8,128)(2,1)} %x_hbm.1, s32[32,4,1024]{2,1,0:T(4,128)} %bitcast.4), custom_call_target="tpu_custom_call" | custom-call | flops 9200000000 | bytes 28800000 | tf_op jit(solution)/shard_map/prep/pallas_call | solution.py:67
  5.4 3.2 %sib_far.1.refs_0_ = bf16[8,512,128]{2,1,0:T(8,128)(2,1)S(1)} custom-call(s32[32,128]{1,0:T(8,128)S(1)} %get-tuple-element.26.bound_ref, f32[32,8,1024]{2,1,0:T(8,128)S(1)} %get-tuple-element.27.ids_ref, bf16[32,1024,128]{2,1,0:T(8,128)(2,1)S(1)} %get-tuple-element.28.x_ref), custom_call_target="tpu_custom_call" | custom-call | flops 9200000000 | bytes 28800000 | tf_op jit(solution)/shard_map/sib_far/pallas_call | solution.py:182
  8.6 0.3 collective-permute-start.1
  8.9 7.0 %sib_next.1 = (bf16[8,512,128]{2,1,0:T(8,128)(2,1)S(1)}, bf16[8,512,128]{2,1,0:T(8,128)(2,1)S(1)}) custom-call(s32[32,128]{1,0:T(8,128)S(1)} %get-tuple-element.26.bound_ref, f32[32,8,1024]{2,1,0:T(8,128)S(1)} %get-tuple-element.27.ids_ref, bf16[32,1024,128]{2,1,0:T(8,128)(2,1)S(1)} %get-tuple-element.28.x_ref, bf16[8,512,128]{2,1,0:T(8,128)(2,1)S(1)} %sib_far.1.refs_0_), custom_call_target="tpu_custom_call" | custom-call | flops 18400000000 | bytes 57600000 | tf_op jit(solution)/shard_map/sib_next/pallas_call | solution.py:182
  15.8 0.8 %collective-permute-start = (bf16[8,512,128]{2,1,0:T(8,128)(2,1)S(1)}, bf16[8,512,128]{2,1,0:T(8,128)(2,1)S(1)}, u32[]{:S(2)}, u32[]{:S(2)}) collective-permute-start(bf16[8,512,128]{2,1,0:T(8,128)(2,1)S(1)} %get-tuple-element.29.refs_1_), channel_id=1, source_target_pairs={{0,4},{4,0},{1,5},{5,1},{2,6},{6,2},{3,7},{7,3},{8,12},{12,8},{9,1... | collective-permute-start | bytes 3145736 | tf_op jit(solution)/shard_map/ppermute | solution.py:422
  16.8 3.4 %own_far.1 = (bf16[8,256,128]{2,1,0:T(8,128)(2,1)S(1)}, bf16[8,256,128]{2,1,0:T(8,128)(2,1)S(1)}) custom-call(s32[32,128]{1,0:T(8,128)S(1)} %get-tuple-element.26.bound_ref, f32[32,8,1024]{2,1,0:T(8,128)S(1)} %get-tuple-element.27.ids_ref, bf16[32,1024,128]{2,1,0:T(8,128)(2,1)S(1)} %get-tuple-element.28.x_ref, ...), custom_call_target="tpu_custom_call" | custom-call | flops 9200000000 | bytes 28800000 | tf_op jit(solution)/shard_map/own_far/pallas_call | solution.py:182
  20.2 2.4 %collective-permute-start.2 = (bf16[8,256,128]{2,1,0:T(8,128)(2,1)S(1)}, bf16[8,256,128]{2,1,0:T(8,128)(2,1)S(1)}, u32[]{:S(2)}, u32[]{:S(2)}) collective-permute-start(bf16[8,256,128]{2,1,0:T(8,128)(2,1)S(1)} %get-tuple-element.30.refs_2_), channel_id=1, source_target_pairs={{0,32},{4,12},{8,40},{12,20},{16,48},{20,28},{24,56},{28,4},{32,64... | collective-permute-start | bytes 1572872 | tf_op jit(solution)/shard_map/ppermute | solution.py:426
  22.7 2.0 %collective-permute-start.4 = (bf16[8,256,128]{2,1,0:T(8,128)(2,1)S(1)}, bf16[8,256,128]{2,1,0:T(8,128)(2,1)S(1)}, u32[]{:S(2)}, u32[]{:S(2)}) collective-permute-start(bf16[8,256,128]{2,1,0:T(8,128)(2,1)S(1)} %get-tuple-element.32), channel_id=1, source_target_pairs={{0,96},{4,28},{8,104},{12,4},{16,112},{20,12},{24,120},{28,20},{32... | collective-permute-start | bytes 1572872 | tf_op jit(solution)/shard_map/ppermute | solution.py:426
  24.7 4.2 %free.1 = (bf16[8,256,128]{2,1,0:T(8,128)(2,1)S(1)}, bf16[8,256,128]{2,1,0:T(8,128)(2,1)S(1)}) custom-call(s32[32,128]{1,0:T(8,128)S(1)} %get-tuple-element.26.bound_ref, f32[32,8,1024]{2,1,0:T(8,128)S(1)} %get-tuple-element.27.ids_ref, bf16[32,1024,128]{2,1,0:T(8,128)(2,1)S(1)} %get-tuple-element.28.x_ref, ...), custom_call_target="tpu_custom_call" | custom-call | flops 9200000000 | bytes 28800000 | tf_op jit(solution)/shard_map/free/pallas_call | solution.py:182
  28.9 0.1 collective-permute-start.6
  29.0 3.2 %collective-permute-start.7 = (bf16[8,256,128]{2,1,0:T(8,128)(2,1)S(1)}, bf16[8,256,128]{2,1,0:T(8,128)(2,1)S(1)}, u32[]{:S(2)}, u32[]{:S(2)}) collective-permute-start(bf16[8,256,128]{2,1,0:T(8,128)(2,1)S(1)} %get-tuple-element.35), channel_id=1, source_target_pairs={{0,96},{4,28},{8,104},{12,4},{16,112},{20,12},{24,120},{28,20},{32... | collective-permute-start | bytes 1572872 | tf_op jit(solution)/shard_map/ppermute | solution.py:426
  32.2 4.4 %bound.1 = (bf16[8,256,128]{2,1,0:T(8,128)(2,1)S(1)}, bf16[8,256,128]{2,1,0:T(8,128)(2,1)S(1)}) custom-call(s32[32,128]{1,0:T(8,128)S(1)} %get-tuple-element.26.bound_ref, f32[32,8,1024]{2,1,0:T(8,128)S(1)} %get-tuple-element.27.ids_ref, bf16[32,1024,128]{2,1,0:T(8,128)(2,1)S(1)} %get-tuple-element.28.x_ref, ...), custom_call_target="tpu_custom_call" | custom-call | flops 9200000000 | bytes 28800000 | tf_op jit(solution)/shard_map/bound/pallas_call | solution.py:182
  36.6 2.2 %collective-permute-start.5 = (bf16[8,256,128]{2,1,0:T(8,128)(2,1)S(1)}, bf16[8,256,128]{2,1,0:T(8,128)(2,1)S(1)}, u32[]{:S(2)}, u32[]{:S(2)}) collective-permute-start(bf16[8,256,128]{2,1,0:T(8,128)(2,1)S(1)} %get-tuple-element.34.refs_0_), channel_id=1, source_target_pairs={{0,32},{4,12},{8,40},{12,20},{16,48},{20,28},{24,56},{28,4},{32,64... | collective-permute-start | bytes 1572872 | tf_op jit(solution)/shard_map/ppermute | solution.py:426
  38.8 1.1 %collective-permute-start.8 = (bf16[8,256,128]{2,1,0:T(8,128)(2,1)S(1)}, bf16[8,256,128]{2,1,0:T(8,128)(2,1)S(1)}, u32[]{:S(2)}, u32[]{:S(2)}) collective-permute-start(bf16[8,256,128]{2,1,0:T(8,128)(2,1)S(1)} %get-tuple-element.36), channel_id=1, source_target_pairs={{0,96},{4,28},{8,104},{12,4},{16,112},{20,12},{24,120},{28,20},{32... | collective-permute-start | bytes 1572872 | tf_op jit(solution)/shard_map/ppermute | solution.py:426
  39.9 3.4 %sib_here.1.refs_0_ = bf16[8,512,128]{2,1,0:T(8,128)(2,1)S(1)} custom-call(s32[32,128]{1,0:T(8,128)S(1)} %get-tuple-element.26.bound_ref, f32[32,8,1024]{2,1,0:T(8,128)S(1)} %get-tuple-element.27.ids_ref, bf16[32,1024,128]{2,1,0:T(8,128)(2,1)S(1)} %get-tuple-element.28.x_ref, bf16[8,256,128]{2,1,0:T(8,128)(2,1)S(1)} %get-tuple-element.34.refs_0_), custom_call_target="tpu_custom_call" | custom-call | flops 9200000000 | bytes 28800000 | tf_op jit(solution)/shard_map/sib_here/pallas_call | solution.py:182
  43.4 3.9 %own_here.1.here_ref = f32[8,512,128]{2,1,0:T(8,128)S(1)} custom-call(s32[32,128]{1,0:T(8,128)S(1)} %get-tuple-element.26.bound_ref, f32[32,8,1024]{2,1,0:T(8,128)S(1)} %get-tuple-element.27.ids_ref, bf16[32,1024,128]{2,1,0:T(8,128)(2,1)S(1)} %get-tuple-element.28.x_ref, bf16[8,512,128]{2,1,0:T(8,128)(2,1)S(1)} %sib_here.1.refs_0_), custom_call_target="tpu_custom_call" | custom-call | flops 2300000000 | bytes 7200000 | tf_op jit(solution)/shard_map/own_here/pallas_call | solution.py:182
  47.4 0.6 collective-permute-done.8.back_high
  48.0 0.3 gather.1.here_ref
  48.4 0.3 fold.1
  48.6 1.7 %collective-permute-start.10 = (bf16[2,512,128]{2,1,0:T(8,128)(2,1)S(1)}, bf16[2,512,128]{2,1,0:T(8,128)(2,1)S(1)}, u32[]{:S(2)}, u32[]{:S(2)}) collective-permute-start(bf16[2,512,128]{2,1,0:T(8,128)(2,1)S(1)} %get-tuple-element.37.after_ref), channel_id=1, source_target_pairs={{0,8},{4,36},{8,16},{12,44},{16,24},{20,52},{24,0},{28,60},{32,40}... | collective-permute-start | bytes 786440 | tf_op jit(solution)/shard_map/ppermute | solution.py:426
  50.3 3.1 %collective-permute-start.11 = (bf16[2,512,128]{2,1,0:T(8,128)(2,1)S(1)}, bf16[2,512,128]{2,1,0:T(8,128)(2,1)S(1)}, u32[]{:S(2)}, u32[]{:S(2)}) collective-permute-start(bf16[2,512,128]{2,1,0:T(8,128)(2,1)S(1)} %get-tuple-element.40), channel_id=1, source_target_pairs={{0,16},{4,68},{8,24},{12,76},{16,0},{20,84},{24,8},{28,92},{32,48}... | collective-permute-start | bytes 786440 | tf_op jit(solution)/shard_map/ppermute | solution.py:426
  53.4 1.2 %collective-permute-start.12 = (bf16[2,512,128]{2,1,0:T(8,128)(2,1)S(1)}, bf16[2,512,128]{2,1,0:T(8,128)(2,1)S(1)}, u32[]{:S(2)}, u32[]{:S(2)}) collective-permute-start(bf16[2,512,128]{2,1,0:T(8,128)(2,1)S(1)} %get-tuple-element.41), channel_id=1, source_target_pairs={{0,24},{4,100},{8,0},{12,108},{16,8},{20,116},{24,16},{28,124},{32... | collective-permute-start | bytes 786440 | tf_op jit(solution)/shard_map/ppermute | solution.py:426
  54.6 4.1 %old_values.1 = (f32[1024,128]{1,0:T(8,128)S(1)}, f32[1,1024]{1,0:T(1,128)S(1)}, f32[8192,128]{1,0:T(8,128)S(1)}) custom-call(s32[1,1024]{1,0:T(1,128)S(1)} %copy-done.2, f32[8192,128]{1,0:T(8,128)S(1)} %bitcast.3, f32[1,8192]{1,0:T(1,128)S(1)} %copy-done.1, bf16[2,512,128]{2,1,0:T(8,128)(2,1)S(1)} %get-tuple-element.37.after_ref), custom_call_target="tpu_custom_call" | custom-call | flops 9200000000 | bytes 28800000 | tf_op jit(solution)/shard_map/old_values/pallas_call | solution.py:217
  58.7 1.8 %collective-permute-done.11.c_ref = bf16[2,512,128]{2,1,0:T(8,128)(2,1)S(1)} collective-permute-done((bf16[2,512,128]{2,1,0:T(8,128)(2,1)S(1)}, bf16[2,512,128]{2,1,0:T(8,128)(2,1)S(1)}, u32[]{:S(2)}, u32[]{:S(2)}) %collective-permute-start.11) | collective-permute-done | bytes 262176 | tf_op jit(solution)/shard_map/ppermute | solution.py:426
  60.5 0.1 total.1
  60.8 1.5 %collective-permute-done.13.got_ref = f32[512,128]{1,0:T(8,128)S(1)} collective-permute-done((f32[512,128]{1,0:T(8,128)S(1)}, f32[512,128]{1,0:T(8,128)S(1)}, u32[]{:S(2)}, u32[]{:S(2)}) %collective-permute-start.13) | collective-permute-done | bytes 262176 | tf_op jit(solution)/shard_map/ppermute | solution.py:422
  62.3 0.2 square.1
  62.5 1.6 %collective-permute-start.14 = (f32[1,1024]{1,0:T(1,128)S(1)}, f32[1,1024]{1,0:T(1,128)S(1)}, u32[]{:S(2)}, u32[]{:S(2)}) collective-permute-start(f32[1,1024]{1,0:T(1,128)S(1)} %get-tuple-element.46), channel_id=1, source_target_pairs={{0,1},{1,0},{2,3},{3,2},{4,5},{5,4},{6,7},{7,6},{8,9},{9,8},{10,11... | collective-permute-start | bytes 12296 | tf_op jit(solution)/shard_map/ppermute | solution.py:454
  64.1 2.1 %collective-permute-done.14 = f32[1,1024]{1,0:T(1,128)S(1)} collective-permute-done((f32[1,1024]{1,0:T(1,128)S(1)}, f32[1,1024]{1,0:T(1,128)S(1)}, u32[]{:S(2)}, u32[]{:S(2)}) %collective-permute-start.14) | collective-permute-done | bytes 4128 | tf_op jit(solution)/shard_map/ppermute | solution.py:454
  66.2 2.8 %collective-permute-start.15 = (f32[1,1024]{1,0:T(1,128)S(1)}, f32[1,1024]{1,0:T(1,128)S(1)}, u32[]{:S(2)}, u32[]{:S(2)}) collective-permute-start(f32[1,1024]{1,0:T(1,128)S(1)} %add.3.s0_ref), channel_id=1, source_target_pairs={{0,3},{1,2},{2,1},{3,0},{4,7},{5,6},{6,5},{7,4},{8,11},{9,10},{10,... | collective-permute-start | bytes 12296 | tf_op jit(solution)/shard_map/ppermute | solution.py:454
  69.6 1.4 %collective-permute-done.15.s1_ref = f32[1,1024]{1,0:T(1,128)S(1)} collective-permute-done((f32[1,1024]{1,0:T(1,128)S(1)}, f32[1,1024]{1,0:T(1,128)S(1)}, u32[]{:S(2)}, u32[]{:S(2)}) %collective-permute-start.15) | collective-permute-done | bytes 4128 | tf_op jit(solution)/shard_map/ppermute | solution.py:454
  71.0 4.7 %apply_rows.1 = (f32[8192,128]{1,0:T(8,128)}, f32[1,8192]{1,0:T(1,128)}, f32[8192,128]{1,0:T(8,128)S(1)}) custom-call(s32[1,1024]{1,0:T(1,128)S(1)} %copy-done.2, s32[1]{0:T(128)S(6)} %copy.10.live_hbm, f32[8192,128]{1,0:T(8,128)S(1)} %get-tuple-element.38.emb_in, f32[1024,128]{1,0:T(8,128)S(1)} %get-tuple-element.45.grad_ref, ...), custom_call_target="tpu_custom_call", output_to_operand_aliasing={{2}: (2, {})} | custom-call | flops 13799999488 | bytes 43200000 | tf_op jit(solution)/shard_map/apply_rows/pallas_call | solution.py:383
  (21 shorter events, 0.3 us)
Async XLA Ops:
  8.6 8.2 %collective-permute-start.1 = (bf16[8,512,128]{2,1,0:T(8,128)(2,1)S(1)}, bf16[8,512,128]{2,1,0:T(8,128)(2,1)S(1)}, u32[]{:S(2)}, u32[]{:S(2)}) collective-permute-start(bf16[8,512,128]{2,1,0:T(8,128)(2,1)S(1)} %sib_far.1.refs_0_), channel_id=1, source_target_pairs={{0,4},{4,0},{1,5},{5,1},{2,6},{6,2},{3,7},{7,3},{8,12},{12,8},{9,1... | collective-permute-start | bytes 3145736 | tf_op jit(solution)/shard_map/ppermute | solution.py:422
  15.8 8.8 %collective-permute-start = (bf16[8,512,128]{2,1,0:T(8,128)(2,1)S(1)}, bf16[8,512,128]{2,1,0:T(8,128)(2,1)S(1)}, u32[]{:S(2)}, u32[]{:S(2)}) collective-permute-start(bf16[8,512,128]{2,1,0:T(8,128)(2,1)S(1)} %get-tuple-element.29.refs_1_), channel_id=1, source_target_pairs={{0,4},{4,0},{1,5},{5,1},{2,6},{6,2},{3,7},{7,3},{8,12},{12,8},{9,1... | collective-permute-start | bytes 3145736 | tf_op jit(solution)/shard_map/ppermute | solution.py:422
  16.7 8.0 %collective-permute-start.3 = (bf16[8,512,128]{2,1,0:T(8,128)(2,1)S(1)}, bf16[8,512,128]{2,1,0:T(8,128)(2,1)S(1)}, u32[]{:S(2)}, u32[]{:S(2)}) collective-permute-start(bf16[8,512,128]{2,1,0:T(8,128)(2,1)S(1)} %get-tuple-element.31), channel_id=1, source_target_pairs={{0,4},{4,0},{1,5},{5,1},{2,6},{6,2},{3,7},{7,3},{8,12},{12,8},{9,1... | collective-permute-start | bytes 3145736 | tf_op jit(solution)/shard_map/ppermute | solution.py:422
  20.2 12.0 %collective-permute-start.2 = (bf16[8,256,128]{2,1,0:T(8,128)(2,1)S(1)}, bf16[8,256,128]{2,1,0:T(8,128)(2,1)S(1)}, u32[]{:S(2)}, u32[]{:S(2)}) collective-permute-start(bf16[8,256,128]{2,1,0:T(8,128)(2,1)S(1)} %get-tuple-element.30.refs_2_), channel_id=1, source_target_pairs={{0,32},{4,12},{8,40},{12,20},{16,48},{20,28},{24,56},{28,4},{32,64... | collective-permute-start | bytes 1572872 | tf_op jit(solution)/shard_map/ppermute | solution.py:426
  22.7 9.5 %collective-permute-start.4 = (bf16[8,256,128]{2,1,0:T(8,128)(2,1)S(1)}, bf16[8,256,128]{2,1,0:T(8,128)(2,1)S(1)}, u32[]{:S(2)}, u32[]{:S(2)}) collective-permute-start(bf16[8,256,128]{2,1,0:T(8,128)(2,1)S(1)} %get-tuple-element.32), channel_id=1, source_target_pairs={{0,96},{4,28},{8,104},{12,4},{16,112},{20,12},{24,120},{28,20},{32... | collective-permute-start | bytes 1572872 | tf_op jit(solution)/shard_map/ppermute | solution.py:426
  28.9 18.5 %collective-permute-start.6 = (bf16[8,256,128]{2,1,0:T(8,128)(2,1)S(1)}, bf16[8,256,128]{2,1,0:T(8,128)(2,1)S(1)}, u32[]{:S(2)}, u32[]{:S(2)}) collective-permute-start(bf16[8,256,128]{2,1,0:T(8,128)(2,1)S(1)} %get-tuple-element.33.refs_4_), channel_id=1, source_target_pairs={{0,32},{4,12},{8,40},{12,20},{16,48},{20,28},{24,56},{28,4},{32,64... | collective-permute-start | bytes 1572872 | tf_op jit(solution)/shard_map/ppermute | solution.py:426
  29.0 18.3 %collective-permute-start.7 = (bf16[8,256,128]{2,1,0:T(8,128)(2,1)S(1)}, bf16[8,256,128]{2,1,0:T(8,128)(2,1)S(1)}, u32[]{:S(2)}, u32[]{:S(2)}) collective-permute-start(bf16[8,256,128]{2,1,0:T(8,128)(2,1)S(1)} %get-tuple-element.35), channel_id=1, source_target_pairs={{0,96},{4,28},{8,104},{12,4},{16,112},{20,12},{24,120},{28,20},{32... | collective-permute-start | bytes 1572872 | tf_op jit(solution)/shard_map/ppermute | solution.py:426
  36.6 10.7 %collective-permute-start.5 = (bf16[8,256,128]{2,1,0:T(8,128)(2,1)S(1)}, bf16[8,256,128]{2,1,0:T(8,128)(2,1)S(1)}, u32[]{:S(2)}, u32[]{:S(2)}) collective-permute-start(bf16[8,256,128]{2,1,0:T(8,128)(2,1)S(1)} %get-tuple-element.34.refs_0_), channel_id=1, source_target_pairs={{0,32},{4,12},{8,40},{12,20},{16,48},{20,28},{24,56},{28,4},{32,64... | collective-permute-start | bytes 1572872 | tf_op jit(solution)/shard_map/ppermute | solution.py:426
  38.8 9.2 %collective-permute-start.8 = (bf16[8,256,128]{2,1,0:T(8,128)(2,1)S(1)}, bf16[8,256,128]{2,1,0:T(8,128)(2,1)S(1)}, u32[]{:S(2)}, u32[]{:S(2)}) collective-permute-start(bf16[8,256,128]{2,1,0:T(8,128)(2,1)S(1)} %get-tuple-element.36), channel_id=1, source_target_pairs={{0,96},{4,28},{8,104},{12,4},{16,112},{20,12},{24,120},{28,20},{32... | collective-permute-start | bytes 1572872 | tf_op jit(solution)/shard_map/ppermute | solution.py:426
  43.3 5.0 %collective-permute-start.9 = (bf16[8,512,128]{2,1,0:T(8,128)(2,1)S(1)}, bf16[8,512,128]{2,1,0:T(8,128)(2,1)S(1)}, u32[]{:S(2)}, u32[]{:S(2)}) collective-permute-start(bf16[8,512,128]{2,1,0:T(8,128)(2,1)S(1)} %sib_here.1.refs_0_), channel_id=1, source_target_pairs={{0,4},{4,0},{1,5},{5,1},{2,6},{6,2},{3,7},{7,3},{8,12},{12,8},{9,1... | collective-permute-start | bytes 3145736 | tf_op jit(solution)/shard_map/ppermute | solution.py:422
  47.3 7.3 %copy-start = (f32[1,8192,128]{2,1,0:T(8,128)S(1)}, f32[1,8192,128]{2,1,0:T(8,128)}, u32[]{:S(2)}) copy-start(f32[1,8192,128]{2,1,0:T(8,128)} %param.10) | copy-start | bytes 12582916
  47.3 7.3 %copy-start.1 = (f32[1,8192]{1,0:T(1,128)S(1)}, f32[1,8192]{1,0:T(1,128)}, u32[]{:S(2)}) copy-start(f32[1,8192]{1,0:T(1,128)} %acc_in.1) | copy-start | bytes 98308
  47.3 7.2 %copy-start.2 = (s32[1,1024]{1,0:T(1,128)S(1)}, s32[1,1024]{1,0:T(1,128)}, u32[]{:S(2)}) copy-start(s32[1,1024]{1,0:T(1,128)} %row_hbm.3) | copy-start | bytes 12292
  48.6 10.0 %collective-permute-start.10 = (bf16[2,512,128]{2,1,0:T(8,128)(2,1)S(1)}, bf16[2,512,128]{2,1,0:T(8,128)(2,1)S(1)}, u32[]{:S(2)}, u32[]{:S(2)}) collective-permute-start(bf16[2,512,128]{2,1,0:T(8,128)(2,1)S(1)} %get-tuple-element.37.after_ref), channel_id=1, source_target_pairs={{0,8},{4,36},{8,16},{12,44},{16,24},{20,52},{24,0},{28,60},{32,40}... | collective-permute-start | bytes 786440 | tf_op jit(solution)/shard_map/ppermute | solution.py:426
  50.3 10.2 %collective-permute-start.11 = (bf16[2,512,128]{2,1,0:T(8,128)(2,1)S(1)}, bf16[2,512,128]{2,1,0:T(8,128)(2,1)S(1)}, u32[]{:S(2)}, u32[]{:S(2)}) collective-permute-start(bf16[2,512,128]{2,1,0:T(8,128)(2,1)S(1)} %get-tuple-element.40), channel_id=1, source_target_pairs={{0,16},{4,68},{8,24},{12,76},{16,0},{20,84},{24,8},{28,92},{32,48}... | collective-permute-start | bytes 786440 | tf_op jit(solution)/shard_map/ppermute | solution.py:426
  53.4 7.2 %collective-permute-start.12 = (bf16[2,512,128]{2,1,0:T(8,128)(2,1)S(1)}, bf16[2,512,128]{2,1,0:T(8,128)(2,1)S(1)}, u32[]{:S(2)}, u32[]{:S(2)}) collective-permute-start(bf16[2,512,128]{2,1,0:T(8,128)(2,1)S(1)} %get-tuple-element.41), channel_id=1, source_target_pairs={{0,24},{4,100},{8,0},{12,108},{16,8},{20,116},{24,16},{28,124},{32... | collective-permute-start | bytes 786440 | tf_op jit(solution)/shard_map/ppermute | solution.py:426
  60.7 1.6 %collective-permute-start.13 = (f32[512,128]{1,0:T(8,128)S(1)}, f32[512,128]{1,0:T(8,128)S(1)}, u32[]{:S(2)}, u32[]{:S(2)}) collective-permute-start(f32[512,128]{1,0:T(8,128)S(1)} %get-tuple-element.44), channel_id=1, source_target_pairs={{0,4},{4,0},{1,5},{5,1},{2,6},{6,2},{3,7},{7,3},{8,12},{12,8},{9,1... | collective-permute-start | bytes 786440 | tf_op jit(solution)/shard_map/ppermute | solution.py:422
  62.5 3.7 %collective-permute-start.14 = (f32[1,1024]{1,0:T(1,128)S(1)}, f32[1,1024]{1,0:T(1,128)S(1)}, u32[]{:S(2)}, u32[]{:S(2)}) collective-permute-start(f32[1,1024]{1,0:T(1,128)S(1)} %get-tuple-element.46), channel_id=1, source_target_pairs={{0,1},{1,0},{2,3},{3,2},{4,5},{5,4},{6,7},{7,6},{8,9},{9,8},{10,11... | collective-permute-start | bytes 12296 | tf_op jit(solution)/shard_map/ppermute | solution.py:454
  66.2 4.8 %collective-permute-start.15 = (f32[1,1024]{1,0:T(1,128)S(1)}, f32[1,1024]{1,0:T(1,128)S(1)}, u32[]{:S(2)}, u32[]{:S(2)}) collective-permute-start(f32[1,1024]{1,0:T(1,128)S(1)} %add.3.s0_ref), channel_id=1, source_target_pairs={{0,3},{1,2},{2,1},{3,0},{4,7},{5,6},{6,5},{7,4},{8,11},{9,10},{10,... | collective-permute-start | bytes 12296 | tf_op jit(solution)/shard_map/ppermute | solution.py:454

commit v5 on v4

--- a/solution.py
+++ b/solution.py
@@ -37,10 +37,9 @@
         copies.append(pltpu.make_async_copy(x_hbm.at[here], x_ref.at[here], sems.at[i]))
         copies[-1].start()
     seg_copy.wait()
-    for t in range(seg_ref.shape[0]):
-        last = jnp.max(seg_ref[t], axis=(0, 1), keepdims=True)
-        bound_ref[t : t + 1, :] = jnp.broadcast_to(last, (1, bound_ref.shape[1]))
     seg = [seg_ref[:, h, :] for h in range(4)]
+    last = jnp.maximum(jnp.maximum(seg[0], seg[1]), jnp.maximum(seg[2], seg[3]))
+    bound_ref[...] = jnp.broadcast_to(jnp.max(last, axis=1, keepdims=True), bound_ref.shape)
     same = lambda a, b: jnp.where(seg[a] == seg[b], 1, 0)
     e01, e02, e03 = same(0, 1), same(0, 2), same(0, 3)
     e12, e13, e23 = same(1, 2), same(1, 3), same(2, 3)

time: 75.7 us -> 75.1 us (level); the launches traced: 75.9 us -> 74.2 us
  Pallas kernels: 44 us -> 43.2 us
    pallas_call x1, Pallas kernels: 4.67 us -> 3.84 us  [apply_rows(): pl.pallas_call(functools.partial(apply_body, width), in_specs=[ANY, ANY]...]
  transfers between devices with their start and end apart: 16 -> 16, of which waited for: 5 -> 5; matrix products, arithmetic and copies ran while one was open for 0% -> 0% of each run, Pallas kernels for 40% -> 41%
where the time goes in v5:
time: 75.1 us; the launch traced here: 74.2 us
  Pallas kernels  43.2 us (58%)
  starting transfers between devices  22.3 us (30%)
  waiting for transfers between devices  7.02 us (9%)
  between operations  1.65 us (2%)
    pallas_call x7, Pallas kernels, sums(): pl.pallas_call(functools.partial(sums_body, tuple(kinds), len(after)), in...  29.9 us
    ppermute x9, starting transfers between devices, shift(): lax.ppermute(a, owner, [(index(z, y, c), index(*move(z, y, c))) for z, y...  16.6 us
    pallas_call x1, Pallas kernels, prep(): pl.pallas_call(prep_body, in_specs=[pl.BlockSpec(memory_space=pltpu.HBM)]...  4.48 us
    ppermute x2, starting transfers between devices, per_device(): lax.ppermute(a, 'col', [(i, i ^ k) for i in range(cols)])  4.33 us
    pallas_call x1, Pallas kernels, old_values(): pl.pallas_call(old_body, in_specs=[ANY] * 4, out_specs=[VMEM, SMEM, VMEM]...  4.1 us
    pallas_call x1, Pallas kernels, apply_rows(): pl.pallas_call(functools.partial(apply_body, width), in_specs=[ANY, ANY]...  3.84 us
    ppermute x2, waiting for transfers between devices, per_device(): lax.ppermute(a, 'col', [(i, i ^ k) for i in range(cols)])  3.52 us
    ppermute x9, waiting for transfers between devices, shift(): lax.ppermute(a, owner, [(index(z, y, c), index(*move(z, y, c))) for z, y...  1.97 us
  transfers between devices with their start and end apart: 16, of which 5 were waited for; matrix products, arithmetic and copies ran while one was open for 0% of the time, Pallas kernels for 41%

profile of v5, /device:TPU:0, one launch (start us, length us, event | category | flops | bytes accessed | tf_op | source)
XLA Modules:
  0.0 74.2 jit_solution(3309127542102703702)
XLA Ops:
  0.6 4.5 %prep.1 = (bf16[32,1024,128]{2,1,0:T(8,128)(2,1)S(1)}, f32[32,8,1024]{2,1,0:T(8,128)S(1)}, s32[32,128]{1,0:T(8,128)S(1)}) custom-call(bf16[1024,32,128]{2,1,0:T(8,128)(2,1)} %x_hbm.1, s32[32,4,1024]{2,1,0:T(4,128)} %bitcast.4), custom_call_target="tpu_custom_call" | custom-call | flops 9200000000 | bytes 28800000 | tf_op jit(solution)/shard_map/prep/pallas_call | solution.py:66
  5.1 3.6 %sib_far.1.refs_0_ = bf16[8,512,128]{2,1,0:T(8,128)(2,1)S(1)} custom-call(s32[32,128]{1,0:T(8,128)S(1)} %get-tuple-element.26.bound_ref, f32[32,8,1024]{2,1,0:T(8,128)S(1)} %get-tuple-element.27.ids_ref, bf16[32,1024,128]{2,1,0:T(8,128)(2,1)S(1)} %get-tuple-element.28.x_ref), custom_call_target="tpu_custom_call" | custom-call | flops 9200000000 | bytes 28800000 | tf_op jit(solution)/shard_map/sib_far/pallas_call | solution.py:181
  8.7 0.3 collective-permute-start.1
  9.0 7.0 %sib_next.1 = (bf16[8,512,128]{2,1,0:T(8,128)(2,1)S(1)}, bf16[8,512,128]{2,1,0:T(8,128)(2,1)S(1)}) custom-call(s32[32,128]{1,0:T(8,128)S(1)} %get-tuple-element.26.bound_ref, f32[32,8,1024]{2,1,0:T(8,128)S(1)} %get-tuple-element.27.ids_ref, bf16[32,1024,128]{2,1,0:T(8,128)(2,1)S(1)} %get-tuple-element.28.x_ref, bf16[8,512,128]{2,1,0:T(8,128)(2,1)S(1)} %sib_far.1.refs_0_), custom_call_target="tpu_custom_call" | custom-call | flops 18400000000 | bytes 57600000 | tf_op jit(solution)/shard_map/sib_next/pallas_call | solution.py:181
  15.9 0.8 %collective-permute-start = (bf16[8,512,128]{2,1,0:T(8,128)(2,1)S(1)}, bf16[8,512,128]{2,1,0:T(8,128)(2,1)S(1)}, u32[]{:S(2)}, u32[]{:S(2)}) collective-permute-start(bf16[8,512,128]{2,1,0:T(8,128)(2,1)S(1)} %get-tuple-element.29.refs_1_), channel_id=1, source_target_pairs={{0,4},{4,0},{1,5},{5,1},{2,6},{6,2},{3,7},{7,3},{8,12},{12,8},{9,1... | collective-permute-start | bytes 3145736 | tf_op jit(solution)/shard_map/ppermute | solution.py:421
  16.8 0.1 collective-permute-start.3
  16.9 3.6 %own_far.1 = (bf16[8,256,128]{2,1,0:T(8,128)(2,1)S(1)}, bf16[8,256,128]{2,1,0:T(8,128)(2,1)S(1)}) custom-call(s32[32,128]{1,0:T(8,128)S(1)} %get-tuple-element.26.bound_ref, f32[32,8,1024]{2,1,0:T(8,128)S(1)} %get-tuple-element.27.ids_ref, bf16[32,1024,128]{2,1,0:T(8,128)(2,1)S(1)} %get-tuple-element.28.x_ref, ...), custom_call_target="tpu_custom_call" | custom-call | flops 9200000000 | bytes 28800000 | tf_op jit(solution)/shard_map/own_far/pallas_call | solution.py:181
  20.5 2.3 %collective-permute-start.2 = (bf16[8,256,128]{2,1,0:T(8,128)(2,1)S(1)}, bf16[8,256,128]{2,1,0:T(8,128)(2,1)S(1)}, u32[]{:S(2)}, u32[]{:S(2)}) collective-permute-start(bf16[8,256,128]{2,1,0:T(8,128)(2,1)S(1)} %get-tuple-element.30.refs_2_), channel_id=1, source_target_pairs={{0,32},{4,12},{8,40},{12,20},{16,48},{20,28},{24,56},{28,4},{32,64... | collective-permute-start | bytes 1572872 | tf_op jit(solution)/shard_map/ppermute | solution.py:425
  22.8 2.0 %collective-permute-start.4 = (bf16[8,256,128]{2,1,0:T(8,128)(2,1)S(1)}, bf16[8,256,128]{2,1,0:T(8,128)(2,1)S(1)}, u32[]{:S(2)}, u32[]{:S(2)}) collective-permute-start(bf16[8,256,128]{2,1,0:T(8,128)(2,1)S(1)} %get-tuple-element.32), channel_id=1, source_target_pairs={{0,96},{4,28},{8,104},{12,4},{16,112},{20,12},{24,120},{28,20},{32... | collective-permute-start | bytes 1572872 | tf_op jit(solution)/shard_map/ppermute | solution.py:425
  24.8 4.2 %free.1 = (bf16[8,256,128]{2,1,0:T(8,128)(2,1)S(1)}, bf16[8,256,128]{2,1,0:T(8,128)(2,1)S(1)}) custom-call(s32[32,128]{1,0:T(8,128)S(1)} %get-tuple-element.26.bound_ref, f32[32,8,1024]{2,1,0:T(8,128)S(1)} %get-tuple-element.27.ids_ref, bf16[32,1024,128]{2,1,0:T(8,128)(2,1)S(1)} %get-tuple-element.28.x_ref, ...), custom_call_target="tpu_custom_call" | custom-call | flops 9200000000 | bytes 28800000 | tf_op jit(solution)/shard_map/free/pallas_call | solution.py:181
  29.1 3.2 %collective-permute-start.7 = (bf16[8,256,128]{2,1,0:T(8,128)(2,1)S(1)}, bf16[8,256,128]{2,1,0:T(8,128)(2,1)S(1)}, u32[]{:S(2)}, u32[]{:S(2)}) collective-permute-start(bf16[8,256,128]{2,1,0:T(8,128)(2,1)S(1)} %get-tuple-element.35), channel_id=1, source_target_pairs={{0,96},{4,28},{8,104},{12,4},{16,112},{20,12},{24,120},{28,20},{32... | collective-permute-start | bytes 1572872 | tf_op jit(solution)/shard_map/ppermute | solution.py:425
  32.3 4.4 %bound.1 = (bf16[8,256,128]{2,1,0:T(8,128)(2,1)S(1)}, bf16[8,256,128]{2,1,0:T(8,128)(2,1)S(1)}) custom-call(s32[32,128]{1,0:T(8,128)S(1)} %get-tuple-element.26.bound_ref, f32[32,8,1024]{2,1,0:T(8,128)S(1)} %get-tuple-element.27.ids_ref, bf16[32,1024,128]{2,1,0:T(8,128)(2,1)S(1)} %get-tuple-element.28.x_ref, ...), custom_call_target="tpu_custom_call" | custom-call | flops 9200000000 | bytes 28800000 | tf_op jit(solution)/shard_map/bound/pallas_call | solution.py:181
  36.7 1.6 %collective-permute-start.5 = (bf16[8,256,128]{2,1,0:T(8,128)(2,1)S(1)}, bf16[8,256,128]{2,1,0:T(8,128)(2,1)S(1)}, u32[]{:S(2)}, u32[]{:S(2)}) collective-permute-start(bf16[8,256,128]{2,1,0:T(8,128)(2,1)S(1)} %get-tuple-element.34.refs_0_), channel_id=1, source_target_pairs={{0,32},{4,12},{8,40},{12,20},{16,48},{20,28},{24,56},{28,4},{32,64... | collective-permute-start | bytes 1572872 | tf_op jit(solution)/shard_map/ppermute | solution.py:425
  38.4 1.7 %collective-permute-start.8 = (bf16[8,256,128]{2,1,0:T(8,128)(2,1)S(1)}, bf16[8,256,128]{2,1,0:T(8,128)(2,1)S(1)}, u32[]{:S(2)}, u32[]{:S(2)}) collective-permute-start(bf16[8,256,128]{2,1,0:T(8,128)(2,1)S(1)} %get-tuple-element.36), channel_id=1, source_target_pairs={{0,96},{4,28},{8,104},{12,4},{16,112},{20,12},{24,120},{28,20},{32... | collective-permute-start | bytes 1572872 | tf_op jit(solution)/shard_map/ppermute | solution.py:425
  40.0 3.4 %sib_here.1.refs_0_ = bf16[8,512,128]{2,1,0:T(8,128)(2,1)S(1)} custom-call(s32[32,128]{1,0:T(8,128)S(1)} %get-tuple-element.26.bound_ref, f32[32,8,1024]{2,1,0:T(8,128)S(1)} %get-tuple-element.27.ids_ref, bf16[32,1024,128]{2,1,0:T(8,128)(2,1)S(1)} %get-tuple-element.28.x_ref, bf16[8,256,128]{2,1,0:T(8,128)(2,1)S(1)} %get-tuple-element.34.refs_0_), custom_call_target="tpu_custom_call" | custom-call | flops 9200000000 | bytes 28800000 | tf_op jit(solution)/shard_map/sib_here/pallas_call | solution.py:181
  43.5 3.7 %own_here.1.here_ref = f32[8,512,128]{2,1,0:T(8,128)S(1)} custom-call(s32[32,128]{1,0:T(8,128)S(1)} %get-tuple-element.26.bound_ref, f32[32,8,1024]{2,1,0:T(8,128)S(1)} %get-tuple-element.27.ids_ref, bf16[32,1024,128]{2,1,0:T(8,128)(2,1)S(1)} %get-tuple-element.28.x_ref, bf16[8,512,128]{2,1,0:T(8,128)(2,1)S(1)} %sib_here.1.refs_0_), custom_call_target="tpu_custom_call" | custom-call | flops 2300000000 | bytes 7200000 | tf_op jit(solution)/shard_map/own_here/pallas_call | solution.py:181
  47.3 0.3 collective-permute-done.8.back_high
  47.6 0.3 gather.1.here_ref
  47.9 0.3 fold.1
  48.2 1.7 %collective-permute-start.10 = (bf16[2,512,128]{2,1,0:T(8,128)(2,1)S(1)}, bf16[2,512,128]{2,1,0:T(8,128)(2,1)S(1)}, u32[]{:S(2)}, u32[]{:S(2)}) collective-permute-start(bf16[2,512,128]{2,1,0:T(8,128)(2,1)S(1)} %get-tuple-element.37.after_ref), channel_id=1, source_target_pairs={{0,8},{4,36},{8,16},{12,44},{16,24},{20,52},{24,0},{28,60},{32,40}... | collective-permute-start | bytes 786440 | tf_op jit(solution)/shard_map/ppermute | solution.py:425
  49.8 2.7 %collective-permute-start.11 = (bf16[2,512,128]{2,1,0:T(8,128)(2,1)S(1)}, bf16[2,512,128]{2,1,0:T(8,128)(2,1)S(1)}, u32[]{:S(2)}, u32[]{:S(2)}) collective-permute-start(bf16[2,512,128]{2,1,0:T(8,128)(2,1)S(1)} %get-tuple-element.40), channel_id=1, source_target_pairs={{0,16},{4,68},{8,24},{12,76},{16,0},{20,84},{24,8},{28,92},{32,48}... | collective-permute-start | bytes 786440 | tf_op jit(solution)/shard_map/ppermute | solution.py:425
  52.6 1.3 %collective-permute-start.12 = (bf16[2,512,128]{2,1,0:T(8,128)(2,1)S(1)}, bf16[2,512,128]{2,1,0:T(8,128)(2,1)S(1)}, u32[]{:S(2)}, u32[]{:S(2)}) collective-permute-start(bf16[2,512,128]{2,1,0:T(8,128)(2,1)S(1)} %get-tuple-element.41), channel_id=1, source_target_pairs={{0,24},{4,100},{8,0},{12,108},{16,8},{20,116},{24,16},{28,124},{32... | collective-permute-start | bytes 786440 | tf_op jit(solution)/shard_map/ppermute | solution.py:425
  53.9 4.1 %old_values.1 = (f32[1024,128]{1,0:T(8,128)S(1)}, f32[1,1024]{1,0:T(1,128)S(1)}, f32[8192,128]{1,0:T(8,128)S(1)}) custom-call(s32[1,1024]{1,0:T(1,128)S(1)} %copy-done.2, f32[8192,128]{1,0:T(8,128)S(1)} %bitcast.3, f32[1,8192]{1,0:T(1,128)S(1)} %copy-done.1, bf16[2,512,128]{2,1,0:T(8,128)(2,1)S(1)} %get-tuple-element.37.after_ref), custom_call_target="tpu_custom_call" | custom-call | flops 9200000000 | bytes 28800000 | tf_op jit(solution)/shard_map/old_values/pallas_call | solution.py:216
  58.0 1.7 %collective-permute-done.11.c_ref = bf16[2,512,128]{2,1,0:T(8,128)(2,1)S(1)} collective-permute-done((bf16[2,512,128]{2,1,0:T(8,128)(2,1)S(1)}, bf16[2,512,128]{2,1,0:T(8,128)(2,1)S(1)}, u32[]{:S(2)}, u32[]{:S(2)}) %collective-permute-start.11) | collective-permute-done | bytes 262176 | tf_op jit(solution)/shard_map/ppermute | solution.py:425
  59.7 0.1 total.1
  59.9 1.5 %collective-permute-done.13.got_ref = f32[512,128]{1,0:T(8,128)S(1)} collective-permute-done((f32[512,128]{1,0:T(8,128)S(1)}, f32[512,128]{1,0:T(8,128)S(1)}, u32[]{:S(2)}, u32[]{:S(2)}) %collective-permute-start.13) | collective-permute-done | bytes 262176 | tf_op jit(solution)/shard_map/ppermute | solution.py:421
  61.5 0.2 square.1
  61.7 1.6 %collective-permute-start.14 = (f32[1,1024]{1,0:T(1,128)S(1)}, f32[1,1024]{1,0:T(1,128)S(1)}, u32[]{:S(2)}, u32[]{:S(2)}) collective-permute-start(f32[1,1024]{1,0:T(1,128)S(1)} %get-tuple-element.46), channel_id=1, source_target_pairs={{0,1},{1,0},{2,3},{3,2},{4,5},{5,4},{6,7},{7,6},{8,9},{9,8},{10,11... | collective-permute-start | bytes 12296 | tf_op jit(solution)/shard_map/ppermute | solution.py:453
  63.3 2.1 %collective-permute-done.14 = f32[1,1024]{1,0:T(1,128)S(1)} collective-permute-done((f32[1,1024]{1,0:T(1,128)S(1)}, f32[1,1024]{1,0:T(1,128)S(1)}, u32[]{:S(2)}, u32[]{:S(2)}) %collective-permute-start.14) | collective-permute-done | bytes 4128 | tf_op jit(solution)/shard_map/ppermute | solution.py:453
  65.4 2.8 %collective-permute-start.15 = (f32[1,1024]{1,0:T(1,128)S(1)}, f32[1,1024]{1,0:T(1,128)S(1)}, u32[]{:S(2)}, u32[]{:S(2)}) collective-permute-start(f32[1,1024]{1,0:T(1,128)S(1)} %add.3.s0_ref), channel_id=1, source_target_pairs={{0,3},{1,2},{2,1},{3,0},{4,7},{5,6},{6,5},{7,4},{8,11},{9,10},{10,... | collective-permute-start | bytes 12296 | tf_op jit(solution)/shard_map/ppermute | solution.py:453
  68.8 1.4 %collective-permute-done.15.s1_ref = f32[1,1024]{1,0:T(1,128)S(1)} collective-permute-done((f32[1,1024]{1,0:T(1,128)S(1)}, f32[1,1024]{1,0:T(1,128)S(1)}, u32[]{:S(2)}, u32[]{:S(2)}) %collective-permute-start.15) | collective-permute-done | bytes 4128 | tf_op jit(solution)/shard_map/ppermute | solution.py:453
  70.2 3.8 %apply_rows.1 = (f32[8192,128]{1,0:T(8,128)}, f32[1,8192]{1,0:T(1,128)}, f32[8192,128]{1,0:T(8,128)S(1)}) custom-call(s32[1,1024]{1,0:T(1,128)S(1)} %copy-done.2, s32[1]{0:T(128)S(6)} %copy.10.live_hbm, f32[8192,128]{1,0:T(8,128)S(1)} %get-tuple-element.38.emb_in, f32[1024,128]{1,0:T(8,128)S(1)} %get-tuple-element.45.grad_ref, ...), custom_call_target="tpu_custom_call", output_to_operand_aliasing={{2}: (2, {})} | custom-call | flops 13799999488 | bytes 43200000 | tf_op jit(solution)/shard_map/apply_rows/pallas_call | solution.py:382
  (21 shorter events, 0.3 us)
Async XLA Ops:
  8.7 8.2 %collective-permute-start.1 = (bf16[8,512,128]{2,1,0:T(8,128)(2,1)S(1)}, bf16[8,512,128]{2,1,0:T(8,128)(2,1)S(1)}, u32[]{:S(2)}, u32[]{:S(2)}) collective-permute-start(bf16[8,512,128]{2,1,0:T(8,128)(2,1)S(1)} %sib_far.1.refs_0_), channel_id=1, source_target_pairs={{0,4},{4,0},{1,5},{5,1},{2,6},{6,2},{3,7},{7,3},{8,12},{12,8},{9,1... | collective-permute-start | bytes 3145736 | tf_op jit(solution)/shard_map/ppermute | solution.py:421
  15.9 8.8 %collective-permute-start = (bf16[8,512,128]{2,1,0:T(8,128)(2,1)S(1)}, bf16[8,512,128]{2,1,0:T(8,128)(2,1)S(1)}, u32[]{:S(2)}, u32[]{:S(2)}) collective-permute-start(bf16[8,512,128]{2,1,0:T(8,128)(2,1)S(1)} %get-tuple-element.29.refs_1_), channel_id=1, source_target_pairs={{0,4},{4,0},{1,5},{5,1},{2,6},{6,2},{3,7},{7,3},{8,12},{12,8},{9,1... | collective-permute-start | bytes 3145736 | tf_op jit(solution)/shard_map/ppermute | solution.py:421
  16.8 8.0 %collective-permute-start.3 = (bf16[8,512,128]{2,1,0:T(8,128)(2,1)S(1)}, bf16[8,512,128]{2,1,0:T(8,128)(2,1)S(1)}, u32[]{:S(2)}, u32[]{:S(2)}) collective-permute-start(bf16[8,512,128]{2,1,0:T(8,128)(2,1)S(1)} %get-tuple-element.31), channel_id=1, source_target_pairs={{0,4},{4,0},{1,5},{5,1},{2,6},{6,2},{3,7},{7,3},{8,12},{12,8},{9,1... | collective-permute-start | bytes 3145736 | tf_op jit(solution)/shard_map/ppermute | solution.py:421
  20.5 11.8 %collective-permute-start.2 = (bf16[8,256,128]{2,1,0:T(8,128)(2,1)S(1)}, bf16[8,256,128]{2,1,0:T(8,128)(2,1)S(1)}, u32[]{:S(2)}, u32[]{:S(2)}) collective-permute-start(bf16[8,256,128]{2,1,0:T(8,128)(2,1)S(1)} %get-tuple-element.30.refs_2_), channel_id=1, source_target_pairs={{0,32},{4,12},{8,40},{12,20},{16,48},{20,28},{24,56},{28,4},{32,64... | collective-permute-start | bytes 1572872 | tf_op jit(solution)/shard_map/ppermute | solution.py:425
  22.8 9.5 %collective-permute-start.4 = (bf16[8,256,128]{2,1,0:T(8,128)(2,1)S(1)}, bf16[8,256,128]{2,1,0:T(8,128)(2,1)S(1)}, u32[]{:S(2)}, u32[]{:S(2)}) collective-permute-start(bf16[8,256,128]{2,1,0:T(8,128)(2,1)S(1)} %get-tuple-element.32), channel_id=1, source_target_pairs={{0,96},{4,28},{8,104},{12,4},{16,112},{20,12},{24,120},{28,20},{32... | collective-permute-start | bytes 1572872 | tf_op jit(solution)/shard_map/ppermute | solution.py:425
  29.0 18.3 %collective-permute-start.6 = (bf16[8,256,128]{2,1,0:T(8,128)(2,1)S(1)}, bf16[8,256,128]{2,1,0:T(8,128)(2,1)S(1)}, u32[]{:S(2)}, u32[]{:S(2)}) collective-permute-start(bf16[8,256,128]{2,1,0:T(8,128)(2,1)S(1)} %get-tuple-element.33.refs_4_), channel_id=1, source_target_pairs={{0,32},{4,12},{8,40},{12,20},{16,48},{20,28},{24,56},{28,4},{32,64... | collective-permute-start | bytes 1572872 | tf_op jit(solution)/shard_map/ppermute | solution.py:425
  29.1 18.2 %collective-permute-start.7 = (bf16[8,256,128]{2,1,0:T(8,128)(2,1)S(1)}, bf16[8,256,128]{2,1,0:T(8,128)(2,1)S(1)}, u32[]{:S(2)}, u32[]{:S(2)}) collective-permute-start(bf16[8,256,128]{2,1,0:T(8,128)(2,1)S(1)} %get-tuple-element.35), channel_id=1, source_target_pairs={{0,96},{4,28},{8,104},{12,4},{16,112},{20,12},{24,120},{28,20},{32... | collective-permute-start | bytes 1572872 | tf_op jit(solution)/shard_map/ppermute | solution.py:425
  36.7 10.6 %collective-permute-start.5 = (bf16[8,256,128]{2,1,0:T(8,128)(2,1)S(1)}, bf16[8,256,128]{2,1,0:T(8,128)(2,1)S(1)}, u32[]{:S(2)}, u32[]{:S(2)}) collective-permute-start(bf16[8,256,128]{2,1,0:T(8,128)(2,1)S(1)} %get-tuple-element.34.refs_0_), channel_id=1, source_target_pairs={{0,32},{4,12},{8,40},{12,20},{16,48},{20,28},{24,56},{28,4},{32,64... | collective-permute-start | bytes 1572872 | tf_op jit(solution)/shard_map/ppermute | solution.py:425
  38.4 9.2 %collective-permute-start.8 = (bf16[8,256,128]{2,1,0:T(8,128)(2,1)S(1)}, bf16[8,256,128]{2,1,0:T(8,128)(2,1)S(1)}, u32[]{:S(2)}, u32[]{:S(2)}) collective-permute-start(bf16[8,256,128]{2,1,0:T(8,128)(2,1)S(1)} %get-tuple-element.36), channel_id=1, source_target_pairs={{0,96},{4,28},{8,104},{12,4},{16,112},{20,12},{24,120},{28,20},{32... | collective-permute-start | bytes 1572872 | tf_op jit(solution)/shard_map/ppermute | solution.py:425
  43.4 4.5 %collective-permute-start.9 = (bf16[8,512,128]{2,1,0:T(8,128)(2,1)S(1)}, bf16[8,512,128]{2,1,0:T(8,128)(2,1)S(1)}, u32[]{:S(2)}, u32[]{:S(2)}) collective-permute-start(bf16[8,512,128]{2,1,0:T(8,128)(2,1)S(1)} %sib_here.1.refs_0_), channel_id=1, source_target_pairs={{0,4},{4,0},{1,5},{5,1},{2,6},{6,2},{3,7},{7,3},{8,12},{12,8},{9,1... | collective-permute-start | bytes 3145736 | tf_op jit(solution)/shard_map/ppermute | solution.py:421
  47.2 6.7 %copy-start = (f32[1,8192,128]{2,1,0:T(8,128)S(1)}, f32[1,8192,128]{2,1,0:T(8,128)}, u32[]{:S(2)}) copy-start(f32[1,8192,128]{2,1,0:T(8,128)} %param.10) | copy-start | bytes 12582916
  47.2 6.7 %copy-start.1 = (f32[1,8192]{1,0:T(1,128)S(1)}, f32[1,8192]{1,0:T(1,128)}, u32[]{:S(2)}) copy-start(f32[1,8192]{1,0:T(1,128)} %acc_in.1) | copy-start | bytes 98308
  47.3 6.7 %copy-start.2 = (s32[1,1024]{1,0:T(1,128)S(1)}, s32[1,1024]{1,0:T(1,128)}, u32[]{:S(2)}) copy-start(s32[1,1024]{1,0:T(1,128)} %row_hbm.3) | copy-start | bytes 12292
  48.2 9.8 %collective-permute-start.10 = (bf16[2,512,128]{2,1,0:T(8,128)(2,1)S(1)}, bf16[2,512,128]{2,1,0:T(8,128)(2,1)S(1)}, u32[]{:S(2)}, u32[]{:S(2)}) collective-permute-start(bf16[2,512,128]{2,1,0:T(8,128)(2,1)S(1)} %get-tuple-element.37.after_ref), channel_id=1, source_target_pairs={{0,8},{4,36},{8,16},{12,44},{16,24},{20,52},{24,0},{28,60},{32,40}... | collective-permute-start | bytes 786440 | tf_op jit(solution)/shard_map/ppermute | solution.py:425
  49.8 9.9 %collective-permute-start.11 = (bf16[2,512,128]{2,1,0:T(8,128)(2,1)S(1)}, bf16[2,512,128]{2,1,0:T(8,128)(2,1)S(1)}, u32[]{:S(2)}, u32[]{:S(2)}) collective-permute-start(bf16[2,512,128]{2,1,0:T(8,128)(2,1)S(1)} %get-tuple-element.40), channel_id=1, source_target_pairs={{0,16},{4,68},{8,24},{12,76},{16,0},{20,84},{24,8},{28,92},{32,48}... | collective-permute-start | bytes 786440 | tf_op jit(solution)/shard_map/ppermute | solution.py:425
  52.6 7.2 %collective-permute-start.12 = (bf16[2,512,128]{2,1,0:T(8,128)(2,1)S(1)}, bf16[2,512,128]{2,1,0:T(8,128)(2,1)S(1)}, u32[]{:S(2)}, u32[]{:S(2)}) collective-permute-start(bf16[2,512,128]{2,1,0:T(8,128)(2,1)S(1)} %get-tuple-element.41), channel_id=1, source_target_pairs={{0,24},{4,100},{8,0},{12,108},{16,8},{20,116},{24,16},{28,124},{32... | collective-permute-start | bytes 786440 | tf_op jit(solution)/shard_map/ppermute | solution.py:425
  59.9 1.6 %collective-permute-start.13 = (f32[512,128]{1,0:T(8,128)S(1)}, f32[512,128]{1,0:T(8,128)S(1)}, u32[]{:S(2)}, u32[]{:S(2)}) collective-permute-start(f32[512,128]{1,0:T(8,128)S(1)} %get-tuple-element.44), channel_id=1, source_target_pairs={{0,4},{4,0},{1,5},{5,1},{2,6},{6,2},{3,7},{7,3},{8,12},{12,8},{9,1... | collective-permute-start | bytes 786440 | tf_op jit(solution)/shard_map/ppermute | solution.py:421
  61.7 3.7 %collective-permute-start.14 = (f32[1,1024]{1,0:T(1,128)S(1)}, f32[1,1024]{1,0:T(1,128)S(1)}, u32[]{:S(2)}, u32[]{:S(2)}) collective-permute-start(f32[1,1024]{1,0:T(1,128)S(1)} %get-tuple-element.46), channel_id=1, source_target_pairs={{0,1},{1,0},{2,3},{3,2},{4,5},{5,4},{6,7},{7,6},{8,9},{9,8},{10,11... | collective-permute-start | bytes 12296 | tf_op jit(solution)/shard_map/ppermute | solution.py:453
  65.4 4.8 %collective-permute-start.15 = (f32[1,1024]{1,0:T(1,128)S(1)}, f32[1,1024]{1,0:T(1,128)S(1)}, u32[]{:S(2)}, u32[]{:S(2)}) collective-permute-start(f32[1,1024]{1,0:T(1,128)S(1)} %add.3.s0_ref), channel_id=1, source_target_pairs={{0,3},{1,2},{2,1},{3,0},{4,7},{5,6},{6,5},{7,4},{8,11},{9,10},{10,... | collective-permute-start | bytes 12296 | tf_op jit(solution)/shard_map/ppermute | solution.py:453

commit v6 on v5

--- a/solution.py
+++ b/solution.py
@@ -345,7 +345,7 @@
     row_load.wait()
     live_load.wait()
     live = live_ref[0]
-    block = 16
+    block = 32
 
     def scatter(put):
         def step(i, carry):

time: 75.1 us -> 74.1 us (0.987)
    pallas_call x7, Pallas kernels: 29.9 us -> 29.1 us  [sums(): pl.pallas_call(functools.partial(sums_body, tuple(kinds), len(after)), in...]
  transfers between devices with their start and end apart: 16 -> 16, of which waited for: 5 -> 6; matrix products, arithmetic and copies ran while one was open for 0% -> 0% of each run, Pallas kernels for 41% -> 41%
where the time goes in v6:
time: 74.1 us; the launch traced here: 73.4 us
  Pallas kernels  42.6 us (57%)
  starting transfers between devices  21.9 us (30%)
  waiting for transfers between devices  7.23 us (10%)
  between operations  1.64 us (2%)
    pallas_call x7, Pallas kernels, sums(): pl.pallas_call(functools.partial(sums_body, tuple(kinds), len(after)), in...  29.1 us
    ppermute x9, starting transfers between devices, shift(): lax.ppermute(a, owner, [(index(z, y, c), index(*move(z, y, c))) for z, y...  16.2 us
    pallas_call x1, Pallas kernels, prep(): pl.pallas_call(prep_body, in_specs=[pl.BlockSpec(memory_space=pltpu.HBM)]...  4.48 us
    ppermute x2, starting transfers between devices, per_device(): lax.ppermute(a, 'col', [(i, i ^ k) for i in range(cols)])  4.34 us
    pallas_call x1, Pallas kernels, old_values(): pl.pallas_call(old_body, in_specs=[ANY] * 4, out_specs=[VMEM, SMEM, VMEM]...  4.1 us
    pallas_call x1, Pallas kernels, apply_rows(): pl.pallas_call(functools.partial(apply_body, width), in_specs=[ANY, ANY]...  3.96 us
    ppermute x2, waiting for transfers between devices, per_device(): lax.ppermute(a, 'col', [(i, i ^ k) for i in range(cols)])  3.52 us
    ppermute x9, waiting for transfers between devices, shift(): lax.ppermute(a, owner, [(index(z, y, c), index(*move(z, y, c))) for z, y...  2.18 us
  transfers between devices with their start and end apart: 16, of which 6 were waited for; matrix products, arithmetic and copies ran while one was open for 0% of the time, Pallas kernels for 41%

profile of v6, /device:TPU:0, one launch (start us, length us, event | category | flops | bytes accessed | tf_op | source)
XLA Modules:
  0.0 73.4 jit_solution(12458006484088912238)
XLA Ops:
  0.6 4.5 %prep.1 = (bf16[32,1024,128]{2,1,0:T(8,128)(2,1)S(1)}, f32[32,8,1024]{2,1,0:T(8,128)S(1)}, s32[32,128]{1,0:T(8,128)S(1)}) custom-call(bf16[1024,32,128]{2,1,0:T(8,128)(2,1)} %x_hbm.1, s32[32,4,1024]{2,1,0:T(4,128)} %bitcast.4), custom_call_target="tpu_custom_call" | custom-call | flops 9200000000 | bytes 28800000 | tf_op jit(solution)/shard_map/prep/pallas_call | solution.py:66
  5.1 3.6 %sib_far.1.refs_0_ = bf16[8,512,128]{2,1,0:T(8,128)(2,1)S(1)} custom-call(s32[32,128]{1,0:T(8,128)S(1)} %get-tuple-element.26.bound_ref, f32[32,8,1024]{2,1,0:T(8,128)S(1)} %get-tuple-element.27.ids_ref, bf16[32,1024,128]{2,1,0:T(8,128)(2,1)S(1)} %get-tuple-element.28.x_ref), custom_call_target="tpu_custom_call" | custom-call | flops 9200000000 | bytes 28800000 | tf_op jit(solution)/shard_map/sib_far/pallas_call | solution.py:181
  8.7 0.3 collective-permute-start.1
  9.0 6.8 %sib_next.1 = (bf16[8,512,128]{2,1,0:T(8,128)(2,1)S(1)}, bf16[8,512,128]{2,1,0:T(8,128)(2,1)S(1)}) custom-call(s32[32,128]{1,0:T(8,128)S(1)} %get-tuple-element.26.bound_ref, f32[32,8,1024]{2,1,0:T(8,128)S(1)} %get-tuple-element.27.ids_ref, bf16[32,1024,128]{2,1,0:T(8,128)(2,1)S(1)} %get-tuple-element.28.x_ref, bf16[8,512,128]{2,1,0:T(8,128)(2,1)S(1)} %sib_far.1.refs_0_), custom_call_target="tpu_custom_call" | custom-call | flops 18400000000 | bytes 57600000 | tf_op jit(solution)/shard_map/sib_next/pallas_call | solution.py:181
  15.8 0.8 %collective-permute-start = (bf16[8,512,128]{2,1,0:T(8,128)(2,1)S(1)}, bf16[8,512,128]{2,1,0:T(8,128)(2,1)S(1)}, u32[]{:S(2)}, u32[]{:S(2)}) collective-permute-start(bf16[8,512,128]{2,1,0:T(8,128)(2,1)S(1)} %get-tuple-element.29.refs_1_), channel_id=1, source_target_pairs={{0,4},{4,0},{1,5},{5,1},{2,6},{6,2},{3,7},{7,3},{8,12},{12,8},{9,1... | collective-permute-start | bytes 3145736 | tf_op jit(solution)/shard_map/ppermute | solution.py:421
  16.7 3.6 %own_far.1 = (bf16[8,256,128]{2,1,0:T(8,128)(2,1)S(1)}, bf16[8,256,128]{2,1,0:T(8,128)(2,1)S(1)}) custom-call(s32[32,128]{1,0:T(8,128)S(1)} %get-tuple-element.26.bound_ref, f32[32,8,1024]{2,1,0:T(8,128)S(1)} %get-tuple-element.27.ids_ref, bf16[32,1024,128]{2,1,0:T(8,128)(2,1)S(1)} %get-tuple-element.28.x_ref, ...), custom_call_target="tpu_custom_call" | custom-call | flops 9200000000 | bytes 28800000 | tf_op jit(solution)/shard_map/own_far/pallas_call | solution.py:181
  20.3 2.1 %collective-permute-start.2 = (bf16[8,256,128]{2,1,0:T(8,128)(2,1)S(1)}, bf16[8,256,128]{2,1,0:T(8,128)(2,1)S(1)}, u32[]{:S(2)}, u32[]{:S(2)}) collective-permute-start(bf16[8,256,128]{2,1,0:T(8,128)(2,1)S(1)} %get-tuple-element.30.refs_2_), channel_id=1, source_target_pairs={{0,32},{4,12},{8,40},{12,20},{16,48},{20,28},{24,56},{28,4},{32,64... | collective-permute-start | bytes 1572872 | tf_op jit(solution)/shard_map/ppermute | solution.py:425
  22.4 1.8 %collective-permute-start.4 = (bf16[8,256,128]{2,1,0:T(8,128)(2,1)S(1)}, bf16[8,256,128]{2,1,0:T(8,128)(2,1)S(1)}, u32[]{:S(2)}, u32[]{:S(2)}) collective-permute-start(bf16[8,256,128]{2,1,0:T(8,128)(2,1)S(1)} %get-tuple-element.32), channel_id=1, source_target_pairs={{0,96},{4,28},{8,104},{12,4},{16,112},{20,12},{24,120},{28,20},{32... | collective-permute-start | bytes 1572872 | tf_op jit(solution)/shard_map/ppermute | solution.py:425
  24.2 4.0 %free.1 = (bf16[8,256,128]{2,1,0:T(8,128)(2,1)S(1)}, bf16[8,256,128]{2,1,0:T(8,128)(2,1)S(1)}) custom-call(s32[32,128]{1,0:T(8,128)S(1)} %get-tuple-element.26.bound_ref, f32[32,8,1024]{2,1,0:T(8,128)S(1)} %get-tuple-element.27.ids_ref, bf16[32,1024,128]{2,1,0:T(8,128)(2,1)S(1)} %get-tuple-element.28.x_ref, ...), custom_call_target="tpu_custom_call" | custom-call | flops 9200000000 | bytes 28800000 | tf_op jit(solution)/shard_map/free/pallas_call | solution.py:181
  28.2 0.5 collective-permute-start.6
  28.7 2.8 %collective-permute-start.7 = (bf16[8,256,128]{2,1,0:T(8,128)(2,1)S(1)}, bf16[8,256,128]{2,1,0:T(8,128)(2,1)S(1)}, u32[]{:S(2)}, u32[]{:S(2)}) collective-permute-start(bf16[8,256,128]{2,1,0:T(8,128)(2,1)S(1)} %get-tuple-element.35), channel_id=1, source_target_pairs={{0,96},{4,28},{8,104},{12,4},{16,112},{20,12},{24,120},{28,20},{32... | collective-permute-start | bytes 1572872 | tf_op jit(solution)/shard_map/ppermute | solution.py:425
  31.6 4.4 %bound.1 = (bf16[8,256,128]{2,1,0:T(8,128)(2,1)S(1)}, bf16[8,256,128]{2,1,0:T(8,128)(2,1)S(1)}) custom-call(s32[32,128]{1,0:T(8,128)S(1)} %get-tuple-element.26.bound_ref, f32[32,8,1024]{2,1,0:T(8,128)S(1)} %get-tuple-element.27.ids_ref, bf16[32,1024,128]{2,1,0:T(8,128)(2,1)S(1)} %get-tuple-element.28.x_ref, ...), custom_call_target="tpu_custom_call" | custom-call | flops 9200000000 | bytes 28800000 | tf_op jit(solution)/shard_map/bound/pallas_call | solution.py:181
  36.0 1.3 %collective-permute-start.5 = (bf16[8,256,128]{2,1,0:T(8,128)(2,1)S(1)}, bf16[8,256,128]{2,1,0:T(8,128)(2,1)S(1)}, u32[]{:S(2)}, u32[]{:S(2)}) collective-permute-start(bf16[8,256,128]{2,1,0:T(8,128)(2,1)S(1)} %get-tuple-element.34.refs_0_), channel_id=1, source_target_pairs={{0,32},{4,12},{8,40},{12,20},{16,48},{20,28},{24,56},{28,4},{32,64... | collective-permute-start | bytes 1572872 | tf_op jit(solution)/shard_map/ppermute | solution.py:425
  37.4 2.0 %collective-permute-start.8 = (bf16[8,256,128]{2,1,0:T(8,128)(2,1)S(1)}, bf16[8,256,128]{2,1,0:T(8,128)(2,1)S(1)}, u32[]{:S(2)}, u32[]{:S(2)}) collective-permute-start(bf16[8,256,128]{2,1,0:T(8,128)(2,1)S(1)} %get-tuple-element.36), channel_id=1, source_target_pairs={{0,96},{4,28},{8,104},{12,4},{16,112},{20,12},{24,120},{28,20},{32... | collective-permute-start | bytes 1572872 | tf_op jit(solution)/shard_map/ppermute | solution.py:425
  39.3 3.4 %sib_here.1.refs_0_ = bf16[8,512,128]{2,1,0:T(8,128)(2,1)S(1)} custom-call(s32[32,128]{1,0:T(8,128)S(1)} %get-tuple-element.26.bound_ref, f32[32,8,1024]{2,1,0:T(8,128)S(1)} %get-tuple-element.27.ids_ref, bf16[32,1024,128]{2,1,0:T(8,128)(2,1)S(1)} %get-tuple-element.28.x_ref, bf16[8,256,128]{2,1,0:T(8,128)(2,1)S(1)} %get-tuple-element.34.refs_0_), custom_call_target="tpu_custom_call" | custom-call | flops 9200000000 | bytes 28800000 | tf_op jit(solution)/shard_map/sib_here/pallas_call | solution.py:181
  42.8 3.3 %own_here.1.here_ref = f32[8,512,128]{2,1,0:T(8,128)S(1)} custom-call(s32[32,128]{1,0:T(8,128)S(1)} %get-tuple-element.26.bound_ref, f32[32,8,1024]{2,1,0:T(8,128)S(1)} %get-tuple-element.27.ids_ref, bf16[32,1024,128]{2,1,0:T(8,128)(2,1)S(1)} %get-tuple-element.28.x_ref, bf16[8,512,128]{2,1,0:T(8,128)(2,1)S(1)} %sib_here.1.refs_0_), custom_call_target="tpu_custom_call" | custom-call | flops 2300000000 | bytes 7200000 | tf_op jit(solution)/shard_map/own_here/pallas_call | solution.py:181
  46.2 0.3 collective-permute-done.5.next_low
  46.5 0.3 gather.1.here_ref
  46.9 0.3 fold.1
  47.2 1.6 %collective-permute-start.10 = (bf16[2,512,128]{2,1,0:T(8,128)(2,1)S(1)}, bf16[2,512,128]{2,1,0:T(8,128)(2,1)S(1)}, u32[]{:S(2)}, u32[]{:S(2)}) collective-permute-start(bf16[2,512,128]{2,1,0:T(8,128)(2,1)S(1)} %get-tuple-element.37.after_ref), channel_id=1, source_target_pairs={{0,8},{4,36},{8,16},{12,44},{16,24},{20,52},{24,0},{28,60},{32,40}... | collective-permute-start | bytes 786440 | tf_op jit(solution)/shard_map/ppermute | solution.py:425
  48.7 2.9 %collective-permute-start.11 = (bf16[2,512,128]{2,1,0:T(8,128)(2,1)S(1)}, bf16[2,512,128]{2,1,0:T(8,128)(2,1)S(1)}, u32[]{:S(2)}, u32[]{:S(2)}) collective-permute-start(bf16[2,512,128]{2,1,0:T(8,128)(2,1)S(1)} %get-tuple-element.40), channel_id=1, source_target_pairs={{0,16},{4,68},{8,24},{12,76},{16,0},{20,84},{24,8},{28,92},{32,48}... | collective-permute-start | bytes 786440 | tf_op jit(solution)/shard_map/ppermute | solution.py:425
  51.6 1.2 %collective-permute-start.12 = (bf16[2,512,128]{2,1,0:T(8,128)(2,1)S(1)}, bf16[2,512,128]{2,1,0:T(8,128)(2,1)S(1)}, u32[]{:S(2)}, u32[]{:S(2)}) collective-permute-start(bf16[2,512,128]{2,1,0:T(8,128)(2,1)S(1)} %get-tuple-element.41), channel_id=1, source_target_pairs={{0,24},{4,100},{8,0},{12,108},{16,8},{20,116},{24,16},{28,124},{32... | collective-permute-start | bytes 786440 | tf_op jit(solution)/shard_map/ppermute | solution.py:425
  52.9 4.1 %old_values.1 = (f32[1024,128]{1,0:T(8,128)S(1)}, f32[1,1024]{1,0:T(1,128)S(1)}, f32[8192,128]{1,0:T(8,128)S(1)}) custom-call(s32[1,1024]{1,0:T(1,128)S(1)} %copy-done.2, f32[8192,128]{1,0:T(8,128)S(1)} %bitcast.3, f32[1,8192]{1,0:T(1,128)S(1)} %copy-done.1, bf16[2,512,128]{2,1,0:T(8,128)(2,1)S(1)} %get-tuple-element.37.after_ref), custom_call_target="tpu_custom_call" | custom-call | flops 9200000000 | bytes 28800000 | tf_op jit(solution)/shard_map/old_values/pallas_call | solution.py:216
  57.0 1.8 %collective-permute-done.11.c_ref = bf16[2,512,128]{2,1,0:T(8,128)(2,1)S(1)} collective-permute-done((bf16[2,512,128]{2,1,0:T(8,128)(2,1)S(1)}, bf16[2,512,128]{2,1,0:T(8,128)(2,1)S(1)}, u32[]{:S(2)}, u32[]{:S(2)}) %collective-permute-start.11) | collective-permute-done | bytes 262176 | tf_op jit(solution)/shard_map/ppermute | solution.py:425
  58.8 0.1 total.1
  59.0 1.5 %collective-permute-done.13.got_ref = f32[512,128]{1,0:T(8,128)S(1)} collective-permute-done((f32[512,128]{1,0:T(8,128)S(1)}, f32[512,128]{1,0:T(8,128)S(1)}, u32[]{:S(2)}, u32[]{:S(2)}) %collective-permute-start.13) | collective-permute-done | bytes 262176 | tf_op jit(solution)/shard_map/ppermute | solution.py:421
  60.6 0.2 square.1
  60.8 1.6 %collective-permute-start.14 = (f32[1,1024]{1,0:T(1,128)S(1)}, f32[1,1024]{1,0:T(1,128)S(1)}, u32[]{:S(2)}, u32[]{:S(2)}) collective-permute-start(f32[1,1024]{1,0:T(1,128)S(1)} %get-tuple-element.46), channel_id=1, source_target_pairs={{0,1},{1,0},{2,3},{3,2},{4,5},{5,4},{6,7},{7,6},{8,9},{9,8},{10,11... | collective-permute-start | bytes 12296 | tf_op jit(solution)/shard_map/ppermute | solution.py:453
  62.4 2.1 %collective-permute-done.14 = f32[1,1024]{1,0:T(1,128)S(1)} collective-permute-done((f32[1,1024]{1,0:T(1,128)S(1)}, f32[1,1024]{1,0:T(1,128)S(1)}, u32[]{:S(2)}, u32[]{:S(2)}) %collective-permute-start.14) | collective-permute-done | bytes 4128 | tf_op jit(solution)/shard_map/ppermute | solution.py:453
  64.5 2.8 %collective-permute-start.15 = (f32[1,1024]{1,0:T(1,128)S(1)}, f32[1,1024]{1,0:T(1,128)S(1)}, u32[]{:S(2)}, u32[]{:S(2)}) collective-permute-start(f32[1,1024]{1,0:T(1,128)S(1)} %add.3.s0_ref), channel_id=1, source_target_pairs={{0,3},{1,2},{2,1},{3,0},{4,7},{5,6},{6,5},{7,4},{8,11},{9,10},{10,... | collective-permute-start | bytes 12296 | tf_op jit(solution)/shard_map/ppermute | solution.py:453
  67.9 1.4 %collective-permute-done.15.s1_ref = f32[1,1024]{1,0:T(1,128)S(1)} collective-permute-done((f32[1,1024]{1,0:T(1,128)S(1)}, f32[1,1024]{1,0:T(1,128)S(1)}, u32[]{:S(2)}, u32[]{:S(2)}) %collective-permute-start.15) | collective-permute-done | bytes 4128 | tf_op jit(solution)/shard_map/ppermute | solution.py:453
  69.3 4.0 %apply_rows.1 = (f32[8192,128]{1,0:T(8,128)}, f32[1,8192]{1,0:T(1,128)}, f32[8192,128]{1,0:T(8,128)S(1)}) custom-call(s32[1,1024]{1,0:T(1,128)S(1)} %copy-done.2, s32[1]{0:T(128)S(6)} %copy.10.live_hbm, f32[8192,128]{1,0:T(8,128)S(1)} %get-tuple-element.38.emb_in, f32[1024,128]{1,0:T(8,128)S(1)} %get-tuple-element.45.grad_ref, ...), custom_call_target="tpu_custom_call", output_to_operand_aliasing={{2}: (2, {})} | custom-call | flops 13799999488 | bytes 43200000 | tf_op jit(solution)/shard_map/apply_rows/pallas_call | solution.py:382
  (21 shorter events, 0.4 us)
Async XLA Ops:
  8.7 8.0 %collective-permute-start.1 = (bf16[8,512,128]{2,1,0:T(8,128)(2,1)S(1)}, bf16[8,512,128]{2,1,0:T(8,128)(2,1)S(1)}, u32[]{:S(2)}, u32[]{:S(2)}) collective-permute-start(bf16[8,512,128]{2,1,0:T(8,128)(2,1)S(1)} %sib_far.1.refs_0_), channel_id=1, source_target_pairs={{0,4},{4,0},{1,5},{5,1},{2,6},{6,2},{3,7},{7,3},{8,12},{12,8},{9,1... | collective-permute-start | bytes 3145736 | tf_op jit(solution)/shard_map/ppermute | solution.py:421
  15.8 8.5 %collective-permute-start = (bf16[8,512,128]{2,1,0:T(8,128)(2,1)S(1)}, bf16[8,512,128]{2,1,0:T(8,128)(2,1)S(1)}, u32[]{:S(2)}, u32[]{:S(2)}) collective-permute-start(bf16[8,512,128]{2,1,0:T(8,128)(2,1)S(1)} %get-tuple-element.29.refs_1_), channel_id=1, source_target_pairs={{0,4},{4,0},{1,5},{5,1},{2,6},{6,2},{3,7},{7,3},{8,12},{12,8},{9,1... | collective-permute-start | bytes 3145736 | tf_op jit(solution)/shard_map/ppermute | solution.py:421
  16.6 7.6 %collective-permute-start.3 = (bf16[8,512,128]{2,1,0:T(8,128)(2,1)S(1)}, bf16[8,512,128]{2,1,0:T(8,128)(2,1)S(1)}, u32[]{:S(2)}, u32[]{:S(2)}) collective-permute-start(bf16[8,512,128]{2,1,0:T(8,128)(2,1)S(1)} %get-tuple-element.31), channel_id=1, source_target_pairs={{0,4},{4,0},{1,5},{5,1},{2,6},{6,2},{3,7},{7,3},{8,12},{12,8},{9,1... | collective-permute-start | bytes 3145736 | tf_op jit(solution)/shard_map/ppermute | solution.py:421
  20.3 11.2 %collective-permute-start.2 = (bf16[8,256,128]{2,1,0:T(8,128)(2,1)S(1)}, bf16[8,256,128]{2,1,0:T(8,128)(2,1)S(1)}, u32[]{:S(2)}, u32[]{:S(2)}) collective-permute-start(bf16[8,256,128]{2,1,0:T(8,128)(2,1)S(1)} %get-tuple-element.30.refs_2_), channel_id=1, source_target_pairs={{0,32},{4,12},{8,40},{12,20},{16,48},{20,28},{24,56},{28,4},{32,64... | collective-permute-start | bytes 1572872 | tf_op jit(solution)/shard_map/ppermute | solution.py:425
  22.4 9.2 %collective-permute-start.4 = (bf16[8,256,128]{2,1,0:T(8,128)(2,1)S(1)}, bf16[8,256,128]{2,1,0:T(8,128)(2,1)S(1)}, u32[]{:S(2)}, u32[]{:S(2)}) collective-permute-start(bf16[8,256,128]{2,1,0:T(8,128)(2,1)S(1)} %get-tuple-element.32), channel_id=1, source_target_pairs={{0,96},{4,28},{8,104},{12,4},{16,112},{20,12},{24,120},{28,20},{32... | collective-permute-start | bytes 1572872 | tf_op jit(solution)/shard_map/ppermute | solution.py:425
  28.2 18.0 %collective-permute-start.6 = (bf16[8,256,128]{2,1,0:T(8,128)(2,1)S(1)}, bf16[8,256,128]{2,1,0:T(8,128)(2,1)S(1)}, u32[]{:S(2)}, u32[]{:S(2)}) collective-permute-start(bf16[8,256,128]{2,1,0:T(8,128)(2,1)S(1)} %get-tuple-element.33.refs_4_), channel_id=1, source_target_pairs={{0,32},{4,12},{8,40},{12,20},{16,48},{20,28},{24,56},{28,4},{32,64... | collective-permute-start | bytes 1572872 | tf_op jit(solution)/shard_map/ppermute | solution.py:425
  28.7 17.5 %collective-permute-start.7 = (bf16[8,256,128]{2,1,0:T(8,128)(2,1)S(1)}, bf16[8,256,128]{2,1,0:T(8,128)(2,1)S(1)}, u32[]{:S(2)}, u32[]{:S(2)}) collective-permute-start(bf16[8,256,128]{2,1,0:T(8,128)(2,1)S(1)} %get-tuple-element.35), channel_id=1, source_target_pairs={{0,96},{4,28},{8,104},{12,4},{16,112},{20,12},{24,120},{28,20},{32... | collective-permute-start | bytes 1572872 | tf_op jit(solution)/shard_map/ppermute | solution.py:425
  36.0 10.5 %collective-permute-start.5 = (bf16[8,256,128]{2,1,0:T(8,128)(2,1)S(1)}, bf16[8,256,128]{2,1,0:T(8,128)(2,1)S(1)}, u32[]{:S(2)}, u32[]{:S(2)}) collective-permute-start(bf16[8,256,128]{2,1,0:T(8,128)(2,1)S(1)} %get-tuple-element.34.refs_0_), channel_id=1, source_target_pairs={{0,32},{4,12},{8,40},{12,20},{16,48},{20,28},{24,56},{28,4},{32,64... | collective-permute-start | bytes 1572872 | tf_op jit(solution)/shard_map/ppermute | solution.py:425
  37.4 9.2 %collective-permute-start.8 = (bf16[8,256,128]{2,1,0:T(8,128)(2,1)S(1)}, bf16[8,256,128]{2,1,0:T(8,128)(2,1)S(1)}, u32[]{:S(2)}, u32[]{:S(2)}) collective-permute-start(bf16[8,256,128]{2,1,0:T(8,128)(2,1)S(1)} %get-tuple-element.36), channel_id=1, source_target_pairs={{0,96},{4,28},{8,104},{12,4},{16,112},{20,12},{24,120},{28,20},{32... | collective-permute-start | bytes 1572872 | tf_op jit(solution)/shard_map/ppermute | solution.py:425
  42.7 4.2 %collective-permute-start.9 = (bf16[8,512,128]{2,1,0:T(8,128)(2,1)S(1)}, bf16[8,512,128]{2,1,0:T(8,128)(2,1)S(1)}, u32[]{:S(2)}, u32[]{:S(2)}) collective-permute-start(bf16[8,512,128]{2,1,0:T(8,128)(2,1)S(1)} %sib_here.1.refs_0_), channel_id=1, source_target_pairs={{0,4},{4,0},{1,5},{5,1},{2,6},{6,2},{3,7},{7,3},{8,12},{12,8},{9,1... | collective-permute-start | bytes 3145736 | tf_op jit(solution)/shard_map/ppermute | solution.py:421
  46.2 6.7 %copy-start = (f32[1,8192,128]{2,1,0:T(8,128)S(1)}, f32[1,8192,128]{2,1,0:T(8,128)}, u32[]{:S(2)}) copy-start(f32[1,8192,128]{2,1,0:T(8,128)} %param.10) | copy-start | bytes 12582916
  46.2 6.7 %copy-start.1 = (f32[1,8192]{1,0:T(1,128)S(1)}, f32[1,8192]{1,0:T(1,128)}, u32[]{:S(2)}) copy-start(f32[1,8192]{1,0:T(1,128)} %acc_in.1) | copy-start | bytes 98308
  46.2 6.7 %copy-start.2 = (s32[1,1024]{1,0:T(1,128)S(1)}, s32[1,1024]{1,0:T(1,128)}, u32[]{:S(2)}) copy-start(s32[1,1024]{1,0:T(1,128)} %row_hbm.3) | copy-start | bytes 12292
  47.2 9.8 %collective-permute-start.10 = (bf16[2,512,128]{2,1,0:T(8,128)(2,1)S(1)}, bf16[2,512,128]{2,1,0:T(8,128)(2,1)S(1)}, u32[]{:S(2)}, u32[]{:S(2)}) collective-permute-start(bf16[2,512,128]{2,1,0:T(8,128)(2,1)S(1)} %get-tuple-element.37.after_ref), channel_id=1, source_target_pairs={{0,8},{4,36},{8,16},{12,44},{16,24},{20,52},{24,0},{28,60},{32,40}... | collective-permute-start | bytes 786440 | tf_op jit(solution)/shard_map/ppermute | solution.py:425
  48.7 10.1 %collective-permute-start.11 = (bf16[2,512,128]{2,1,0:T(8,128)(2,1)S(1)}, bf16[2,512,128]{2,1,0:T(8,128)(2,1)S(1)}, u32[]{:S(2)}, u32[]{:S(2)}) collective-permute-start(bf16[2,512,128]{2,1,0:T(8,128)(2,1)S(1)} %get-tuple-element.40), channel_id=1, source_target_pairs={{0,16},{4,68},{8,24},{12,76},{16,0},{20,84},{24,8},{28,92},{32,48}... | collective-permute-start | bytes 786440 | tf_op jit(solution)/shard_map/ppermute | solution.py:425
  51.6 7.2 %collective-permute-start.12 = (bf16[2,512,128]{2,1,0:T(8,128)(2,1)S(1)}, bf16[2,512,128]{2,1,0:T(8,128)(2,1)S(1)}, u32[]{:S(2)}, u32[]{:S(2)}) collective-permute-start(bf16[2,512,128]{2,1,0:T(8,128)(2,1)S(1)} %get-tuple-element.41), channel_id=1, source_target_pairs={{0,24},{4,100},{8,0},{12,108},{16,8},{20,116},{24,16},{28,124},{32... | collective-permute-start | bytes 786440 | tf_op jit(solution)/shard_map/ppermute | solution.py:425
  58.9 1.6 %collective-permute-start.13 = (f32[512,128]{1,0:T(8,128)S(1)}, f32[512,128]{1,0:T(8,128)S(1)}, u32[]{:S(2)}, u32[]{:S(2)}) collective-permute-start(f32[512,128]{1,0:T(8,128)S(1)} %get-tuple-element.44), channel_id=1, source_target_pairs={{0,4},{4,0},{1,5},{5,1},{2,6},{6,2},{3,7},{7,3},{8,12},{12,8},{9,1... | collective-permute-start | bytes 786440 | tf_op jit(solution)/shard_map/ppermute | solution.py:421
  60.8 3.7 %collective-permute-start.14 = (f32[1,1024]{1,0:T(1,128)S(1)}, f32[1,1024]{1,0:T(1,128)S(1)}, u32[]{:S(2)}, u32[]{:S(2)}) collective-permute-start(f32[1,1024]{1,0:T(1,128)S(1)} %get-tuple-element.46), channel_id=1, source_target_pairs={{0,1},{1,0},{2,3},{3,2},{4,5},{5,4},{6,7},{7,6},{8,9},{9,8},{10,11... | collective-permute-start | bytes 12296 | tf_op jit(solution)/shard_map/ppermute | solution.py:453
  64.5 4.8 %collective-permute-start.15 = (f32[1,1024]{1,0:T(1,128)S(1)}, f32[1,1024]{1,0:T(1,128)S(1)}, u32[]{:S(2)}, u32[]{:S(2)}) collective-permute-start(f32[1,1024]{1,0:T(1,128)S(1)} %add.3.s0_ref), channel_id=1, source_target_pairs={{0,3},{1,2},{2,1},{3,0},{4,7},{5,6},{6,5},{7,4},{8,11},{9,10},{10,... | collective-permute-start | bytes 12296 | tf_op jit(solution)/shard_map/ppermute | solution.py:453
